TPU v7x, 128 devices: a whole 4x4x4 slice. The times are simulated.
128 devices in a mesh: dp: 16 (over z_hi, x, core), tensor: 8 (over y, z_lo).
Axes of the slice: x: 4, y: 4, z: 4 (z_hi: 2, z_lo: 2; z = z_hi * 2 + z_lo), core: 2. Of those that a mesh axis runs over, the one named last changes fastest.
Arguments:
- tokens: bfloat16 [16384, 2048], P(('dp', 'tensor')), may hold values from -6 to 6
- doc_ids: int32 [16384], P(('dp', 'tensor')), may hold values from -1 to 3, as said below
- qkv_weight: bfloat16 [3, 2048, 2048], P(None, 'dp', 'tensor'), may hold values from -0.125 to 0.125
- qkv_bias: float32 [3, 2048], P(None, 'tensor'), may hold values from -3 to 3
- out_weight: bfloat16 [2048, 2048], P('tensor', 'dp'), may hold values from -0.375 to 0.375
- norm1_gain: float32 [2048], replicated, may hold values from 0.5 to 1.5
- norm1_shift: float32 [2048], replicated, may hold values from -2 to 2
- norm2_gain: float32 [2048], replicated, may hold values from 0.5 to 1.5
- norm2_shift: float32 [2048], replicated, may hold values from -2 to 2
- gate_up_weight: bfloat16 [2, 2048, 5632], P(None, 'dp', 'tensor'), may hold values from -0.125 to 0.125
- down_weight: bfloat16 [5632, 2048], P('tensor', 'dp'), may hold values from -0.109375 to 0.109375
- cotangent: bfloat16 [16384, 2048], P(('dp', 'tensor')), may hold values from -6 to 6
Outputs:
- layer_out: bfloat16 [16384, 2048], P(('dp', 'tensor'))
- token_grad: bfloat16 [16384, 2048], P(('dp', 'tensor'))
- qkv_weight_grad: float32 [3, 2048, 2048], P(None, 'dp', 'tensor')
- qkv_bias_grad: float32 [3, 2048], P(None, 'tensor')
- out_weight_grad: float32 [2048, 2048], P('tensor', 'dp')
- norm1_gain_grad: float32 [2048], replicated
- norm1_shift_grad: float32 [2048], replicated
- norm2_gain_grad: float32 [2048], replicated
- norm2_shift_grad: float32 [2048], replicated
- gate_up_weight_grad: float32 [2, 2048, 5632], P(None, 'dp', 'tensor')
- down_weight_grad: float32 [5632, 2048], P('tensor', 'dp')
Inputs may be any that keep to these rules, and one draw needn't show every extreme that they name: `doc_ids`: within each aligned block of 1024 tokens, documents 0 to 3 are consecutive runs in increasing order and the padding (-1) is one run at the block's end, at least one token long.
All inputs are finite; a program needn't handle non-finite values.
Results may differ from a plain program's by a relative error of at most 0.025.
Values may be sent and summed in bfloat16 or wider, within the bound.
A program may use at most 192 MiB of HBM per device.

v0:
```python
import jax
import jax.numpy as jnp
from jax import lax
from jax.sharding import PartitionSpec as P

HEAD_DIM = 64
ROT = 16
DOCS = 4


EPS = 1e-05


def norm_parts(values, gain, shift):
    centred = values - jnp.mean(values, axis=-1, keepdims=True)
    variance = jnp.mean(centred * centred, axis=-1, keepdims=True)
    rinv = lax.rsqrt(variance + EPS)
    normal = centred * rinv
    return (normal * gain + shift, normal, rinv)


def norm_back(incoming, normal, rinv, gain):
    scaled = incoming * gain
    inner = (
        scaled
        - jnp.mean(scaled, axis=-1, keepdims=True)
        - normal * jnp.mean(scaled * normal, axis=-1, keepdims=True)
    )
    return (rinv * inner, jnp.sum(incoming * normal, axis=0), jnp.sum(incoming, axis=0))


def angles(group_ids):
    group = group_ids.shape[0]
    index = jnp.arange(group, dtype=jnp.int32)
    numbers = jnp.arange(DOCS, dtype=jnp.int32)
    before = (group_ids[None, :] >= 0) & (group_ids[None, :] < numbers[:, None])
    starts = jnp.sum(before.astype(jnp.int32), axis=1)
    offset = jnp.sum(jnp.where(group_ids[:, None] == numbers[None, :], starts[None, :], 0), axis=1)
    position = (index - offset).astype(jnp.float32)
    freq = jnp.power(10000.0, -2.0 * jnp.arange(ROT // 2, dtype=jnp.float32) / ROT)
    angle = position[:, None] * freq[None, :]
    return (jnp.cos(angle), jnp.sin(angle))


def rotate(values, cosine, sine):
    half = ROT // 2
    first_part = values[..., :half]
    second_part = values[..., half:ROT]
    cosine = cosine[:, None, :]
    sine = sine[:, None, :]
    return jnp.concatenate(
        [
            first_part * cosine - second_part * sine,
            second_part * cosine + first_part * sine,
            values[..., ROT:],
        ],
        axis=-1,
    )


def allowed_keys(row_ids, row_first, col_ids):
    rows = row_first + jnp.arange(row_ids.shape[0], dtype=jnp.int32)
    cols = jnp.arange(col_ids.shape[0], dtype=jnp.int32)
    same = (
        (row_ids[:, None] == col_ids[None, :])
        & (col_ids[None, :] >= 0)
        & (cols[None, :] < rows[:, None])
    )
    return same | (cols[None, :] == rows[:, None])


def body(
    tokens,
    doc_ids,
    qkv_weight,
    qkv_bias,
    out_weight,
    norm1_gain,
    norm1_shift,
    norm2_gain,
    norm2_shift,
    gate_up_weight,
    down_weight,
    cotangent,
):
    inputs = tokens.astype(jnp.float32)
    qkv_full, out_full = (
        lax.all_gather(qkv_weight, "dp", axis=1, tiled=True),
        lax.all_gather(out_weight, "dp", axis=1, tiled=True),
    )
    normed1, normal1, rinv1 = norm_parts(inputs, norm1_gain, norm1_shift)
    rows1, id_rows = (
        lax.all_gather(normed1.astype(jnp.bfloat16), "tensor", axis=0, tiled=True),
        lax.all_gather(doc_ids.astype(jnp.bfloat16), "tensor", axis=0, tiled=True),
    )
    group_ids = id_rows.astype(jnp.int32)
    group = rows1.shape[0]
    local_width = qkv_full.shape[2]
    heads = local_width // HEAD_DIM
    scale = HEAD_DIM ** (-0.5)
    cosine, sine = angles(group_ids)
    projected = (
        jnp.einsum("td,cde->cte", rows1, qkv_full, preferred_element_type=jnp.float32)
        + qkv_bias[:, None, :]
    )
    query = rotate(projected[0].reshape(group, heads, HEAD_DIM), cosine, sine).astype(jnp.bfloat16)
    keys_all = rotate(projected[1].reshape(group, heads, HEAD_DIM), cosine, sine).astype(
        jnp.bfloat16
    )
    values_all = projected[2].reshape(group, heads, HEAD_DIM).astype(jnp.bfloat16)
    block = min(512, group)
    outputs = []
    lse_parts = []
    for first_row in range(0, group, block):
        query_block = query[first_row : first_row + block]
        scores = (
            jnp.einsum("qhd,khd->hqk", query_block, keys_all, preferred_element_type=jnp.float32)
            * scale
        )
        allow = allowed_keys(group_ids[first_row : first_row + block], first_row, group_ids)
        masked = jnp.where(allow[None], scores, -1e30)
        highest = jnp.max(masked, axis=-1, keepdims=True)
        expon = jnp.exp(masked - highest)
        totals = jnp.sum(expon, axis=-1, keepdims=True)
        probs = expon / totals
        lse_parts.append(highest + jnp.log(totals))
        outputs.append(
            jnp.einsum(
                "hqk,khd->qhd",
                probs.astype(jnp.bfloat16),
                values_all,
                preferred_element_type=jnp.float32,
            )
        )
    attended = jnp.concatenate(outputs, axis=0).reshape(group, local_width).astype(jnp.bfloat16)
    log_totals = jnp.concatenate(lse_parts, axis=1)
    picked = attended
    mixed = inputs + lax.psum_scatter(
        jnp.dot(picked, out_full, preferred_element_type=jnp.float32).astype(jnp.bfloat16),
        "tensor",
        scatter_dimension=0,
        tiled=True,
    ).astype(jnp.float32)
    gate_up_full, down_full = (
        lax.all_gather(gate_up_weight, "dp", axis=1, tiled=True),
        lax.all_gather(down_weight, "dp", axis=1, tiled=True),
    )
    normed2, normal2, rinv2 = norm_parts(mixed, norm2_gain, norm2_shift)
    rows2 = lax.all_gather(normed2.astype(jnp.bfloat16), "tensor", axis=0, tiled=True)
    gate_up = jnp.einsum("td,cdf->ctf", rows2, gate_up_full, preferred_element_type=jnp.float32)
    gate = gate_up[0]
    upward = gate_up[1]
    hidden = (jax.nn.silu(gate) * upward).astype(jnp.bfloat16)
    picked = hidden
    layer_out = (
        mixed
        + lax.psum_scatter(
            jnp.dot(picked, down_full, preferred_element_type=jnp.float32).astype(jnp.bfloat16),
            "tensor",
            scatter_dimension=0,
            tiled=True,
        ).astype(jnp.float32)
    ).astype(jnp.bfloat16)
    grad_rows = lax.all_gather(cotangent, "tensor", axis=0, tiled=True)
    down_grad = jnp.einsum("tf,td->fd", hidden, grad_rows, preferred_element_type=jnp.float32)
    grad_hidden = jnp.einsum("td,fd->tf", grad_rows, down_full, preferred_element_type=jnp.float32)
    sigma = jax.nn.sigmoid(gate)
    grad_gate = grad_hidden * upward * sigma * (1.0 + gate * (1.0 - sigma))
    grad_upward = grad_hidden * (gate * sigma)
    grad_gate_up = jnp.stack([grad_gate, grad_upward]).astype(jnp.bfloat16)
    gate_up_grad = jnp.einsum(
        "td,ctf->cdf", rows2, grad_gate_up, preferred_element_type=jnp.float32
    )
    picked = grad_gate_up
    grad_normed2 = lax.psum_scatter(
        jnp.einsum("ctf,cdf->td", picked, gate_up_full, preferred_element_type=jnp.float32).astype(
            jnp.bfloat16
        ),
        "tensor",
        scatter_dimension=0,
        tiled=True,
    ).astype(jnp.float32)
    back2, gain2_grad, shift2_grad = norm_back(grad_normed2, normal2, rinv2, norm2_gain)
    grad_mixed = cotangent.astype(jnp.float32) + back2
    branch_grad = lax.all_gather(grad_mixed.astype(jnp.bfloat16), "tensor", axis=0, tiled=True)
    out_grad = jnp.einsum("te,td->ed", attended, branch_grad, preferred_element_type=jnp.float32)
    grad_attended = jnp.einsum(
        "td,ed->te", branch_grad, out_full, preferred_element_type=jnp.float32
    )
    grad_attended = grad_attended.astype(jnp.bfloat16).reshape(group, heads, HEAD_DIM)
    grad_query_parts = []
    grad_keys = jnp.zeros((group, heads, HEAD_DIM), jnp.float32)
    grad_values = jnp.zeros((group, heads, HEAD_DIM), jnp.float32)
    for first_row in range(0, group, block):
        query_block = query[first_row : first_row + block]
        scores = (
            jnp.einsum("qhd,khd->hqk", query_block, keys_all, preferred_element_type=jnp.float32)
            * scale
        )
        allow = allowed_keys(group_ids[first_row : first_row + block], first_row, group_ids)
        probs = jnp.where(
            allow[None], jnp.exp(scores - log_totals[:, first_row : first_row + block]), 0.0
        )
        grad_block = grad_attended[first_row : first_row + block]
        grad_probs = jnp.einsum(
            "qhd,khd->hqk", grad_block, values_all, preferred_element_type=jnp.float32
        )
        inner = jnp.sum(probs * grad_probs, axis=-1, keepdims=True)
        grad_scores = (probs * (grad_probs - inner)).astype(jnp.bfloat16)
        grad_query_parts.append(
            jnp.einsum("hqk,khd->qhd", grad_scores, keys_all, preferred_element_type=jnp.float32)
            * scale
        )
        grad_keys = (
            grad_keys
            + jnp.einsum(
                "hqk,qhd->khd", grad_scores, query_block, preferred_element_type=jnp.float32
            )
            * scale
        )
        grad_values = grad_values + jnp.einsum(
            "hqk,qhd->khd",
            probs.astype(jnp.bfloat16),
            grad_block,
            preferred_element_type=jnp.float32,
        )
    grad_query = rotate(jnp.concatenate(grad_query_parts, axis=0), cosine, -sine)
    grad_keys = rotate(grad_keys, cosine, -sine)
    grad_pre = (
        jnp.stack([grad_query, grad_keys, grad_values])
        .reshape(3, group, local_width)
        .astype(jnp.bfloat16)
    )
    bias_part = jnp.sum(grad_pre.astype(jnp.float32), axis=1)
    qkv_grad = jnp.einsum("td,cte->cde", rows1, grad_pre, preferred_element_type=jnp.float32)
    picked = grad_pre
    grad_normed1 = lax.psum_scatter(
        jnp.einsum("cte,cde->td", picked, qkv_full, preferred_element_type=jnp.float32).astype(
            jnp.bfloat16
        ),
        "tensor",
        scatter_dimension=0,
        tiled=True,
    ).astype(jnp.float32)
    back1, gain1_grad, shift1_grad = norm_back(grad_normed1, normal1, rinv1, norm1_gain)
    token_grad = (grad_mixed + back1).astype(jnp.bfloat16)
    column_first = lax.axis_index("tensor") * local_width
    bias_full = lax.dynamic_update_slice(
        jnp.zeros((3, local_width * lax.axis_size("tensor")), jnp.float32),
        bias_part,
        (0, column_first),
    )
    gain1_sum, shift1_sum, gain2_sum, shift2_sum, bias_sum = lax.psum(
        (gain1_grad, shift1_grad, gain2_grad, shift2_grad, bias_full), ("dp", "tensor")
    )
    bias_grad = lax.dynamic_slice(bias_sum, (0, column_first), (3, local_width))
    qkv_shard, out_shard, gate_up_shard, down_shard = (
        lax.psum_scatter(
            qkv_grad.astype(jnp.bfloat16), "dp", scatter_dimension=1, tiled=True
        ).astype(jnp.float32),
        lax.psum_scatter(
            out_grad.astype(jnp.bfloat16), "dp", scatter_dimension=1, tiled=True
        ).astype(jnp.float32),
        lax.psum_scatter(
            gate_up_grad.astype(jnp.bfloat16), "dp", scatter_dimension=1, tiled=True
        ).astype(jnp.float32),
        lax.psum_scatter(
            down_grad.astype(jnp.bfloat16), "dp", scatter_dimension=1, tiled=True
        ).astype(jnp.float32),
    )
    return (
        layer_out,
        token_grad,
        qkv_shard,
        bias_grad,
        out_shard,
        gain1_sum,
        shift1_sum,
        gain2_sum,
        shift2_sum,
        gate_up_shard,
        down_shard,
    )


def solution(mesh):
    in_specs = (
        P(("dp", "tensor"), None),
        P(("dp", "tensor")),
        P(None, "dp", "tensor"),
        P(None, "tensor"),
        P("tensor", "dp"),
        P(),
        P(),
        P(),
        P(),
        P(None, "dp", "tensor"),
        P("tensor", "dp"),
        P(("dp", "tensor"), None),
    )
    out_specs = (
        P(("dp", "tensor"), None),
        P(("dp", "tensor"), None),
        P(None, "dp", "tensor"),
        P(None, "tensor"),
        P("tensor", "dp"),
        P(),
        P(),
        P(),
        P(),
        P(None, "dp", "tensor"),
        P("tensor", "dp"),
    )
    return jax.shard_map(body, mesh=mesh, in_specs=in_specs, out_specs=out_specs, check_vma=False)
```

profile of v0, /device:TPU:0, one launch (start us, length us, event | category | flops | bytes accessed | tf_op | source)
XLA Modules:
  0.0 1336.2 jit_solution(2468805201723880927)
XLA Ops:
  15.4 19.4 %all-gather = bf16[8,1,128]{2,1,0:T(2,128)(2,1)S(1)} all-gather(bf16[1,1,128]{2,1,0:T(2,128)(2,1)S(1)} %convert_bitcast_fusion.1), channel_id=1, replica_groups=mesh['dp'=16,'tensor'=8] {'tensor'}, dimensions={0}, use_global_device_ids=true | all-gather | bytes 2304 | tf_op jit(solution)/shard_map/all_gather | solution.py:94
  37.7 29.9 %all-gather.12.cloned.1.call-done = bf16[3,2048,256]{1,2,0:T(8,128)(2,1)} async-done(((bf16[3,128,256]{1,2,0:T(8,128)(2,1)}), bf16[3,2048,256]{1,2,0:T(8,128)(2,1)}) %all-gather.12.cloned.1.call-update) | async-done | bytes 3145744 | tf_op jit(solution)/shard_map/all_gather | solution.py:88
  67.6 90.6 %all-gather.10.cloned.1.call-done = bf16[1024,2048]{1,0:T(8,128)(2,1)} async-done(((bf16[128,2048]{1,0:T(8,128)(2,1)}), bf16[1024,2048]{1,0:T(8,128)(2,1)}) %all-gather.10.cloned.1.call-update) | async-done | bytes 4194320 | tf_op jit(solution)/shard_map/all_gather | solution.py:93
  158.2 6.2 add_bitcast_fusion
  179.6 28.9 %all-gather.14.cloned.1.call-done = bf16[256,2048]{1,0:T(8,128)(2,1)} async-done(((bf16[256,128]{1,0:T(8,128)(2,1)}), bf16[256,2048]{1,0:T(8,128)(2,1)}) %all-gather.14.cloned.1.call-update) | async-done | bytes 1048592 | tf_op jit(solution)/shard_map/all_gather | solution.py:89
  213.8 88.2 %reduce-scatter.17.cloned.1.call-done = bf16[128,2048]{1,0:T(8,128)(2,1)} async-done(((bf16[1024,2048]{1,0:T(8,128)(2,1)}), bf16[128,2048]{1,0:T(8,128)(2,1)}) %reduce-scatter.17.cloned.1.call-update) | async-done | bytes 524304 | tf_op jit(solution)/shard_map/reduce_scatter | solution.py:138
  308.4 63.7 %all-gather.18.cloned.1.call-done = bf16[2,2048,704]{1,2,0:T(8,128)(2,1)} async-done(((bf16[2,128,704]{1,2,0:T(8,128)(2,1)}), bf16[2,2048,704]{1,2,0:T(8,128)(2,1)}) %all-gather.18.cloned.1.call-update) | async-done | bytes 5767184 | tf_op jit(solution)/shard_map/all_gather | solution.py:145
  372.1 90.3 %all-gather.16.cloned.1.call-done = bf16[1024,2048]{1,0:T(8,128)(2,1)} async-done(((bf16[128,2048]{1,0:T(8,128)(2,1)}), bf16[1024,2048]{1,0:T(8,128)(2,1)}) %all-gather.16.cloned.1.call-update) | async-done | bytes 4194320 | tf_op jit(solution)/shard_map/all_gather | solution.py:149
  462.4 11.0 fusion.26
  473.4 46.8 %all-gather.20.cloned.1.call-done = bf16[704,2048]{1,0:T(8,128)(2,1)} async-done(((bf16[704,128]{1,0:T(8,128)(2,1)}), bf16[704,2048]{1,0:T(8,128)(2,1)}) %all-gather.20.cloned.1.call-update) | async-done | bytes 2883600 | tf_op jit(solution)/shard_map/all_gather | solution.py:146
  520.2 90.0 %all-gather.22.cloned.1.call-done = bf16[1024,2048]{1,0:T(8,128)(2,1)} async-done(((bf16[128,2048]{1,0:T(8,128)(2,1)}), bf16[1024,2048]{1,0:T(8,128)(2,1)}) %all-gather.22.cloned.1.call-update) | async-done | bytes 4194320 | tf_op jit(solution)/shard_map/all_gather | solution.py:164
  610.2 10.2 fusion.42
  622.0 8.6 bitcast_convert_fusion.1
  630.6 92.9 %reduce-scatter.21.cloned.1.call-done = bf16[128,2048]{1,0:T(8,128)(2,1)} async-done(((bf16[1024,2048]{1,0:T(8,128)(2,1)}), bf16[128,2048]{1,0:T(8,128)(2,1)}) %reduce-scatter.21.cloned.1.call-update) | async-done | bytes 524304 | tf_op jit(solution)/shard_map/reduce_scatter | solution.py:175
  729.7 7.3 convolution_convert_fusion.2
  741.7 10.5 convert_bitcast_fusion
  752.3 16.3 %copy.50 = bf16[2,2048,704]{2,0,1:T(2,128)(2,1)} copy(bf16[2,2048,704]{1,2,0:T(8,128)(2,1)} %convert_bitcast_fusion) | data formatting | bytes 11534336
  768.5 13.9 %reshape.355 = bf16[2048,1408]{1,0:T(8,128)(2,1)} reshape(bf16[2048,2,704]{2,1,0:T(2,128)(2,1)} %bitcast.126) | data formatting | bytes 11534336
  784.5 35.6 %all-gather.24.cloned.1.call-done = bf16[1024,2048]{1,0:T(8,128)(2,1)} async-done(((bf16[128,2048]{1,0:T(8,128)(2,1)}), bf16[1024,2048]{1,0:T(8,128)(2,1)}) %all-gather.24.cloned.1.call-update) | async-done | bytes 4194320 | tf_op jit(solution)/shard_map/all_gather | solution.py:185
  841.1 8.3 multiply_reduce_fusion.1
  849.5 7.9 multiply_reduce_fusion
  858.1 8.8 multiply_convert_fusion
  877.3 7.7 fusion.22
  885.0 7.2 copy.46
  897.1 6.9 bitcast_convert_fusion
  904.3 7.7 convolution_convert_fusion
  914.1 77.6 %reduce-scatter.29.cloned.1.call-done = bf16[128,1408]{1,0:T(8,128)(2,1)} async-done(((bf16[2048,1408]{1,0:T(8,128)(2,1)}), bf16[128,1408]{1,0:T(8,128)(2,1)}) %reduce-scatter.29.cloned.1.call-update) | async-done | bytes 360464
  997.5 63.5 %reduce-scatter.27.cloned.1.call-done = bf16[128,256]{1,0:T(8,128)(2,1)} async-done(((bf16[2048,256]{1,0:T(8,128)(2,1)}), bf16[128,256]{1,0:T(8,128)(2,1)}) %reduce-scatter.27.cloned.1.call-update) | async-done | bytes 65552
  1062.6 77.1 %reduce-scatter.25.cloned.1.call-done = bf16[128,768]{1,0:T(8,128)(2,1)} async-done(((bf16[2048,768]{1,0:T(8,128)(2,1)}), bf16[128,768]{1,0:T(8,128)(2,1)}) %reduce-scatter.25.cloned.1.call-update) | async-done | bytes 196624
  1141.8 89.2 %reduce-scatter.23.cloned.1.call-done = bf16[128,2048]{1,0:T(8,128)(2,1)} async-done(((bf16[1024,2048]{1,0:T(8,128)(2,1)}), bf16[128,2048]{1,0:T(8,128)(2,1)}) %reduce-scatter.23.cloned.1.call-update) | async-done | bytes 524304 | tf_op jit(solution)/shard_map/reduce_scatter | solution.py:237
  1232.6 82.0 %all-reduce = (f32[3,2048]{1,0:T(4,128)S(1)}, f32[2048]{0:T(1024)}, f32[2048]{0:T(1024)}, f32[2048]{0:T(1024)}, f32[2048]{0:T(1024)}) all-reduce(f32[3,2048]{1,0:T(4,128)S(1)} %constant_dynamic-update-slice_fusion, f32[2048]{0:T(1024)S(1)} %get-tuple-element.46, ...), channel_id=1, replica_groups=mesh['dp'=16,'tensor'=8] {'dp','tensor'}, use_global_device_ids=true, to_apply=%region_22.23 | all-reduce | flops 14336 | bytes 114688 | tf_op jit(solution)/shard_map/psum | solution.py:253
  1315.2 10.7 reduce-scatter.19.cloned.1.call-done
  (228 shorter events, 106.0 us)
Async XLA Ops:
  7.2 151.0 %copy-start.47 = (f32[3,256]{1,0:T(4,128)S(1)}, f32[3,256]{1,0:T(4,128)}, u32[]{:S(2)}) copy-start(f32[3,256]{1,0:T(4,128)} %param.15) | copy-start | bytes 9220
  7.2 60.4 %all-gather.12.cloned.1.call-start = ((), (), s32[]{:S(2)}) async-start(), calls=%async_computation.9 | async-start | bytes 3342336 | tf_op jit(solution)/shard_map/all_gather | solution.py:88
  9.0 149.2 %all-gather.10.cloned.1.call-start = ((), (), s32[]{:S(2)}) async-start(), calls=%async_computation.8 | async-start | bytes 4718592 | tf_op jit(solution)/shard_map/all_gather | solution.py:93
  13.9 194.6 %all-gather.14.cloned.1.call-start = ((), (), s32[]{:S(2)}) async-start(), calls=%async_computation.10 | async-start | bytes 1114112 | tf_op jit(solution)/shard_map/all_gather | solution.py:89
  14.6 287.4 %reduce-scatter.17.cloned.1.call-start = ((), (), s32[]{:S(2)}) async-start(), calls=%async_computation.11 | async-start | bytes 4718592 | tf_op jit(solution)/shard_map/reduce_scatter | solution.py:138
  35.9 128.9 %copy-start.20 = (f32[1024,8]{0,1:T(8,128)}, f32[1024,8]{0,1:T(8,128)S(1)}, u32[]{:S(2)}) copy-start(f32[1024,8]{0,1:T(8,128)S(1)} %get-tuple-element.82) | copy-start | bytes 98308
  213.0 159.1 %all-gather.18.cloned.1.call-start = ((), (), s32[]{:S(2)}) async-start(), calls=%async_computation.13 | async-start | bytes 6127616 | tf_op jit(solution)/shard_map/all_gather | solution.py:145
  213.6 248.8 %all-gather.16.cloned.1.call-start = ((), (), s32[]{:S(2)}) async-start(), calls=%async_computation.12 | async-start | bytes 4718592 | tf_op jit(solution)/shard_map/all_gather | solution.py:149
  303.3 422.4 %copy-start.33 = (f32[128]{0:T(128)}, f32[128]{0:T(128)S(1)}, u32[]{:S(2)}) copy-start(f32[128]{0:T(128)S(1)} %broadcast_multiply_fusion.4) | copy-start | bytes 1540
  304.7 421.0 %copy-start.38 = (f32[128]{0:T(128)}, f32[128]{0:T(128)S(1)}, u32[]{:S(2)}) copy-start(f32[128]{0:T(128)S(1)} %add_rsqrt_fusion) | copy-start | bytes 1540
  306.8 213.4 %all-gather.20.cloned.1.call-start = ((), (), s32[]{:S(2)}) async-start(), calls=%async_computation.14 | async-start | bytes 3063808 | tf_op jit(solution)/shard_map/all_gather | solution.py:146
  307.6 302.6 %all-gather.22.cloned.1.call-start = ((), (), s32[]{:S(2)}) async-start(), calls=%async_computation.16 | async-start | bytes 4718592 | tf_op jit(solution)/shard_map/all_gather | solution.py:164
  308.3 415.2 %reduce-scatter.21.cloned.1.call-start = ((), (), s32[]{:S(2)}) async-start(), calls=%async_computation.17 | async-start | bytes 4718592 | tf_op jit(solution)/shard_map/reduce_scatter | solution.py:175
  630.5 93.0 %copy-start.4 = (bf16[128,2048]{1,0:T(8,128)(2,1)S(1)}, bf16[128,2048]{1,0:T(8,128)(2,1)}, u32[]{:S(2)}) copy-start(bf16[128,2048]{1,0:T(8,128)(2,1)} %reduce-scatter.17.cloned.1.call-done) | copy-start | bytes 1572868
  630.5 96.2 %copy-start.5 = (bf16[128,2048]{1,0:T(8,128)(2,1)S(1)}, bf16[128,2048]{1,0:T(8,128)(2,1)}, u32[]{:S(2)}) copy-start(bf16[128,2048]{1,0:T(8,128)(2,1)} %param.23) | copy-start | bytes 1572868
  630.6 189.5 %all-gather.24.cloned.1.call-start = ((), (), s32[]{:S(2)}) async-start(), calls=%async_computation.18 | async-start | bytes 4718592 | tf_op jit(solution)/shard_map/all_gather | solution.py:185
  729.2 182.9 %reduce-scatter.31.cloned.1.call-start = ((), (), s32[]{:S(2)}) async-start(), calls=%async_computation.23 | async-start | bytes 3342336
  741.7 250.0 %reduce-scatter.29.cloned.1.call-start = ((), (), s32[]{:S(2)}) async-start(), calls=%async_computation.22 | async-start | bytes 6127616
  782.4 278.5 %reduce-scatter.27.cloned.1.call-start = ((), (), s32[]{:S(2)}) async-start(), calls=%async_computation.21 | async-start | bytes 1114112
  871.1 268.6 %reduce-scatter.25.cloned.1.call-start = ((), (), s32[]{:S(2)}) async-start(), calls=%async_computation.20 | async-start | bytes 3342336
  897.0 334.0 %reduce-scatter.23.cloned.1.call-start = ((), (), s32[]{:S(2)}) async-start(), calls=%async_computation.19 | async-start | bytes 4718592 | tf_op jit(solution)/shard_map/reduce_scatter | solution.py:237
  904.0 421.9 %reduce-scatter.19.cloned.1.call-start = ((), (), s32[]{:S(2)}) async-start(), calls=%async_computation.15 | async-start | bytes 4718592 | tf_op jit(solution)/shard_map/reduce_scatter | solution.py:157
  912.0 319.0 %copy-start.26 = (f32[2048]{0:T(1024)S(1)}, f32[2048]{0:T(1024)}, u32[]{:S(2)}) copy-start(f32[2048]{0:T(1024)} %param.17) | copy-start | bytes 24580
  912.1 413.9 %copy-start.6 = (bf16[128,2048]{1,0:T(8,128)(2,1)S(1)}, bf16[128,2048]{1,0:T(8,128)(2,1)}, u32[]{:S(2)}) copy-start(bf16[128,2048]{1,0:T(8,128)(2,1)} %reduce-scatter.21.cloned.1.call-done) | copy-start | bytes 1572868
  994.2 236.8 %copy-start.36 = (f32[128]{0:T(128)S(1)}, f32[128]{0:T(128)}, u32[]{:S(2)}) copy-start(f32[128]{0:T(128)} %copy-done.35) | copy-start | bytes 1540
  994.2 236.8 %copy-start.41 = (f32[128]{0:T(128)S(1)}, f32[128]{0:T(128)}, u32[]{:S(2)}) copy-start(f32[128]{0:T(128)} %copy-done.40) | copy-start | bytes 1540
  994.2 238.4 %copy-start.27 = (f32[2048]{0:T(1024)S(1)}, f32[2048]{0:T(1024)}, u32[]{:S(2)}) copy-start(f32[2048]{0:T(1024)} %get-tuple-element.44) | copy-start | bytes 24580
  994.2 238.4 %copy-start.28 = (f32[2048]{0:T(1024)S(1)}, f32[2048]{0:T(1024)}, u32[]{:S(2)}) copy-start(f32[2048]{0:T(1024)} %get-tuple-element.50) | copy-start | bytes 24580
  994.2 331.7 %copy-start.34 = (f32[128]{0:T(128)S(1)}, f32[128]{0:T(128)}, u32[]{:S(2)}) copy-start(f32[128]{0:T(128)} %copy-done.33) | copy-start | bytes 1540
  994.2 331.7 %copy-start.39 = (f32[128]{0:T(128)S(1)}, f32[128]{0:T(128)}, u32[]{:S(2)}) copy-start(f32[128]{0:T(128)} %copy-done.38) | copy-start | bytes 1540
  994.2 331.7 %copy-start.43 = (f32[128]{0:T(128)S(1)}, f32[128]{0:T(128)}, u32[]{:S(2)}) copy-start(f32[128]{0:T(128)} %copy-done.42) | copy-start | bytes 1540
  994.3 331.7 %copy-start.45 = (f32[128]{0:T(128)S(1)}, f32[128]{0:T(128)}, u32[]{:S(2)}) copy-start(f32[128]{0:T(128)} %copy-done.44) | copy-start | bytes 1540
  (40 other events, 520.1 us)
Sparse Core Ops, SparseCore 0:
  10.9 56.6 all-gather.11
  69.8 88.3 all-gather.9
  160.4 47.9 all-gather.13
  213.1 88.8 reduce-scatter.16
  304.1 67.8 all-gather.17
  374.1 88.1 all-gather.15
  464.6 55.5 all-gather.19
  521.9 88.3 all-gather.21
  630.7 92.7 reduce-scatter.20
  729.4 90.7 all-gather.23
  824.1 77.8 reduce-scatter.30
  906.0 85.6 reduce-scatter.28
  995.5 65.3 reduce-scatter.26
  1065.3 74.3 reduce-scatter.24
  1142.1 88.8 reduce-scatter.22
  1233.4 92.4 reduce-scatter.18
where the time goes:
time: 1350 us; the launch traced here: 1340 us
  waiting for transfers between devices  978 us (72%)
  matrix products  129 us (10%)
  blocking collectives  101 us (7%)
  local copies, waits for them, and re-layouts  66.2 us (5%)
  other arithmetic  44.7 us (3%)
  between operations  15.2 us (1%)
    unnamed x20, waiting for transfers between devices  221 us
    reduce_scatter x1, waiting for transfers between devices, body(): lax.psum_scatter(jnp.einsum('ctf,cdf->td', picked, gate_up_full, preferre...  92.9 us
    all_gather x1, waiting for transfers between devices, body(): lax.all_gather(normed1.astype(jnp.bfloat16), 'tensor', axis=0, tiled=True)  90.6 us
    all_gather x1, waiting for transfers between devices, body(): lax.all_gather(normed2.astype(jnp.bfloat16), 'tensor', axis=0, tiled=True)  90.3 us
    all_gather x1, waiting for transfers between devices, body(): grad_rows = lax.all_gather(cotangent, 'tensor', axis=0, tiled=True)  90 us
    reduce_scatter x1, waiting for transfers between devices, body(): lax.psum_scatter(jnp.einsum('cte,cde->td', picked, qkv_full, preferred_el...  89.2 us
    reduce_scatter x1, waiting for transfers between devices, body(): lax.psum_scatter(jnp.dot(picked, out_full, preferred_element_type=jnp.flo...  88.2 us
    psum x1, blocking collectives, body(): lax.psum((gain1_grad, shift1_grad, gain2_grad, shift2_grad, bias_full), (...  82 us
  transfers between devices with their start and end apart: 16, of which 15 were waited for; matrix products, arithmetic and copies ran while one was open for 15% of the time, Pallas kernels for 0%

commit v1 on v0

v1 whole, which is shorter than its diff:
```python
import functools

import jax
import jax.numpy as jnp
from jax import lax
from jax.experimental import pallas as pl
from jax.experimental.pallas import tpu as pltpu
from jax.sharding import PartitionSpec as P

HEAD_DIM = 64
ROT = 16
DOCS = 4
EPS = 1e-05

ROWS = 128
WIDTH = 2048
TENSOR = 8
HALF = ROWS // 2
QUARTER = ROWS // 4
MESH = pl.DeviceIdType.MESH
BF16 = jnp.bfloat16
F32 = jnp.float32
VMEM_LIMIT = 56 * 2**20


def coordinates():
    tensor = lax.axis_index("tensor")
    return lax.axis_index("dp"), tensor // 2, lax.rem(tensor, 2)


class Around:
    def __init__(self):
        dp, y, z = coordinates()
        up, down, far = lax.rem(y + 1, 4), lax.rem(y + 3, 4), lax.rem(y + 2, 4)
        other = 1 - z
        self.me, self.across = y * 2 + z, y * 2 + other
        self.up, self.down, self.far = up * 2 + z, down * 2 + z, far * 2 + z
        self.up_o, self.down_o, self.far_o = up * 2 + other, down * 2 + other, far * 2 + other
        self.y, self.z = y, z
        self.y_up, self.y_down, self.y_far = up, down, far
        self.to_up, self.to_down, self.to_across = (dp, self.up), (dp, self.down), (dp, self.across)

    def peers(self):
        return [self.to_up, self.to_down, self.to_across]


class Ring:
    def __init__(self):
        dp = lax.axis_index("dp")
        tensor = lax.axis_index("tensor")
        zh, x, core = dp // 8, lax.rem(dp // 2, 4), lax.rem(dp, 2)
        self.zh, self.x, self.core, self.dp, self.tensor = zh, x, core, dp, tensor
        self.xs = [lax.rem(x + step, 4) for step in range(4)]
        self.to_x = [(self.index(zh, self.xs[step], core), tensor) for step in range(4)]
        self.to_zh = (self.index(1 - zh, x, core), tensor)
        self.to_core = (self.index(zh, x, 1 - core), tensor)

    def index(self, zh, x, core):
        return zh * 8 + x * 2 + core

    def peers(self):
        return self.to_x[1:] + [self.to_zh, self.to_core]


def greet(peers):
    barrier = pltpu.get_barrier_semaphore()
    for peer in peers:
        pl.semaphore_signal(barrier, inc=1, device_id=peer, device_id_type=MESH)
    pl.semaphore_wait(barrier, len(peers))


class Mail:
    def __init__(self, sends, receives):
        self.sends, self.receives = sends, receives
        self.out = []

    def send(self, number, source, target, device):
        copy = pltpu.make_async_remote_copy(
            src_ref=source,
            dst_ref=target,
            send_sem=self.sends.at[number],
            recv_sem=self.receives.at[number],
            device_id=device,
            device_id_type=MESH,
        )
        copy.start()
        self.out.append(copy)

    def landed(self, number, target, device):
        pltpu.make_async_remote_copy(
            src_ref=target,
            dst_ref=target,
            send_sem=self.sends.at[number],
            recv_sem=self.receives.at[number],
            device_id=device,
            device_id_type=MESH,
        ).wait_recv()

    def finish(self):
        for copy in self.out:
            copy.wait_send()


def gather_steps(around, mail, own, rows):
    a = around

    def part(slot, first, count):
        return rows.at[slot, pl.ds(first, count)]

    def begin():
        for number, first, device in (
            (0, 0, a.to_up),
            (1, HALF, a.to_down),
            (2, HALF, a.to_across),
            (3, HALF, a.to_up),
            (4, 0, a.to_down),
            (5, 0, a.to_across),
        ):
            mail.send(number, own.at[pl.ds(first, HALF)], part(a.me, first, HALF), device)

    def pass_on(number, slot, first, count, device):
        mail.send(number, part(slot, first, count), part(slot, first, count), device)

    def got(number, slot, first, count):
        mail.landed(number, part(slot, first, count), a.to_up)

    def one():
        got(0, a.down, 0, HALF)
        pass_on(6, a.down, 0, HALF, a.to_up)
        pass_on(7, a.down, 0, HALF, a.to_across)
        got(1, a.up, HALF, HALF)
        pass_on(8, a.up, HALF, HALF, a.to_down)
        got(2, a.across, HALF, HALF)
        pass_on(9, a.across, HALF, HALF, a.to_up)
        pass_on(10, a.across, HALF, HALF, a.to_down)

    def two():
        got(4, a.up, 0, HALF)
        pass_on(11, a.up, 0, HALF, a.to_across)
        got(3, a.down, HALF, HALF)
        got(5, a.across, 0, HALF)

    def three():
        got(6, a.far, 0, HALF)
        pass_on(12, a.far, 0, HALF, a.to_across)
        got(8, a.far, HALF, HALF)

    def four():
        got(9, a.down_o, HALF, HALF)
        pass_on(13, a.down_o, HALF, QUARTER, a.to_up)
        got(10, a.up_o, HALF, HALF)
        pass_on(14, a.up_o, HALF + QUARTER, QUARTER, a.to_down)

    def five():
        got(7, a.down_o, 0, HALF)
        got(11, a.up_o, 0, HALF)

    def six():
        got(13, a.far_o, HALF, QUARTER)
        got(14, a.far_o, HALF + QUARTER, QUARTER)
        got(12, a.far_o, 0, HALF)

    return begin, one, two, three, four, five, six


GATHER_MAILS = 15


def gather_kernel(own, rows, sends, receives, local):
    around = Around()
    mail = Mail(sends, receives)
    keep = pltpu.make_async_copy(own, rows.at[around.me], local.at[0])
    keep.start()
    greet(around.peers())
    for step in gather_steps(around, mail, own, rows):
        step()
    mail.finish()
    keep.wait()


def gather_rows(own, collective):
    return pl.pallas_call(
        gather_kernel,
        out_shape=jax.ShapeDtypeStruct((TENSOR,) + own.shape, own.dtype),
        in_specs=[pl.BlockSpec(memory_space=pltpu.VMEM)],
        out_specs=pl.BlockSpec(memory_space=pl.ANY),
        scratch_shapes=[
            pltpu.SemaphoreType.DMA((GATHER_MAILS,)),
            pltpu.SemaphoreType.DMA((GATHER_MAILS,)),
            pltpu.SemaphoreType.DMA((1,)),
        ],
        compiler_params=pltpu.CompilerParams(
            collective_id=collective, has_side_effects=True, vmem_limit_bytes=VMEM_LIMIT
        ),
        name="gather_rows",
    )(own)


IDS = 4


def gather_weights_kernel(
    own, ids, shard, rows, id_rows, full, sends, receives, w_sends, w_receives, i_sends, i_receives, local
):
    around = Around()
    ring = Ring()
    mail, wmail, imail = (
        Mail(sends, receives),
        Mail(w_sends, w_receives),
        Mail(i_sends, i_receives),
    )
    a, r = around, ring
    keeps = [
        pltpu.make_async_copy(own, rows.at[a.me], local.at[0]),
        pltpu.make_async_copy(ids, id_rows.at[a.z, a.y], local.at[1]),
    ]

    def block(zh, x, core):
        first = pl.multiple_of(r.index(zh, x, core) * ROWS, ROWS)
        return full.at[:, pl.ds(first, ROWS), :]

    mine = block(r.zh, r.x, r.core)
    keeps.append(pltpu.make_async_copy(shard, mine, local.at[2]))
    for keep in keeps:
        keep.start()
    greet(a.peers() + r.peers())

    def share(number, zh, x, device):
        wmail.send(number, block(zh, x, r.core), block(zh, x, r.core), device)

    def came(number, zh, x, core):
        wmail.landed(number, block(zh, x, core), r.to_core)

    begin, one, two, three, four, five, six = gather_steps(a, mail, own, rows)
    begin()
    imail.send(0, ids, id_rows.at[a.z, a.y], a.to_up)
    imail.send(1, ids, id_rows.at[a.z, a.y], a.to_down)
    wmail.send(0, shard, mine, r.to_zh)
    for step in (1, 2, 3):
        wmail.send(step, shard, mine, r.to_x[step])
    wmail.send(7, shard, mine, r.to_core)
    imail.landed(0, id_rows.at[a.z, a.y_down], a.to_up)
    imail.send(2, id_rows.at[a.z, a.y_down], id_rows.at[a.z, a.y_down], a.to_up)
    imail.landed(1, id_rows.at[a.z, a.y_up], a.to_up)
    imail.landed(2, id_rows.at[a.z, a.y_far], a.to_up)
    keeps[1].wait()
    imail.send(3, id_rows.at[a.z], id_rows.at[a.z], a.to_across)
    one()
    came(0, 1 - r.zh, r.x, r.core)
    for step in (1, 2, 3):
        share(3 + step, 1 - r.zh, r.x, r.to_x[step])
    share(8, 1 - r.zh, r.x, r.to_core)
    two()
    for step in (1, 2, 3):
        came(step, r.zh, r.xs[4 - step], r.core)
        share(8 + step, r.zh, r.xs[4 - step], r.to_core)
    three()
    four()
    for step in (1, 2, 3):
        came(3 + step, 1 - r.zh, r.xs[4 - step], r.core)
        share(11 + step, 1 - r.zh, r.xs[4 - step], r.to_core)
    five()
    six()
    sibling = 1 - r.core
    came(7, r.zh, r.x, sibling)
    came(8, 1 - r.zh, r.x, sibling)
    for step in (1, 2, 3):
        came(8 + step, r.zh, r.xs[4 - step], sibling)
        came(11 + step, 1 - r.zh, r.xs[4 - step], sibling)
    imail.landed(3, id_rows.at[1 - a.z], a.to_up)
    mail.finish()
    wmail.finish()
    imail.finish()
    keeps[0].wait()
    keeps[2].wait()


WEIGHT_MAILS = 15


def gather_weights(own, ids, shard, collective):
    parts, rows, columns = shard.shape
    return pl.pallas_call(
        gather_weights_kernel,
        out_shape=(
            jax.ShapeDtypeStruct((TENSOR,) + own.shape, own.dtype),
            jax.ShapeDtypeStruct((2, 4) + ids.shape, ids.dtype),
            jax.ShapeDtypeStruct((parts, rows * 16, columns), shard.dtype),
        ),
        in_specs=[pl.BlockSpec(memory_space=pltpu.VMEM)] * 3,
        out_specs=(pl.BlockSpec(memory_space=pl.ANY),) * 3,
        scratch_shapes=[
            pltpu.SemaphoreType.DMA((GATHER_MAILS,)),
            pltpu.SemaphoreType.DMA((GATHER_MAILS,)),
            pltpu.SemaphoreType.DMA((WEIGHT_MAILS,)),
            pltpu.SemaphoreType.DMA((WEIGHT_MAILS,)),
            pltpu.SemaphoreType.DMA((IDS,)),
            pltpu.SemaphoreType.DMA((IDS,)),
            pltpu.SemaphoreType.DMA((3,)),
        ],
        compiler_params=pltpu.CompilerParams(
            collective_id=collective, has_side_effects=True, vmem_limit_bytes=VMEM_LIMIT
        ),
        name="gather_weights",
    )(own, ids, shard)


def added(*terms):
    total = terms[0].astype(F32)
    for term in terms[1:]:
        total = total + term.astype(F32)
    return total


SCATTER_MAILS = 17
SCATTER_ROWS = (32, 32, 64, 64, 64, 64, 32, 32, 64, 64, 64, 32, 32, 64, 64, 64, 64)
SCATTER_FIRST = tuple(sum(SCATTER_ROWS[:k]) for k in range(SCATTER_MAILS))


def scatter_steps(around, mail, parts, total, land):
    a = around

    def part(slot, first, count):
        return parts.at[slot, pl.ds(first, count)]

    def box(number):
        return land.at[pl.ds(SCATTER_FIRST[number], SCATTER_ROWS[number])]

    def direct(number, slot, first, device):
        mail.send(number, part(slot, first, SCATTER_ROWS[number]), box(number), device)

    def got(number):
        mail.landed(number, box(number), a.to_up)

    def fold(stage, slot, first, others=()):
        count = SCATTER_ROWS[stage]
        terms = [part(slot, first, count)[...], box(stage)[...]]
        terms += [box(other)[...] for other in others]
        box(stage)[...] = added(*terms).astype(BF16)

    def begin():
        direct(0, a.far_o, 96, a.to_up)
        direct(1, a.far_o, 64, a.to_down)
        direct(2, a.far_o, 0, a.to_across)
        direct(3, a.far, 64, a.to_up)
        direct(4, a.up_o, 0, a.to_across)
        direct(5, a.down_o, 0, a.to_across)
        direct(6, a.down_o, 96, a.to_down)
        direct(7, a.up_o, 64, a.to_up)
        direct(8, a.down, 64, a.to_down)
        direct(9, a.across, 0, a.to_across)

    def one():
        got(1)
        fold(1, a.down_o, 64)
        mail.send(11, box(1), box(11), a.to_down)
        got(0)
        fold(0, a.up_o, 96)
        mail.send(12, box(0), box(12), a.to_up)
        got(2)
        fold(2, a.far, 0)
        mail.send(10, box(2), box(10), a.to_down)
        got(3)
        fold(3, a.up, 64)
        mail.send(13, box(3), box(13), a.to_up)

    def two():
        got(4)
        fold(4, a.up, 0)
        mail.send(14, box(4), box(14), a.to_up)
        got(5)
        got(10)
        fold(5, a.down, 0, (10,))
        mail.send(15, box(5), box(15), a.to_down)
        got(6)
        got(7)
        got(11)
        got(12)
        upper = added(part(a.across, 64, 32)[...], box(7)[...], box(11)[...]).astype(BF16)
        lower = added(part(a.across, 96, 32)[...], box(6)[...], box(12)[...]).astype(BF16)
        land.at[pl.ds(SCATTER_FIRST[6], 32)][...] = upper
        land.at[pl.ds(SCATTER_FIRST[7], 32)][...] = lower
        both = land.at[pl.ds(SCATTER_FIRST[6], 64)]
        mail.send(16, both, box(16), a.to_across)

    def three():
        got(9)
        got(14)
        got(15)
        total[pl.ds(0, HALF), :] = added(
            part(a.me, 0, HALF)[...], box(9)[...], box(14)[...], box(15)[...]
        )
        got(8)
        got(13)
        got(16)
        total[pl.ds(HALF, HALF), :] = added(
            part(a.me, HALF, HALF)[...], box(8)[...], box(13)[...], box(16)[...]
        )

    return begin, one, two, three


def scatter_kernel(parts, total, land, sends, receives):
    around = Around()
    mail = Mail(sends, receives)
    greet(around.peers())
    for step in scatter_steps(around, mail, parts, total, land):
        step()
    mail.finish()


def scatter_rows(parts, collective):
    return pl.pallas_call(
        scatter_kernel,
        out_shape=jax.ShapeDtypeStruct(parts.shape[1:], F32),
        in_specs=[pl.BlockSpec(memory_space=pltpu.VMEM)],
        out_specs=pl.BlockSpec(memory_space=pltpu.VMEM),
        scratch_shapes=[
            pltpu.VMEM((sum(SCATTER_ROWS), parts.shape[2]), parts.dtype),
            pltpu.SemaphoreType.DMA((SCATTER_MAILS,)),
            pltpu.SemaphoreType.DMA((SCATTER_MAILS,)),
        ],
        compiler_params=pltpu.CompilerParams(
            collective_id=collective, has_side_effects=True, vmem_limit_bytes=VMEM_LIMIT
        ),
        name="scatter_rows",
    )(parts)


def scatter_weights_kernel(
    parts, grads, total, shard, land, w_land, w_sum, sends, receives, w_sends, w_receives
):
    around, ring = Around(), Ring()
    mail, wmail = Mail(sends, receives), Mail(w_sends, w_receives)
    a, r = around, ring
    greet(a.peers() + r.peers())
    begin, one, two, three = scatter_steps(a, mail, parts, total, land)
    begin()
    blocks = [(side, step) for step in (1, 2, 3, 0) for side in (0, 1)]

    def place(side, step):
        zh = r.zh if side == 0 else 1 - r.zh
        return zh * 4 + r.xs[step]

    for number, (side, step) in enumerate(blocks):
        wmail.send(number, grads.at[place(side, step), 1 - r.core], w_land.at[number], r.to_core)
    for number, (side, step) in enumerate(blocks):
        wmail.landed(number, w_land.at[number], r.to_core)
        w_land[number] = added(grads[place(side, step), r.core], w_land[number]).astype(BF16)
        if step:
            wmail.send(8 + number, w_land.at[number], w_land.at[8 + number], r.to_x[step])
    one()
    two()
    for number in range(6):
        wmail.landed(8 + number, w_land.at[8 + number], r.to_core)
    w_land[7] = added(w_land[7], w_land[9], w_land[11], w_land[13]).astype(BF16)
    wmail.send(14, w_land.at[7], w_land.at[14], r.to_zh)
    w_sum[...] = added(w_land[6], w_land[8], w_land[10], w_land[12])
    three()
    wmail.landed(14, w_land.at[14], r.to_core)
    shard[...] = added(w_sum[...], w_land[14])
    mail.finish()
    wmail.finish()


def scatter_weights(parts, grads, collective):
    block = grads.shape[2:]
    return pl.pallas_call(
        scatter_weights_kernel,
        out_shape=(
            jax.ShapeDtypeStruct(parts.shape[1:], F32),
            jax.ShapeDtypeStruct(block, F32),
        ),
        in_specs=[pl.BlockSpec(memory_space=pltpu.VMEM)] * 2,
        out_specs=(pl.BlockSpec(memory_space=pltpu.VMEM),) * 2,
        scratch_shapes=[
            pltpu.VMEM((sum(SCATTER_ROWS), parts.shape[2]), parts.dtype),
            pltpu.VMEM((15,) + block, grads.dtype),
            pltpu.VMEM(block, F32),
            pltpu.SemaphoreType.DMA((SCATTER_MAILS,)),
            pltpu.SemaphoreType.DMA((SCATTER_MAILS,)),
            pltpu.SemaphoreType.DMA((15,)),
            pltpu.SemaphoreType.DMA((15,)),
        ],
        compiler_params=pltpu.CompilerParams(
            collective_id=collective, has_side_effects=True, vmem_limit_bytes=VMEM_LIMIT
        ),
        name="scatter_weights",
    )(parts, grads)


SUM_ROWS, SUM_NORMS = 72, 64


def sum_kernel(values, total, boxes, sends, receives):
    a, r = Around(), Ring()
    mail = Mail(sends, receives)
    x_peers = r.to_x[1:]
    z_peers = [
        (r.index(1 - r.zh, r.x, r.core), r.tensor),
        (r.index(r.zh, r.x, 1 - r.core), r.tensor),
        (r.index(1 - r.zh, r.x, 1 - r.core), r.tensor),
    ]
    y_peers = [(r.dp, a.up), (r.dp, a.far), (r.dp, a.down)]
    greet(x_peers + z_peers + y_peers + [a.to_across])

    def stage(base, count, mine, sources, peers):
        view = pl.ds(0, count)
        for number, peer in enumerate(peers):
            mail.send(base + number, boxes.at[base + mine, view], boxes.at[base + mine, view], peer)
        for number, source in enumerate(sources):
            mail.landed(base + number, boxes.at[base + source, view], peers[0])
        result = boxes[base, view]
        for k in range(1, len(peers) + 1):
            result = result + boxes[base + k, view]
        return result

    boxes[r.x] = values[...]
    first = stage(0, SUM_ROWS, r.x, [r.xs[3], r.xs[2], r.xs[1]], x_peers)
    place = r.zh * 2 + r.core
    boxes[4 + place] = first
    second = stage(
        4,
        SUM_ROWS,
        place,
        [(1 - r.zh) * 2 + r.core, r.zh * 2 + 1 - r.core, (1 - r.zh) * 2 + 1 - r.core],
        z_peers,
    )
    total[...] = second
    boxes[8 + a.y, pl.ds(0, SUM_NORMS)] = second[:SUM_NORMS]
    third = stage(8, SUM_NORMS, a.y, [a.y_down, a.y_far, a.y_up], y_peers)
    boxes[12 + a.z, pl.ds(0, SUM_NORMS)] = third
    total[pl.ds(0, SUM_NORMS), :] = stage(12, SUM_NORMS, a.z, [1 - a.z], [a.to_across])
    mail.finish()


def sum_all(values, collective):
    return pl.pallas_call(
        sum_kernel,
        out_shape=jax.ShapeDtypeStruct(values.shape, F32),
        in_specs=[pl.BlockSpec(memory_space=pltpu.VMEM)],
        out_specs=pl.BlockSpec(memory_space=pltpu.VMEM),
        scratch_shapes=[
            pltpu.VMEM((14, SUM_ROWS, 128), F32),
            pltpu.SemaphoreType.DMA((13,)),
            pltpu.SemaphoreType.DMA((13,)),
        ],
        compiler_params=pltpu.CompilerParams(
            collective_id=collective, has_side_effects=True, vmem_limit_bytes=VMEM_LIMIT
        ),
        name="sum_all",
    )(values)


def norm_parts(values, gain, shift):
    centred = values - jnp.mean(values, axis=-1, keepdims=True)
    variance = jnp.mean(centred * centred, axis=-1, keepdims=True)
    rinv = lax.rsqrt(variance + EPS)
    normal = centred * rinv
    return (normal * gain + shift, normal, rinv)


def norm_back(incoming, normal, rinv, gain):
    scaled = incoming * gain
    inner = (
        scaled
        - jnp.mean(scaled, axis=-1, keepdims=True)
        - normal * jnp.mean(scaled * normal, axis=-1, keepdims=True)
    )
    return (rinv * inner, jnp.sum(incoming * normal, axis=0), jnp.sum(incoming, axis=0))


def angles(group_ids):
    group = group_ids.shape[0]
    index = jnp.arange(group, dtype=jnp.int32)
    numbers = jnp.arange(DOCS, dtype=jnp.int32)
    before = (group_ids[None, :] >= 0) & (group_ids[None, :] < numbers[:, None])
    starts = jnp.sum(before.astype(jnp.int32), axis=1)
    offset = jnp.sum(jnp.where(group_ids[:, None] == numbers[None, :], starts[None, :], 0), axis=1)
    position = (index - offset).astype(jnp.float32)
    freq = jnp.power(10000.0, -2.0 * jnp.arange(ROT // 2, dtype=jnp.float32) / ROT)
    angle = position[:, None] * freq[None, :]
    return (jnp.cos(angle), jnp.sin(angle))


def rotate(values, cosine, sine):
    half = ROT // 2
    first_part = values[..., :half]
    second_part = values[..., half:ROT]
    cosine = cosine[:, None, :]
    sine = sine[:, None, :]
    return jnp.concatenate(
        [
            first_part * cosine - second_part * sine,
            second_part * cosine + first_part * sine,
            values[..., ROT:],
        ],
        axis=-1,
    )


def allowed_keys(row_ids, row_first, col_ids):
    rows = row_first + jnp.arange(row_ids.shape[0], dtype=jnp.int32)
    cols = jnp.arange(col_ids.shape[0], dtype=jnp.int32)
    same = (
        (row_ids[:, None] == col_ids[None, :])
        & (col_ids[None, :] >= 0)
        & (cols[None, :] < rows[:, None])
    )
    return same | (cols[None, :] == rows[:, None])


def product(spec, left, right):
    return jnp.einsum(spec, left, right, preferred_element_type=F32)


def body(
    tokens,
    doc_ids,
    qkv_weight,
    qkv_bias,
    out_weight,
    norm1_gain,
    norm1_shift,
    norm2_gain,
    norm2_shift,
    gate_up_weight,
    down_weight,
    cotangent,
):
    inputs = tokens.astype(F32)
    group = ROWS * TENSOR
    feed_shard = jnp.concatenate([jnp.swapaxes(gate_up_weight, 1, 2), down_weight[None]])
    feed = lax.all_gather(feed_shard, "dp", axis=2, tiled=True)
    normed1, normal1, rinv1 = norm_parts(inputs, norm1_gain, norm1_shift)
    shard = jnp.concatenate([qkv_weight, out_weight.T[None]])
    rows1, id_rows, projections = gather_weights(
        normed1.astype(BF16), jnp.broadcast_to(doc_ids[None], (8, ROWS)), shard, 0
    )
    rows1 = rows1.reshape(group, WIDTH)
    qkv_full, out_full = projections[:3], projections[3]
    group_ids = jnp.swapaxes(id_rows[:, :, 0], 0, 1).reshape(group)
    local_width = qkv_full.shape[2]
    heads = local_width // HEAD_DIM
    scale = HEAD_DIM ** (-0.5)
    cosine, sine = angles(group_ids)
    projected = product("td,cde->cte", rows1, qkv_full) + qkv_bias[:, None, :]
    query = rotate(projected[0].reshape(group, heads, HEAD_DIM), cosine, sine).astype(BF16)
    keys_all = rotate(projected[1].reshape(group, heads, HEAD_DIM), cosine, sine).astype(BF16)
    values_all = projected[2].reshape(group, heads, HEAD_DIM).astype(BF16)
    block = min(512, group)
    outputs = []
    lse_parts = []
    for first_row in range(0, group, block):
        query_block = query[first_row : first_row + block]
        scores = product("qhd,khd->hqk", query_block, keys_all) * scale
        allow = allowed_keys(group_ids[first_row : first_row + block], first_row, group_ids)
        masked = jnp.where(allow[None], scores, -1e30)
        highest = jnp.max(masked, axis=-1, keepdims=True)
        expon = jnp.exp(masked - highest)
        totals = jnp.sum(expon, axis=-1, keepdims=True)
        probs = expon / totals
        lse_parts.append(highest + jnp.log(totals))
        outputs.append(product("hqk,khd->qhd", probs.astype(BF16), values_all))
    attended = jnp.concatenate(outputs, axis=0).reshape(group, local_width).astype(BF16)
    log_totals = jnp.concatenate(lse_parts, axis=1)
    branch = product("te,de->td", attended, out_full).astype(BF16)
    mixed = inputs + scatter_rows(branch.reshape(TENSOR, ROWS, WIDTH), 1)
    normed2, normal2, rinv2 = norm_parts(mixed, norm2_gain, norm2_shift)
    rows2 = gather_rows(normed2.astype(BF16), 2).reshape(group, WIDTH)
    grad_rows = gather_rows(cotangent, 3).reshape(group, WIDTH)
    gate_up = product("td,cfd->ctf", rows2, feed[:2])
    gate = gate_up[0]
    upward = gate_up[1]
    sigma = jax.nn.sigmoid(gate)
    hidden = (gate * sigma * upward).astype(BF16)
    feed_out = product("tf,fd->td", hidden, feed[2]).astype(BF16)
    grad_hidden = product("td,fd->tf", grad_rows, feed[2])
    grad_gate = grad_hidden * upward * sigma * (1.0 + gate * (1.0 - sigma))
    grad_upward = grad_hidden * (gate * sigma)
    grad_gate_up = jnp.stack([grad_gate, grad_upward]).astype(BF16)
    grad_feed = product("ctf,cfd->td", grad_gate_up, feed[:2]).astype(BF16)
    grad_normed2 = scatter_rows(grad_feed.reshape(TENSOR, ROWS, WIDTH), 4)
    layer_out = (mixed + scatter_rows(feed_out.reshape(TENSOR, ROWS, WIDTH), 5)).astype(BF16)
    down_grad = product("tf,td->fd", hidden, grad_rows).astype(BF16)
    gate_up_grad = product("ctf,td->cfd", grad_gate_up, rows2).astype(BF16)
    units = down_grad.shape[0]
    feed_grad = jnp.concatenate([gate_up_grad, down_grad[None]]).reshape(3 * units, 16, ROWS)
    feed_grad = lax.psum_scatter(
        jnp.swapaxes(feed_grad, 0, 1), "dp", scatter_dimension=0, tiled=False
    ).astype(F32)
    gate_up_shard = jnp.swapaxes(feed_grad[: 2 * units].reshape(2, units, ROWS), 1, 2)
    down_shard = feed_grad[2 * units :]
    back2, gain2_grad, shift2_grad = norm_back(grad_normed2, normal2, rinv2, norm2_gain)
    grad_mixed = cotangent.astype(F32) + back2
    branch_grad = gather_rows(grad_mixed.astype(BF16), 6).reshape(group, WIDTH)
    out_grad = product("td,te->de", branch_grad, attended).astype(BF16)
    grad_attended = product("td,de->te", branch_grad, out_full)
    grad_attended = grad_attended.astype(BF16).reshape(group, heads, HEAD_DIM)
    grad_query_parts = []
    grad_keys = jnp.zeros((group, heads, HEAD_DIM), F32)
    grad_values = jnp.zeros((group, heads, HEAD_DIM), F32)
    for first_row in range(0, group, block):
        query_block = query[first_row : first_row + block]
        scores = product("qhd,khd->hqk", query_block, keys_all) * scale
        allow = allowed_keys(group_ids[first_row : first_row + block], first_row, group_ids)
        probs = jnp.where(
            allow[None], jnp.exp(scores - log_totals[:, first_row : first_row + block]), 0.0
        )
        grad_block = grad_attended[first_row : first_row + block]
        grad_probs = product("qhd,khd->hqk", grad_block, values_all)
        inner = jnp.sum(probs * grad_probs, axis=-1, keepdims=True)
        grad_scores = (probs * (grad_probs - inner)).astype(BF16)
        grad_query_parts.append(product("hqk,khd->qhd", grad_scores, keys_all) * scale)
        grad_keys = grad_keys + product("hqk,qhd->khd", grad_scores, query_block) * scale
        grad_values = grad_values + product("hqk,qhd->khd", probs.astype(BF16), grad_block)
    grad_query = rotate(jnp.concatenate(grad_query_parts, axis=0), cosine, -sine)
    grad_keys = rotate(grad_keys, cosine, -sine)
    grad_pre = (
        jnp.stack([grad_query, grad_keys, grad_values]).reshape(3, group, local_width).astype(BF16)
    )
    bias_part = jnp.sum(grad_pre.astype(F32), axis=1)
    qkv_grad = product("td,cte->cde", rows1, grad_pre).astype(BF16)
    grad_back = product("cte,cde->td", grad_pre, qkv_full).astype(BF16)
    grads = jnp.concatenate([qkv_grad, out_grad[None]]).reshape(4, 8, 2, ROWS, local_width)
    grad_normed1, weight_shard = scatter_weights(
        grad_back.reshape(TENSOR, ROWS, WIDTH), jnp.moveaxis(grads, 0, 2), 7
    )
    qkv_shard, out_shard = weight_shard[:3], weight_shard[3].T
    back1, gain1_grad, shift1_grad = norm_back(grad_normed1, normal1, rinv1, norm1_gain)
    token_grad = (grad_mixed + back1).astype(BF16)
    norms = jnp.concatenate([gain1_grad, shift1_grad, gain2_grad, shift2_grad, bias_part.reshape(-1)])
    sums = sum_all(jnp.pad(norms.reshape(-1, 128), ((0, 2), (0, 0))), 8)
    gain1_sum, shift1_sum, gain2_sum, shift2_sum = sums[:64].reshape(4, WIDTH)
    bias_grad = sums[64:70].reshape(3, local_width)
    return (
        layer_out,
        token_grad,
        qkv_shard,
        bias_grad,
        out_shard,
        gain1_sum,
        shift1_sum,
        gain2_sum,
        shift2_sum,
        gate_up_shard,
        down_shard,
    )


def solution(mesh):
    in_specs = (
        P(("dp", "tensor"), None),
        P(("dp", "tensor")),
        P(None, "dp", "tensor"),
        P(None, "tensor"),
        P("tensor", "dp"),
        P(),
        P(),
        P(),
        P(),
        P(None, "dp", "tensor"),
        P("tensor", "dp"),
        P(("dp", "tensor"), None),
    )
    out_specs = (
        P(("dp", "tensor"), None),
        P(("dp", "tensor"), None),
        P(None, "dp", "tensor"),
        P(None, "tensor"),
        P("tensor", "dp"),
        P(),
        P(),
        P(),
        P(),
        P(None, "dp", "tensor"),
        P("tensor", "dp"),
    )
    return jax.shard_map(body, mesh=mesh, in_specs=in_specs, out_specs=out_specs, check_vma=False)
```

time: 1350 us -> 573 us (0.42)
  waiting for transfers between devices: 978 us -> 0.06 us
  Pallas kernels: 0 us -> 347 us
  blocking collectives: 101 us -> 0 us
  local copies, waits for them, and re-layouts: 66.2 us -> 43.7 us
  matrix products: 129 us -> 112 us
    all_gather x8 -> x1, waiting for transfers between devices: 476 us -> 0.02 us  [body(): feed = lax.all_gather(feed_shard, 'dp', axis=2, tiled=True)]
    pallas_call x0 -> x9, Pallas kernels: none -> 347 us  [the longest x3 115 us: scatter_rows(): pl.pallas_call(scatter_kernel, out_shape=jax.ShapeDtypeStruct(parts.shape...]
    reduce_scatter x4 -> x1, waiting for transfers between devices: 281 us -> 0.01 us  [body(): lax.psum_scatter(jnp.swapaxes(feed_grad, 0, 1), 'dp', scatter_dimension=0...]
    unnamed x20 -> x2, waiting for transfers between devices: 221 us -> 0.03 us
    psum x1 -> x0, blocking collectives: 82 us -> none  [body(): lax.psum((gain1_grad, shift1_grad, gain2_grad, shift2_grad, bias_full), (...]
    unnamed x126 -> x105, local copies, waits for them, and re-layouts: 61.9 us -> 18.1 us
    all_gather x1 -> x0, blocking collectives: 19.4 us -> none  [body(): lax.all_gather(doc_ids.astype(jnp.bfloat16), 'tensor', axis=0, tiled=True)]
    dot_general x24, matrix products: 129 us -> 112 us  [product(): return jnp.einsum(spec, left, right, preferred_element_type=F32)]
  transfers between devices with their start and end apart: 16 -> 2, of which waited for: 15 -> 0; matrix products, arithmetic and copies ran while one was open for 15% -> 24% of each run, Pallas kernels for 0% -> 62%
where the time goes in v1:
time: 573 us; the launch traced here: 563 us
  Pallas kernels  347 us (61%)
  matrix products  112 us (20%)
  other arithmetic  44.8 us (8%)
  local copies, waits for them, and re-layouts  43.7 us (8%)
  between operations  15.2 us (3%)
    pallas_call x3, Pallas kernels, scatter_rows(): pl.pallas_call(scatter_kernel, out_shape=jax.ShapeDtypeStruct(parts.shape...  115 us
    dot_general x24, matrix products, product(): return jnp.einsum(spec, left, right, preferred_element_type=F32)  112 us
    pallas_call x3, Pallas kernels, gather_rows(): pl.pallas_call(gather_kernel, out_shape=jax.ShapeDtypeStruct((TENSOR,) +...  103 us
    pallas_call x1, Pallas kernels, gather_weights(): pl.pallas_call(gather_weights_kernel, out_shape=(jax.ShapeDtypeStruct((TE...  66.1 us
    pallas_call x1, Pallas kernels, scatter_weights(): pl.pallas_call(scatter_weights_kernel, out_shape=(jax.ShapeDtypeStruct(pa...  43.7 us
    pallas_call x1, Pallas kernels, sum_all(): pl.pallas_call(sum_kernel, out_shape=jax.ShapeDtypeStruct(values.shape, F...  18.8 us
    unnamed x105, local copies, waits for them, and re-layouts  18.1 us
  transfers between devices with their start and end apart: 2, of which 0 were waited for; matrix products, arithmetic and copies ran while one was open for 24% of the time, Pallas kernels for 62%

profile of v1, /device:TPU:0, one launch (start us, length us, event | category | flops | bytes accessed | tf_op | source)
XLA Modules:
  0.0 562.7 jit_solution(7403616500178727184)
XLA Ops:
  10.3 40.8 %gather_rows.4 = bf16[8,128,2048]{2,1,0:T(8,128)(2,1)} custom-call(bf16[128,2048]{1,0:T(8,128)(2,1)} %own.1), custom_call_target="tpu_custom_call" | custom-call | tf_op jit(solution)/shard_map/gather_rows/pallas_call | solution.py:182
  54.2 66.1 %gather_weights.1 = (bf16[8,128,2048]{2,1,0:T(8,128)(2,1)}, s32[2,4,8,128]{3,2,1,0:T(8,128)}, bf16[4,2048,256]{2,1,0:T(8,128)(2,1)}) custom-call(bf16[128,2048]{1,0:T(8,128)(2,1)} %fusion.56.own, s32[8,128]{1,0:T(8,128)} %broadcast_in_dim.48.ids, bf16[4,128,256]{2,1,0:T(8,128)(2,1)} %pad_maximum_fusion.14.shard), custom_call_target="tpu_custom_call" | custom-call | tf_op jit(solution)/shard_map/gather_weights/pallas_call | solution.py:283
  121.0 6.4 %add_bitcast_fusion = f32[3,1024,256]{1,2,0:T(8,128)S(1)} fusion(bf16[4,2048,256]{2,1,0:T(8,128)(2,1)} %get-tuple-element.16, bf16[1024,2048,1]{1,0,2:T(8,128)(2,1)} %bitcast.225, f32[3,256]{1,0:T(4,128)S(1)} %copy-done.36), kind=kOutput, calls=%fused_computation.35 | convolution fusion | flops 3222011904 | bytes 11537408 | tf_op jit(solution)/shard_map/td,cde->cte/dot_general | solution.py:614
  139.7 2.9 fusion.53
  142.7 3.4 fusion.54
  146.1 4.6 convolution_convert_fusion.2
  150.7 34.7 %scatter_rows.3 = f32[128,2048]{1,0:T(8,128)} custom-call(bf16[8,128,2048]{2,1,0:T(8,128)(2,1)} %bitcast.181), custom_call_target="tpu_custom_call" | custom-call | tf_op jit(solution)/shard_map/scatter_rows/pallas_call | solution.py:413
  188.1 32.9 %gather_rows.3 = bf16[8,128,2048]{2,1,0:T(8,128)(2,1)} custom-call(bf16[128,2048]{1,0:T(8,128)(2,1)} %add_convert_fusion.1.own), custom_call_target="tpu_custom_call" | custom-call | tf_op jit(solution)/shard_map/gather_rows/pallas_call | solution.py:182
  221.1 9.5 %convolution_bitcast_fusion = f32[2,1024,704]{1,2,0:T(8,128)S(1)} fusion(bf16[3,704,2048]{2,1,0:T(8,128)(2,1)} %all-gather.2.cloned.1.call-done, bf16[1024,2048,1]{1,0,2:T(8,128)(2,1)} %bitcast.193), kind=kOutput, calls=%fused_computation.56 | convolution fusion | flops 5905580032 | bytes 18612224 | tf_op jit(solution)/shard_map/td,cfd->ctf/dot_general | solution.py:614
  233.2 4.5 fusion.18
  237.7 6.0 %fusion.36 = (bf16[1,1024,704]{1,2,0:T(8,128)(2,1)S(1)}, bf16[1,1024,704]{1,2,0:T(8,128)(2,1)S(1)}) fusion(f32[2,1024,704]{1,2,0:T(8,128)S(1)} %convolution_bitcast_fusion, bf16[1024,2048]{1,0:T(8,128)(2,1)S(1)} %bitcast.190, bf16[3,704,2048]{2,1,0:T(8,128)(2,1)} %all-gather.2.cloned.1.call-done), kind=kOutput, calls=%fused_computation.73 | convolution fusion | flops 2962161664 | bytes 15728640 | tf_op jit(solution)/shard_map/td,fd->tf/dot_general | solution.py:614
  245.3 8.1 %convolution_convert_fusion = bf16[2,704,2048]{2,1,0:T(8,128)(2,1)} fusion(bf16[1024,2048,1]{1,0,2:T(8,128)(2,1)S(1)} %bitcast.194, bf16[1,1024,704]{1,2,0:T(8,128)(2,1)S(1)} %get-tuple-element.67, bf16[1,1024,704]{1,2,0:T(8,128)(2,1)S(1)} %get-tuple-element.66), kind=kOutput, calls=%fused_computation.22 | convolution fusion | flops 5909905408 | bytes 12845056 | tf_op jit(solution)/shard_map/ctf,td->cfd/dot_general | solution.py:614
  253.4 7.6 %pad_maximum_fusion = bf16[3,704,2048]{2,1,0:T(8,128)(2,1)} fusion(bf16[1,704,2048]{2,1,0:T(8,128)(2,1)} %fusion.18, bf16[2,704,2048]{2,1,0:T(8,128)(2,1)} %convolution_convert_fusion), kind=kLoop, calls=%fused_computation | loop fusion | flops 4325376 | bytes 17301504 | tf_op jit(solution)/shard_map/concatenate | solution.py:688
  261.0 10.1 %copy.59 = bf16[264,8,16,128]{3,2,1,0:T(8,128)(2,1)} copy(bf16[264,8,16,128]{3,1,2,0:T(8,128)(2,1)} %bitcast.179) | data formatting | bytes 17301504
  271.1 9.0 %copy.63 = bf16[2112,16,128]{2,0,1:T(8,128)(2,1)} copy(bf16[2112,16,128]{2,1,0:T(8,128)(2,1)} %bitcast.180) | data formatting | bytes 17301504 | tf_op jit(solution)/shard_map/reshape | solution.py:688
  280.2 7.7 %convolution_convert_fusion.1 = bf16[1024,2048]{1,0:T(8,128)(2,1)} fusion(bf16[3,704,2048]{2,1,0:T(8,128)(2,1)} %all-gather.2.cloned.1.call-done, bf16[1,1024,704]{1,2,0:T(8,128)(2,1)} %copy-done.14), kind=kOutput, calls=%fused_computation.30 | convolution fusion | flops 2954887168 | bytes 8519680 | tf_op jit(solution)/shard_map/tf,fd->td/dot_general | solution.py:614
  287.9 39.8 %scatter_rows.4 = f32[128,2048]{1,0:T(8,128)} custom-call(bf16[8,128,2048]{2,1,0:T(8,128)(2,1)} %bitcast.188), custom_call_target="tpu_custom_call" | custom-call | tf_op jit(solution)/shard_map/scatter_rows/pallas_call | solution.py:413
  327.7 11.2 %bitcast_convert_fusion.1 = bf16[1024,2048]{1,0:T(8,128)(2,1)} fusion(bf16[3,704,2048]{2,1,0:T(8,128)(2,1)} %all-gather.2.cloned.1.call-done, bf16[1,1024,704]{1,2,0:T(8,128)(2,1)S(1)} %copy-done.40, bf16[1,1024,704]{1,2,0:T(8,128)(2,1)S(1)} %copy-done.38), kind=kOutput, calls=%fused_computation.3 | convolution fusion | flops 5909118976 | bytes 12845056 | tf_op jit(solution)/shard_map/ctf,cfd->td/dot_general | solution.py:614
  338.9 40.6 %scatter_rows.5 = f32[128,2048]{1,0:T(8,128)} custom-call(bf16[8,128,2048]{2,1,0:T(8,128)(2,1)} %bitcast.187), custom_call_target="tpu_custom_call" | custom-call | tf_op jit(solution)/shard_map/scatter_rows/pallas_call | solution.py:413
  381.2 3.2 fusion.92
  384.4 29.6 %gather_rows.5 = bf16[8,128,2048]{2,1,0:T(8,128)(2,1)} custom-call(bf16[128,2048]{1,0:T(8,128)(2,1)} %get-tuple-element.62.own), custom_call_target="tpu_custom_call" | custom-call | tf_op jit(solution)/shard_map/gather_rows/pallas_call | solution.py:182
  414.1 3.9 convolution_convert_fusion.6
  423.6 7.8 %multiply_reduce_fusion.1 = (f32[4,512]{1,0:T(4,128)S(1)}, f32[4,512,1024]{2,1,0:T(8,128)}) fusion(f32[4,512,1024]{2,1,0:T(8,128)} %copy-done.1, f32[4,512]{1,0:T(4,128)S(1)} %log_add_fusion.1, pred[512,1024]{1,0:T(8,128)(4,1)S(1)} %get-tuple-element.89, bf16[512,4,64]{0,2,1:T(8,128)(2,1)S(1)} %bitcast.205, bf16[1024,4,64]{0,2,1:T(8,128)(2,1)S(1)} %bitcast.185), kind=kOutput, calls=%fused_computation.8 | convolution fusion | flops 278919168 | bytes 18104320 | tf_op jit(solution)/shard_map/qhd,khd->hqk/dot_general | solution.py:614
  431.4 8.1 %multiply_reduce_fusion = (f32[4,512]{1,0:T(4,128)S(1)}, f32[4,512,1024]{2,1,0:T(8,128)}) fusion(f32[4,512,1024]{2,1,0:T(8,128)} %copy-done, f32[4,512]{1,0:T(4,128)S(1)} %log_add_fusion, pred[512,1024]{1,0:T(8,128)(4,1)S(1)} %get-tuple-element.90, bf16[512,4,64]{0,2,1:T(8,128)(2,1)S(1)} %bitcast.203, bf16[1024,4,64]{0,2,1:T(8,128)(2,1)S(1)} %bitcast.186), kind=kOutput, calls=%fused_computation.5 | convolution fusion | flops 278919168 | bytes 18104320 | tf_op jit(solution)/shard_map/qhd,khd->hqk/dot_general | solution.py:614
  439.5 8.5 %multiply_convert_fusion = (bf16[4,512,1024]{2,1,0:T(8,128)(2,1)S(1)}, bf16[4,512,1024]{2,1,0:T(8,128)(2,1)S(1)}) fusion(f32[4,512,1024]{2,1,0:T(8,128)} %get-tuple-element.103, f32[4,512,1024]{2,1,0:T(8,128)S(1)} %bitcast.173, f32[4,512]{1,0:T(4,128)S(1)} %get-tuple-element.102, f32[4,512]{1,0:T(4,128)S(1)} %log_add_fusion, ...), kind=kLoop, calls=%fused_computation.4 | loop fusion | flops 25165824 | bytes 43024384 | tf_op jit(solution)/shard_map/convert_element_type | solution.py:713
  453.8 7.0 %fusion.17 = bf16[3,2048,256]{1,2,0:T(8,128)(2,1)} fusion(bf16[1024,2048,1]{1,0,2:T(8,128)(2,1)} %bitcast.226, bf16[1,1024,256]{2,1,0:T(8,128)(2,1)S(1)} %copy-done.12, bf16[1,1024,256]{2,1,0:T(8,128)(2,1)S(1)} %copy.50, bf16[1,1024,256]{2,1,0:T(8,128)(2,1)S(1)} %copy.49), kind=kOutput, calls=%fused_computation.37 | convolution fusion | flops 3224371200 | bytes 8912896 | tf_op jit(solution)/shard_map/td,cte->cde/dot_general | solution.py:614
  460.8 4.7 copy.53
  465.8 3.7 convolution_convert_fusion.5
  473.2 5.2 bitcast_convert_fusion
  478.4 43.7 %scatter_weights.1 = (f32[128,2048]{1,0:T(8,128)}, f32[4,128,256]{2,1,0:T(8,128)}) custom-call(bf16[8,128,2048]{2,1,0:T(8,128)(2,1)} %bitcast.195, bf16[8,2,4,128,256]{4,3,2,1,0:T(8,128)(2,1)} %maximum_bitcast_fusion.grads), custom_call_target="tpu_custom_call" | custom-call | tf_op jit(solution)/shard_map/scatter_weights/pallas_call | solution.py:468
  524.5 18.8 %sum_all.1 = f32[72,128]{1,0:T(8,128)} custom-call(f32[72,128]{1,0:T(8,128)} %pad.4.values), custom_call_target="tpu_custom_call" | custom-call | tf_op jit(solution)/shard_map/sum_all/pallas_call | solution.py:538
  549.4 2.5 fusion.61
  (187 shorter events, 55.0 us)
Async XLA Ops:
  7.2 43.9 %copy-start.24 = (bf16[3,128,256]{2,1,0:T(8,128)(2,1)S(1)}, bf16[3,128,256]{2,1,0:T(8,128)(2,1)}, u32[]{:S(2)}) copy-start(bf16[3,128,256]{2,1,0:T(8,128)(2,1)} %param.14) | copy-start | bytes 589828
  7.2 44.7 %copy-start.2 = (bf16[128,2048]{1,0:T(8,128)(2,1)S(1)}, bf16[128,2048]{1,0:T(8,128)(2,1)}, u32[]{:S(2)}) copy-start(bf16[128,2048]{1,0:T(8,128)(2,1)} %param.12) | copy-start | bytes 1572868
  7.2 45.1 %copy-start.27 = (f32[2048]{0:T(1024)S(1)}, f32[2048]{0:T(1024)}, u32[]{:S(2)}) copy-start(f32[2048]{0:T(1024)} %param.17) | copy-start | bytes 24580
  7.2 45.1 %copy-start.29 = (f32[2048]{0:T(1024)S(1)}, f32[2048]{0:T(1024)}, u32[]{:S(2)}) copy-start(f32[2048]{0:T(1024)} %param.18) | copy-start | bytes 24580
  7.2 213.8 %all-gather.2.cloned.1.call-start = ((), (), s32[]{:S(2)}) async-start(), calls=%async_computation.1 | async-start | bytes 9191424 | tf_op jit(solution)/shard_map/all_gather | solution.py:634
  9.3 44.3 %copy-start.35 = (s32[128]{0:T(128)S(1)}, s32[128]{0:T(128)}, u32[]{:S(2)}) copy-start(s32[128]{0:T(128)} %param.13) | copy-start | bytes 1540
  9.3 111.7 %copy-start.36 = (f32[3,256]{1,0:T(4,128)S(1)}, f32[3,256]{1,0:T(4,128)}, u32[]{:S(2)}) copy-start(f32[3,256]{1,0:T(4,128)} %param.15) | copy-start | bytes 9220
  9.3 542.6 %reduce-scatter.2.cloned.1.call-start = ((), (), s32[]{:S(2)}) async-start(), calls=%async_computation.2 | async-start | bytes 9191424 | tf_op jit(solution)/shard_map/reduce_scatter | solution.py:689
  52.0 75.5 %copy-start.31 = (f32[128]{0:T(128)}, f32[128]{0:T(128)S(1)}, u32[]{:S(2)}) copy-start(f32[128]{0:T(128)S(1)} %broadcast_multiply_fusion.5) | copy-start | bytes 1540
  52.3 75.1 %copy-start.33 = (f32[128]{0:T(128)}, f32[128]{0:T(128)S(1)}, u32[]{:S(2)}) copy-start(f32[128]{0:T(128)S(1)} %add_rsqrt_fusion.1) | copy-start | bytes 1540
  127.9 5.4 copy-start.8
  133.3 6.4 %copy-start = (f32[4,512,1024]{2,1,0:T(8,128)}, f32[4,512,1024]{2,1,0:T(8,128)S(1)}, u32[]{:S(2)}) copy-start(f32[4,512,1024]{2,1,0:T(8,128)S(1)} %get-tuple-element.97) | copy-start | bytes 25165828
  135.0 7.6 %copy-start.1 = (f32[4,512,1024]{2,1,0:T(8,128)}, f32[4,512,1024]{2,1,0:T(8,128)S(1)}, u32[]{:S(2)}) copy-start(f32[4,512,1024]{2,1,0:T(8,128)S(1)} %get-tuple-element.99) | copy-start | bytes 25165828
  150.7 36.4 %copy-start.26 = (f32[2048]{0:T(1024)S(1)}, f32[2048]{0:T(1024)}, u32[]{:S(2)}) copy-start(f32[2048]{0:T(1024)} %param.19) | copy-start | bytes 24580
  150.7 36.4 %copy-start.30 = (f32[2048]{0:T(1024)S(1)}, f32[2048]{0:T(1024)}, u32[]{:S(2)}) copy-start(f32[2048]{0:T(1024)} %param.20) | copy-start | bytes 24580
  237.7 7.6 %copy-start.5 = (bf16[8,128,2048]{2,1,0:T(8,128)(2,1)S(1)}, bf16[8,128,2048]{2,1,0:T(8,128)(2,1)}, u32[]{:S(2)}) copy-start(bf16[8,128,2048]{2,1,0:T(8,128)(2,1)} %gather_rows.3) | copy-start | bytes 12582916
  287.9 39.8 %copy-start.38 = (bf16[1,1024,704]{1,2,0:T(8,128)(2,1)S(1)}, bf16[1,1024,704]{1,2,0:T(8,128)(2,1)}, u32[]{:S(2)}) copy-start(bf16[1,1024,704]{1,2,0:T(8,128)(2,1)} %copy-done.37) | copy-start | bytes 4325380
  287.9 39.8 %copy-start.40 = (bf16[1,1024,704]{1,2,0:T(8,128)(2,1)S(1)}, bf16[1,1024,704]{1,2,0:T(8,128)(2,1)}, u32[]{:S(2)}) copy-start(bf16[1,1024,704]{1,2,0:T(8,128)(2,1)} %copy-done.39) | copy-start | bytes 4325380
  338.9 42.3 %copy-start.6 = (f32[128,2048]{1,0:T(8,128)S(1)}, f32[128,2048]{1,0:T(8,128)}, u32[]{:S(2)}) copy-start(f32[128,2048]{1,0:T(8,128)} %scatter_rows.4) | copy-start | bytes 3145732
  338.9 42.3 %copy-start.13 = (bf16[128,2048]{1,0:T(8,128)(2,1)S(1)}, bf16[128,2048]{1,0:T(8,128)(2,1)}, u32[]{:S(2)}) copy-start(bf16[128,2048]{1,0:T(8,128)(2,1)} %own.1) | copy-start | bytes 1572868
  384.4 33.7 %slice-start = ((s8[8388608]{0:T(1024)(128)(4,1)}), s8[4194304]{0:T(1024)(128)(4,1)S(1)}, s32[]{:S(2)}) async-start(s8[8388608]{0:T(1024)(128)(4,1)} %bitcast.170), calls=%async_computation.3 | async-start | bytes 8388608
  414.1 5.9 %slice-start.4 = ((s8[8388608]{0:T(1024)(128)(4,1)}), s8[4194304]{0:T(1024)(128)(4,1)S(1)}, s32[]{:S(2)}) async-start(s8[8388608]{0:T(1024)(128)(4,1)} %bitcast.174), calls=%async_computation.7 | async-start | bytes 8388608
  423.6 15.9 %slice-start.2 = ((s8[8388608]{0:T(1024)(128)(4,1)}), s8[4194304]{0:T(1024)(128)(4,1)S(1)}, s32[]{:S(2)}) async-start(s8[8388608]{0:T(1024)(128)(4,1)} %bitcast.172), calls=%async_computation.5 | async-start | bytes 8388608
  423.6 15.9 %slice-start.6 = ((s8[8388608]{0:T(1024)(128)(4,1)}), s8[4194304]{0:T(1024)(128)(4,1)S(1)}, s32[]{:S(2)}) async-start(s8[8388608]{0:T(1024)(128)(4,1)} %bitcast.176), calls=%async_computation.9 | async-start | bytes 8388608
  431.4 8.1 %slice-start.3 = ((s8[8388608]{0:T(1024)(128)(4,1)}), s8[4194304]{0:T(1024)(128)(4,1)S(1)}, s32[]{:S(2)}) async-start(s8[8388608]{0:T(1024)(128)(4,1)} %bitcast.172), calls=%async_computation.6 | async-start | bytes 8388608
  431.4 8.1 %slice-start.7 = ((s8[8388608]{0:T(1024)(128)(4,1)}), s8[4194304]{0:T(1024)(128)(4,1)S(1)}, s32[]{:S(2)}) async-start(s8[8388608]{0:T(1024)(128)(4,1)} %bitcast.176), calls=%async_computation.10 | async-start | bytes 8388608
  439.5 8.5 %copy-start.11 = (bf16[1024,4,64]{0,2,1:T(8,128)(2,1)S(1)}, bf16[1024,4,64]{0,2,1:T(8,128)(2,1)}, u32[]{:S(2)}) copy-start(bf16[1024,4,64]{0,2,1:T(8,128)(2,1)} %copy-done.10) | copy-start | bytes 1572868
  460.8 5.0 copy-start.23
  478.4 43.7 %copy-start.28 = (f32[2048]{0:T(1024)S(1)}, f32[2048]{0:T(1024)}, u32[]{:S(2)}) copy-start(f32[2048]{0:T(1024)} %param.17) | copy-start | bytes 24580
  478.4 43.7 %copy-start.32 = (f32[128]{0:T(128)S(1)}, f32[128]{0:T(128)}, u32[]{:S(2)}) copy-start(f32[128]{0:T(128)} %copy-done.31) | copy-start | bytes 1540
  478.4 43.7 %copy-start.34 = (f32[128]{0:T(128)S(1)}, f32[128]{0:T(128)}, u32[]{:S(2)}) copy-start(f32[128]{0:T(128)} %copy-done.33) | copy-start | bytes 1540
  478.4 71.0 %copy-start.7 = (f32[128,2048]{1,0:T(8,128)S(1)}, f32[128,2048]{1,0:T(8,128)}, u32[]{:S(2)}) copy-start(f32[128,2048]{1,0:T(8,128)} %get-tuple-element.63) | copy-start | bytes 3145732
  (19 other events, 44.7 us)
Sparse Core Ops, SparseCore 0:
  10.9 112.6 all-gather.1
  280.3 120.6 reduce-scatter.1

commit v2 on v1

v2 whole, which is shorter than its diff:
```python
import functools

import jax
import jax.numpy as jnp
from jax import lax
from jax.experimental import pallas as pl
from jax.experimental.pallas import tpu as pltpu
from jax.sharding import PartitionSpec as P

HEAD_DIM = 64
ROT = 16
DOCS = 4
EPS = 1e-05

ROWS = 128
WIDTH = 2048
TENSOR = 8
HALF = ROWS // 2
QUARTER = ROWS // 4
MESH = pl.DeviceIdType.MESH
BF16 = jnp.bfloat16
F32 = jnp.float32
VMEM_LIMIT = 56 * 2**20


def coordinates():
    tensor = lax.axis_index("tensor")
    return lax.axis_index("dp"), tensor // 2, lax.rem(tensor, 2)


class Around:
    def __init__(self):
        dp, y, z = coordinates()
        up, down, far = lax.rem(y + 1, 4), lax.rem(y + 3, 4), lax.rem(y + 2, 4)
        other = 1 - z
        self.me, self.across = y * 2 + z, y * 2 + other
        self.up, self.down, self.far = up * 2 + z, down * 2 + z, far * 2 + z
        self.up_o, self.down_o, self.far_o = up * 2 + other, down * 2 + other, far * 2 + other
        self.y, self.z = y, z
        self.y_up, self.y_down, self.y_far = up, down, far
        self.to_up, self.to_down, self.to_across = (dp, self.up), (dp, self.down), (dp, self.across)

    def peers(self):
        return [self.to_up, self.to_down, self.to_across]


class Ring:
    def __init__(self):
        dp = lax.axis_index("dp")
        tensor = lax.axis_index("tensor")
        zh, x, core = dp // 8, lax.rem(dp // 2, 4), lax.rem(dp, 2)
        self.zh, self.x, self.core, self.dp, self.tensor = zh, x, core, dp, tensor
        self.xs = [lax.rem(x + step, 4) for step in range(4)]
        self.to_x = [(self.index(zh, self.xs[step], core), tensor) for step in range(4)]
        self.to_zh = (self.index(1 - zh, x, core), tensor)
        self.to_core = (self.index(zh, x, 1 - core), tensor)

    def index(self, zh, x, core):
        return zh * 8 + x * 2 + core

    def peers(self):
        return self.to_x[1:] + [self.to_zh, self.to_core]


def greet(peers):
    barrier = pltpu.get_barrier_semaphore()
    for peer in peers:
        pl.semaphore_signal(barrier, inc=1, device_id=peer, device_id_type=MESH)
    pl.semaphore_wait(barrier, len(peers))


class Mail:
    def __init__(self, sends, receives):
        self.sends, self.receives = sends, receives
        self.out = []

    def send(self, number, source, target, device):
        copy = pltpu.make_async_remote_copy(
            src_ref=source,
            dst_ref=target,
            send_sem=self.sends.at[number],
            recv_sem=self.receives.at[number],
            device_id=device,
            device_id_type=MESH,
        )
        copy.start()
        self.out.append(copy)

    def landed(self, number, target, device):
        pltpu.make_async_remote_copy(
            src_ref=target,
            dst_ref=target,
            send_sem=self.sends.at[number],
            recv_sem=self.receives.at[number],
            device_id=device,
            device_id_type=MESH,
        ).wait_recv()

    def finish(self):
        for copy in self.out:
            copy.wait_send()


def gather_steps(around, mail, own, rows):
    a = around

    def part(slot, first, count):
        return rows.at[slot, pl.ds(first, count)]

    def begin():
        for number, first, device in (
            (0, 0, a.to_up),
            (1, HALF, a.to_down),
            (2, HALF, a.to_across),
            (3, HALF, a.to_up),
            (4, 0, a.to_down),
            (5, 0, a.to_across),
        ):
            mail.send(number, own.at[pl.ds(first, HALF)], part(a.me, first, HALF), device)

    def pass_on(number, slot, first, count, device):
        mail.send(number, part(slot, first, count), part(slot, first, count), device)

    def got(number, slot, first, count):
        mail.landed(number, part(slot, first, count), a.to_up)

    def one():
        got(0, a.down, 0, HALF)
        pass_on(6, a.down, 0, HALF, a.to_up)
        pass_on(7, a.down, 0, HALF, a.to_across)
        got(1, a.up, HALF, HALF)
        pass_on(8, a.up, HALF, HALF, a.to_down)
        got(2, a.across, HALF, HALF)
        pass_on(9, a.across, HALF, HALF, a.to_up)
        pass_on(10, a.across, HALF, HALF, a.to_down)

    def two():
        got(4, a.up, 0, HALF)
        pass_on(11, a.up, 0, HALF, a.to_across)
        got(3, a.down, HALF, HALF)
        got(5, a.across, 0, HALF)

    def three():
        got(6, a.far, 0, HALF)
        pass_on(12, a.far, 0, HALF, a.to_across)
        got(8, a.far, HALF, HALF)

    def four():
        got(9, a.down_o, HALF, HALF)
        pass_on(13, a.down_o, HALF, QUARTER, a.to_up)
        got(10, a.up_o, HALF, HALF)
        pass_on(14, a.up_o, HALF + QUARTER, QUARTER, a.to_down)

    def five():
        got(7, a.down_o, 0, HALF)
        got(11, a.up_o, 0, HALF)

    def six():
        got(13, a.far_o, HALF, QUARTER)
        got(14, a.far_o, HALF + QUARTER, QUARTER)
        got(12, a.far_o, 0, HALF)

    return begin, one, two, three, four, five, six


GATHER_MAILS = 15


def spread_steps(ring, mail, shard, block):
    r = ring

    def share(number, zh, x, device):
        mail.send(number, block(zh, x, r.core), block(zh, x, r.core), device)

    def came(number, zh, x, core):
        mail.landed(number, block(zh, x, core), r.to_core)

    def begin():
        mine = block(r.zh, r.x, r.core)
        mail.send(0, shard, mine, r.to_zh)
        for step in (1, 2, 3):
            mail.send(step, shard, mine, r.to_x[step])
        mail.send(7, shard, mine, r.to_core)

    def one():
        came(0, 1 - r.zh, r.x, r.core)
        for step in (1, 2, 3):
            share(3 + step, 1 - r.zh, r.x, r.to_x[step])
        share(8, 1 - r.zh, r.x, r.to_core)

    def two():
        for step in (1, 2, 3):
            came(step, r.zh, r.xs[4 - step], r.core)
            share(8 + step, r.zh, r.xs[4 - step], r.to_core)

    def three():
        for step in (1, 2, 3):
            came(3 + step, 1 - r.zh, r.xs[4 - step], r.core)
            share(11 + step, 1 - r.zh, r.xs[4 - step], r.to_core)

    def four():
        sibling = 1 - r.core
        came(7, r.zh, r.x, sibling)
        came(8, 1 - r.zh, r.x, sibling)
        for step in (1, 2, 3):
            came(8 + step, r.zh, r.xs[4 - step], sibling)
            came(11 + step, 1 - r.zh, r.xs[4 - step], sibling)

    return begin, one, two, three, four


IDS = 4


def gather_weights_kernel(
    own, ids, shard, rows, id_rows, full, sends, receives, w_sends, w_receives, i_sends, i_receives, local
):
    a, r = Around(), Ring()
    mail, wmail, imail = (
        Mail(sends, receives),
        Mail(w_sends, w_receives),
        Mail(i_sends, i_receives),
    )

    def block(zh, x, core):
        first = pl.multiple_of(r.index(zh, x, core) * ROWS, ROWS)
        return full.at[:, pl.ds(first, ROWS), :]

    keeps = [
        pltpu.make_async_copy(own, rows.at[a.me], local.at[0]),
        pltpu.make_async_copy(ids, id_rows.at[a.z, a.y], local.at[1]),
        pltpu.make_async_copy(shard, block(r.zh, r.x, r.core), local.at[2]),
    ]
    for keep in keeps:
        keep.start()
    greet(a.peers() + r.peers())
    steps = gather_steps(a, mail, own, rows)
    spread = spread_steps(r, wmail, shard, block)
    steps[0]()
    imail.send(0, ids, id_rows.at[a.z, a.y], a.to_up)
    imail.send(1, ids, id_rows.at[a.z, a.y], a.to_down)
    spread[0]()
    imail.landed(0, id_rows.at[a.z, a.y_down], a.to_up)
    imail.send(2, id_rows.at[a.z, a.y_down], id_rows.at[a.z, a.y_down], a.to_up)
    imail.landed(1, id_rows.at[a.z, a.y_up], a.to_up)
    imail.landed(2, id_rows.at[a.z, a.y_far], a.to_up)
    keeps[1].wait()
    imail.send(3, id_rows.at[a.z], id_rows.at[a.z], a.to_across)
    steps[1]()
    spread[1]()
    steps[2]()
    spread[2]()
    steps[3]()
    steps[4]()
    spread[3]()
    steps[5]()
    steps[6]()
    spread[4]()
    imail.landed(3, id_rows.at[1 - a.z], a.to_up)
    mail.finish()
    wmail.finish()
    imail.finish()
    keeps[0].wait()
    keeps[2].wait()


WEIGHT_MAILS = 15


def gather_weights(own, ids, shard, collective):
    parts, rows, columns = shard.shape
    return pl.pallas_call(
        gather_weights_kernel,
        out_shape=(
            jax.ShapeDtypeStruct((TENSOR,) + own.shape, own.dtype),
            jax.ShapeDtypeStruct((2, 4) + ids.shape, ids.dtype),
            jax.ShapeDtypeStruct((parts, rows * 16, columns), shard.dtype),
        ),
        in_specs=[pl.BlockSpec(memory_space=pltpu.VMEM)] * 3,
        out_specs=(pl.BlockSpec(memory_space=pl.ANY),) * 3,
        scratch_shapes=[
            pltpu.SemaphoreType.DMA((GATHER_MAILS,)),
            pltpu.SemaphoreType.DMA((GATHER_MAILS,)),
            pltpu.SemaphoreType.DMA((WEIGHT_MAILS,)),
            pltpu.SemaphoreType.DMA((WEIGHT_MAILS,)),
            pltpu.SemaphoreType.DMA((IDS,)),
            pltpu.SemaphoreType.DMA((IDS,)),
            pltpu.SemaphoreType.DMA((3,)),
        ],
        compiler_params=pltpu.CompilerParams(
            collective_id=collective, has_side_effects=True, vmem_limit_bytes=VMEM_LIMIT
        ),
        name="gather_weights",
    )(own, ids, shard)


def added(*terms):
    total = terms[0].astype(F32)
    for term in terms[1:]:
        total = total + term.astype(F32)
    return total


SCATTER_MAILS = 17
SCATTER_ROWS = (32, 32, 64, 64, 64, 64, 32, 32, 64, 64, 64, 32, 32, 64, 64, 64, 64)
SCATTER_FIRST = tuple(sum(SCATTER_ROWS[:k]) for k in range(SCATTER_MAILS))


def scatter_steps(around, mail, parts, total, land):
    a = around

    def part(slot, first, count):
        return parts.at[slot, pl.ds(first, count)]

    def box(number):
        return land.at[pl.ds(SCATTER_FIRST[number], SCATTER_ROWS[number])]

    def direct(number, slot, first, device):
        mail.send(number, part(slot, first, SCATTER_ROWS[number]), box(number), device)

    def got(number):
        mail.landed(number, box(number), a.to_up)

    def fold(stage, slot, first, others=()):
        count = SCATTER_ROWS[stage]
        terms = [part(slot, first, count)[...], box(stage)[...]]
        terms += [box(other)[...] for other in others]
        box(stage)[...] = added(*terms).astype(BF16)

    def begin():
        direct(0, a.far_o, 96, a.to_up)
        direct(1, a.far_o, 64, a.to_down)
        direct(2, a.far_o, 0, a.to_across)
        direct(3, a.far, 64, a.to_up)
        direct(4, a.up_o, 0, a.to_across)
        direct(5, a.down_o, 0, a.to_across)
        direct(6, a.down_o, 96, a.to_down)
        direct(7, a.up_o, 64, a.to_up)
        direct(8, a.down, 64, a.to_down)
        direct(9, a.across, 0, a.to_across)

    def one():
        got(1)
        fold(1, a.down_o, 64)
        mail.send(11, box(1), box(11), a.to_down)
        got(0)
        fold(0, a.up_o, 96)
        mail.send(12, box(0), box(12), a.to_up)
        got(2)
        fold(2, a.far, 0)
        mail.send(10, box(2), box(10), a.to_down)
        got(3)
        fold(3, a.up, 64)
        mail.send(13, box(3), box(13), a.to_up)

    def two():
        got(4)
        fold(4, a.up, 0)
        mail.send(14, box(4), box(14), a.to_up)
        got(5)
        got(10)
        fold(5, a.down, 0, (10,))
        mail.send(15, box(5), box(15), a.to_down)
        got(6)
        got(7)
        got(11)
        got(12)
        upper = added(part(a.across, 64, 32)[...], box(7)[...], box(11)[...]).astype(BF16)
        lower = added(part(a.across, 96, 32)[...], box(6)[...], box(12)[...]).astype(BF16)
        land.at[pl.ds(SCATTER_FIRST[6], 32)][...] = upper
        land.at[pl.ds(SCATTER_FIRST[7], 32)][...] = lower
        both = land.at[pl.ds(SCATTER_FIRST[6], 64)]
        mail.send(16, both, box(16), a.to_across)

    def three():
        got(9)
        got(14)
        got(15)
        total[pl.ds(0, HALF), :] = added(
            part(a.me, 0, HALF)[...], box(9)[...], box(14)[...], box(15)[...]
        )
        got(8)
        got(13)
        got(16)
        total[pl.ds(HALF, HALF), :] = added(
            part(a.me, HALF, HALF)[...], box(8)[...], box(13)[...], box(16)[...]
        )

    return begin, one, two, three


def blocks_steps(ring, mail, grads, land, own_sum, shard):
    r = ring
    blocks = [(side, step) for step in (1, 2, 3, 0) for side in (0, 1)]

    def place(side, step, core):
        zh = r.zh if side == 0 else 1 - r.zh
        return r.index(zh, r.xs[step], core)

    def begin():
        for number, (side, step) in enumerate(blocks):
            mail.send(number, grads.at[place(side, step, 1 - r.core)], land.at[number], r.to_core)

    def one():
        for number, (side, step) in enumerate(blocks):
            mail.landed(number, land.at[number], r.to_core)
            land[number] = added(grads[place(side, step, r.core)], land[number]).astype(BF16)
            if step:
                mail.send(8 + number, land.at[number], land.at[8 + number], r.to_x[step])

    def two():
        for number in (1, 3, 5):
            mail.landed(8 + number, land.at[8 + number], r.to_core)
        land[7] = added(land[7], land[9], land[11], land[13]).astype(BF16)
        mail.send(14, land.at[7], land.at[14], r.to_zh)
        for number in (0, 2, 4):
            mail.landed(8 + number, land.at[8 + number], r.to_core)
        own_sum[...] = added(land[6], land[8], land[10], land[12])

    def three():
        mail.landed(14, land.at[14], r.to_core)
        shard[...] = added(own_sum[...], land[14])

    return begin, one, two, three


BLOCK_MAILS = 15


SUM_ROWS, SUM_NORMS = 72, 64


def sum_kernel(values, total, boxes, sends, receives):
    a, r = Around(), Ring()
    mail = Mail(sends, receives)
    x_peers = r.to_x[1:]
    z_peers = [
        (r.index(1 - r.zh, r.x, r.core), r.tensor),
        (r.index(r.zh, r.x, 1 - r.core), r.tensor),
        (r.index(1 - r.zh, r.x, 1 - r.core), r.tensor),
    ]
    y_peers = [(r.dp, a.up), (r.dp, a.far), (r.dp, a.down)]
    greet(x_peers + z_peers + y_peers + [a.to_across])

    def stage(base, count, mine, sources, peers):
        view = pl.ds(0, count)
        for number, peer in enumerate(peers):
            mail.send(base + number, boxes.at[base + mine, view], boxes.at[base + mine, view], peer)
        for number, source in enumerate(sources):
            mail.landed(base + number, boxes.at[base + source, view], peers[0])
        result = boxes[base, view]
        for k in range(1, len(peers) + 1):
            result = result + boxes[base + k, view]
        return result

    boxes[r.x] = values[...]
    first = stage(0, SUM_ROWS, r.x, [r.xs[3], r.xs[2], r.xs[1]], x_peers)
    place = r.zh * 2 + r.core
    boxes[4 + place] = first
    second = stage(
        4,
        SUM_ROWS,
        place,
        [(1 - r.zh) * 2 + r.core, r.zh * 2 + 1 - r.core, (1 - r.zh) * 2 + 1 - r.core],
        z_peers,
    )
    total[...] = second
    boxes[8 + a.y, pl.ds(0, SUM_NORMS)] = second[:SUM_NORMS]
    third = stage(8, SUM_NORMS, a.y, [a.y_down, a.y_far, a.y_up], y_peers)
    boxes[12 + a.z, pl.ds(0, SUM_NORMS)] = third
    total[pl.ds(0, SUM_NORMS), :] = stage(12, SUM_NORMS, a.z, [1 - a.z], [a.to_across])
    mail.finish()


def sum_all(values, collective):
    return pl.pallas_call(
        sum_kernel,
        out_shape=jax.ShapeDtypeStruct(values.shape, F32),
        in_specs=[pl.BlockSpec(memory_space=pltpu.VMEM)],
        out_specs=pl.BlockSpec(memory_space=pltpu.VMEM),
        scratch_shapes=[
            pltpu.VMEM((14, SUM_ROWS, 128), F32),
            pltpu.SemaphoreType.DMA((13,)),
            pltpu.SemaphoreType.DMA((13,)),
        ],
        compiler_params=pltpu.CompilerParams(
            collective_id=collective, has_side_effects=True, vmem_limit_bytes=VMEM_LIMIT
        ),
        name="sum_all",
    )(values)


HEADS_DEV = 4
LOCAL = HEADS_DEV * HEAD_DIM
GROUP = ROWS * TENSOR
QBLOCK = 256
UNITS = 704
LANES = 128
SCALE = HEAD_DIM ** (-0.5)


def dot(left, right):
    return lax.dot_general(left, right, (((1,), (0,)), ((), ())), preferred_element_type=F32)


def dot_t(left, right):
    return lax.dot_general(left, right, (((1,), (1,)), ((), ())), preferred_element_type=F32)


def turned(values, tables, row, sign):
    rows = pl.ds(row, values.shape[0])
    cosine, minus, plus = tables[0, rows], tables[1, rows], tables[2, rows]
    halves = []
    for first in range(0, LOCAL, LANES):
        part = values[:, first : first + LANES]
        left = pltpu.roll(part, LANES - ROT // 2, 1)
        right = pltpu.roll(part, ROT // 2, 1)
        halves.append(part * cosine + sign * (left * minus + right * plus))
    return jnp.concatenate(halves, axis=1)


def head_lanes(head, rows):
    return lax.broadcasted_iota(jnp.int32, (rows, LOCAL), 1) // HEAD_DIM == head


def only(mask, values):
    return jnp.where(mask, values, jnp.zeros_like(values))


def attention_kernel(
    rows,
    weights,
    bias,
    tables,
    start,
    own,
    shard,
    total,
    gathered,
    feed,
    acts,
    attended,
    logs,
    parts,
    land,
    sends,
    receives,
    g_sends,
    g_receives,
    w_sends,
    w_receives,
    local,
):
    a, r = Around(), Ring()
    mail, gmail, wmail = Mail(sends, receives), Mail(g_sends, g_receives), Mail(w_sends, w_receives)

    def block(zh, x, core):
        return feed.at[r.index(zh, x, core)]

    keeps = [
        pltpu.make_async_copy(own, gathered.at[a.me], local.at[0]),
        pltpu.make_async_copy(shard, block(r.zh, r.x, r.core), local.at[1]),
    ]
    for keep in keeps:
        keep.start()
    greet(a.peers() + r.peers())
    gather = gather_steps(a, gmail, own, gathered)
    spread = spread_steps(r, wmail, shard, block)
    scatter = scatter_steps(a, mail, parts, total, land)
    gather[0]()
    spread[0]()

    def project(index, carry):
        first = pl.multiple_of(index * QBLOCK, QBLOCK)
        chunk = rows[pl.ds(first, QBLOCK), :]
        for c in range(3):
            pre = dot(chunk, weights[c]) + bias[pl.ds(c, 1), :]
            if c < 2:
                pre = turned(pre, tables, first, 1.0)
            acts[c, pl.ds(first, QBLOCK), :] = pre.astype(BF16)
        return carry

    lax.fori_loop(0, GROUP // QBLOCK, project, 0)
    spread[1]()

    def attend(first):
        count = first + QBLOCK
        query = acts[0, pl.ds(first, QBLOCK), :] * BF16(SCALE)
        row = first + lax.broadcasted_iota(jnp.int32, (QBLOCK, count), 0)
        column = lax.broadcasted_iota(jnp.int32, (QBLOCK, count), 1)
        allow = (column <= row) & (column >= start[pl.ds(first, QBLOCK), :])
        lane = lax.broadcasted_iota(jnp.int32, (QBLOCK, LANES), 1)

        def one_head(head, carry):
            out, log = carry
            masked = only(head_lanes(head, QBLOCK), query)
            scores = dot_t(masked, acts[1, pl.ds(0, count), :])
            scores = jnp.where(allow, scores, -1e30)
            highest = jnp.max(scores, axis=1, keepdims=True)
            expon = jnp.exp(scores - highest)
            sums = jnp.sum(expon, axis=1, keepdims=True)
            values = only(head_lanes(head, count), acts[2, pl.ds(0, count), :])
            out = out + dot(expon.astype(BF16), values) / sums
            log = jnp.where(lane == head, highest + jnp.log(sums), log)
            return out, log

        out, log = lax.fori_loop(
            0,
            HEADS_DEV,
            one_head,
            (jnp.zeros((QBLOCK, LOCAL), F32), jnp.zeros((QBLOCK, LANES), F32)),
        )
        attended[pl.ds(first, QBLOCK), :] = out.astype(BF16)
        logs[:, pl.ds(first, QBLOCK)] = log.T[:8]
        branch = dot_t(out.astype(BF16), weights[3]).astype(BF16)
        slot = first // ROWS
        parts[slot] = branch[:ROWS]
        parts[slot + 1] = branch[ROWS:]

    attend(0)
    attend(QBLOCK)
    gather[1]()
    attend(2 * QBLOCK)
    attend(3 * QBLOCK)
    scatter[0]()
    gather[2]()
    spread[2]()
    gather[3]()
    scatter[1]()
    gather[4]()
    scatter[2]()
    spread[3]()
    gather[5]()
    gather[6]()
    scatter[3]()
    spread[4]()
    mail.finish()
    gmail.finish()
    wmail.finish()
    for keep in keeps:
        keep.wait()


def vmem(count):
    return [pl.BlockSpec(memory_space=pltpu.VMEM)] * count


def anywhere(count):
    return [pl.BlockSpec(memory_space=pl.ANY)] * count


def pairs(count):
    return [pltpu.SemaphoreType.DMA((count,)), pltpu.SemaphoreType.DMA((count,))]


def params(collective):
    return pltpu.CompilerParams(
        collective_id=collective, has_side_effects=True, vmem_limit_bytes=VMEM_LIMIT
    )


def attention_forward(rows, weights, bias, tables, start, own, shard, collective):
    return pl.pallas_call(
        attention_kernel,
        out_shape=(
            jax.ShapeDtypeStruct((ROWS, WIDTH), F32),
            jax.ShapeDtypeStruct((TENSOR, ROWS, WIDTH), BF16),
            jax.ShapeDtypeStruct((16,) + shard.shape, BF16),
            jax.ShapeDtypeStruct((3, GROUP, LOCAL), BF16),
            jax.ShapeDtypeStruct((GROUP, LOCAL), BF16),
            jax.ShapeDtypeStruct((8, GROUP), F32),
        ),
        in_specs=vmem(7),
        out_specs=tuple(vmem(1) + anywhere(2) + vmem(3)),
        scratch_shapes=[
            pltpu.VMEM((TENSOR, ROWS, WIDTH), BF16),
            pltpu.VMEM((sum(SCATTER_ROWS), WIDTH), BF16),
            *pairs(SCATTER_MAILS),
            *pairs(GATHER_MAILS),
            *pairs(WEIGHT_MAILS),
            pltpu.SemaphoreType.DMA((2,)),
        ],
        compiler_params=params(collective),
        name="attention_forward",
    )(rows, weights, bias, tables, start, own, shard)


def feed_kernel(
    own,
    gathered,
    feed,
    total,
    outs,
    grads,
    rows,
    cots,
    weights,
    parts,
    acts,
    land,
    sends,
    receives,
    g_sends,
    g_receives,
    w_local,
    local,
):
    a = Around()
    mail, gmail = Mail(sends, receives), Mail(g_sends, g_receives)
    loads = [
        pltpu.make_async_copy(feed.at[n], weights.at[:, pl.ds(n * ROWS, ROWS)], w_local.at[n])
        for n in range(16)
    ]
    keeps = [
        pltpu.make_async_copy(own, rows.at[a.me], local.at[0]),
        pltpu.make_async_copy(gathered, cots, local.at[1]),
    ]
    for copy in keeps[:1] + loads + keeps[1:]:
        copy.start()
    greet(a.peers())
    gather = gather_steps(a, gmail, own, rows)
    scatter = scatter_steps(a, mail, parts, total, land)
    gather[0]()
    for copy in loads + keeps:
        copy.wait()

    def pair(y):
        slots = pl.ds(2 * y, 2)
        x = rows[slots].reshape(2 * ROWS, WIDTH)
        gate = dot_t(x, weights[pl.ds(0, UNITS), :])
        upward = dot_t(x, weights[pl.ds(UNITS, UNITS), :])
        grad_hidden = dot_t(
            cots[slots].reshape(2 * ROWS, WIDTH), weights[pl.ds(2 * UNITS, UNITS), :]
        )
        sigma = jax.nn.sigmoid(gate)
        silu = gate * sigma
        hidden = (silu * upward).astype(BF16)
        grad_gate = (grad_hidden * upward * (sigma + silu * (1.0 - sigma))).astype(BF16)
        grad_up = (grad_hidden * silu).astype(BF16)
        out = dot(hidden, weights[pl.ds(2 * UNITS, UNITS), :]).astype(BF16)
        outs[slots] = out.reshape(2, ROWS, WIDTH)
        back = dot(grad_gate, weights[pl.ds(0, UNITS), :])
        back = back + dot(grad_up, weights[pl.ds(UNITS, UNITS), :])
        parts[slots] = back.astype(BF16).reshape(2, ROWS, WIDTH)
        lanes = pl.ds(pl.multiple_of(y * 2 * ROWS, 2 * ROWS), 2 * ROWS)
        acts[pl.ds(0, UNITS), lanes] = grad_gate.T
        acts[pl.ds(UNITS, UNITS), lanes] = grad_up.T
        acts[pl.ds(2 * UNITS, UNITS), lanes] = hidden.T

    gather[1]()
    gather[2]()
    pair(a.y)
    gather[3]()
    gather[4]()
    gather[5]()
    pair(a.y_down)
    gather[6]()
    pair(a.y_far)
    pair(a.y_up)
    scatter[0]()

    def weight_grad(index, carry):
        columns = pl.ds(pl.multiple_of(index * 2 * ROWS, 2 * ROWS), 2 * ROWS)
        both = dot(acts[pl.ds(0, 2 * UNITS), :], rows[:, :, columns].reshape(GROUP, 2 * ROWS))
        down = dot(acts[pl.ds(2 * UNITS, UNITS), :], cots[:, :, columns].reshape(GROUP, 2 * ROWS))
        for side in range(2):
            lanes = slice(side * ROWS, (side + 1) * ROWS)
            grads[2 * index + side, pl.ds(0, 2 * UNITS), :] = both[:, lanes].astype(BF16)
            grads[2 * index + side, pl.ds(2 * UNITS, UNITS), :] = down[:, lanes].astype(BF16)
        return carry

    lax.fori_loop(0, 3, weight_grad, 0)
    scatter[1]()
    lax.fori_loop(3, 6, weight_grad, 0)
    scatter[2]()
    lax.fori_loop(6, 8, weight_grad, 0)
    scatter[3]()
    mail.finish()
    gmail.finish()


def feed_forward(own, gathered, feed, collective):
    group = (TENSOR, ROWS, WIDTH)
    return pl.pallas_call(
        feed_kernel,
        out_shape=(
            jax.ShapeDtypeStruct((ROWS, WIDTH), F32),
            jax.ShapeDtypeStruct(group, BF16),
            jax.ShapeDtypeStruct((16, 3 * UNITS, ROWS), BF16),
        ),
        in_specs=vmem(1) + anywhere(2),
        out_specs=tuple(vmem(3)),
        scratch_shapes=[
            pltpu.VMEM(group, BF16),
            pltpu.VMEM(group, BF16),
            pltpu.VMEM((3 * UNITS, WIDTH), BF16),
            pltpu.VMEM(group, BF16),
            pltpu.VMEM((3 * UNITS, GROUP), BF16),
            pltpu.VMEM((sum(SCATTER_ROWS), WIDTH), BF16),
            *pairs(SCATTER_MAILS),
            *pairs(GATHER_MAILS),
            pltpu.SemaphoreType.DMA((16,)),
            pltpu.SemaphoreType.DMA((2,)),
        ],
        compiler_params=params(collective),
        name="feed_forward",
    )(own, gathered, feed)


def attention_back_kernel(
    own,
    weights,
    tables,
    start,
    acts,
    attended,
    logs,
    first_rows,
    outs,
    total,
    out_total,
    shard,
    bias_sum,
    rows,
    before,
    grad_out,
    grads_qkv,
    keys_turned,
    turns,
    parts,
    out_parts,
    grads,
    land,
    out_land,
    w_land,
    w_sum,
    sends,
    receives,
    g_sends,
    g_receives,
    o_sends,
    o_receives,
    w_sends,
    w_receives,
    local,
):
    a, r = Around(), Ring()
    mail, gmail, omail, wmail = (
        Mail(sends, receives),
        Mail(g_sends, g_receives),
        Mail(o_sends, o_receives),
        Mail(w_sends, w_receives),
    )
    keeps = [
        pltpu.make_async_copy(own, rows.at[a.me], local.at[0]),
        pltpu.make_async_copy(first_rows, before, local.at[1]),
        pltpu.make_async_copy(outs, out_parts, local.at[2]),
    ]
    for keep in keeps:
        keep.start()
    greet(a.peers() + r.peers())
    gather = gather_steps(a, gmail, own, rows)
    out_scatter = scatter_steps(a, omail, out_parts, out_total, out_land)
    scatter = scatter_steps(a, mail, parts, total, land)
    blocks = blocks_steps(r, wmail, grads, w_land, w_sum, shard)
    gather[0]()
    keys_turned[...] = acts[1].T
    turns[pl.ds(3 * LOCAL, LOCAL), :] = attended[...].T
    for keep in keeps:
        keep.wait()
    gather[1]()
    gather[2]()
    gather[3]()
    gather[4]()
    gather[5]()
    out_scatter[0]()
    gather[6]()

    def back_project(index, carry):
        chunk = rows[pl.ds(2 * index, 2)].reshape(QBLOCK, WIDTH)
        first = pl.multiple_of(index * QBLOCK, QBLOCK)
        grad_out[pl.ds(first, QBLOCK), :] = dot(chunk, weights[3]).astype(BF16)
        return carry

    lax.fori_loop(0, GROUP // QBLOCK, back_project, 0)

    def attend(first):
        count = first + QBLOCK
        span = pl.ds(first, QBLOCK)
        query = acts[0, span, :] * BF16(SCALE)
        given = grad_out[span, :]
        row = lax.broadcasted_iota(jnp.int32, (count, QBLOCK), 0)
        column = first + lax.broadcasted_iota(jnp.int32, (count, QBLOCK), 1)
        allow = (row <= column) & (row >= start[:, span])
        overlap = given.astype(F32) * attended[span, :].astype(F32)
        lane = lax.broadcasted_iota(jnp.int32, (QBLOCK, LANES), 1)
        inner = jnp.zeros((QBLOCK, LANES), F32)
        for head in range(HEADS_DEV):
            summed = jnp.sum(only(head_lanes(head, QBLOCK), overlap), axis=1, keepdims=True)
            inner = jnp.where(lane == head, summed, inner)
        inner = inner.T[:8]
        head_row = lax.broadcasted_iota(jnp.int32, (8, QBLOCK), 0)
        head_rows = lax.broadcasted_iota(jnp.int32, (LOCAL, count), 0) // HEAD_DIM

        def one_head(head, turned_query):
            mask = head_lanes(head, QBLOCK)
            masked, masked_given = only(mask, query), only(mask, given)
            log = jnp.sum(only(head_row == head, logs[:, span]), axis=0, keepdims=True)
            mean = jnp.sum(only(head_row == head, inner), axis=0, keepdims=True)
            scores = dot_t(acts[1, pl.ds(0, count), :], masked)
            probs = only(allow, jnp.exp(scores - log))
            grad_probs = dot_t(acts[2, pl.ds(0, count), :], masked_given)
            grad_scores = (probs * (grad_probs - mean)).astype(BF16)
            grads_qkv[2, pl.ds(0, count), :] += dot(probs.astype(BF16), masked_given)
            grads_qkv[1, pl.ds(0, count), :] += dot(grad_scores, masked)
            keys = only(head_rows == head, keys_turned[:, pl.ds(0, count)])
            return turned_query + dot(keys, grad_scores)

        turned_query = lax.fori_loop(0, HEADS_DEV, one_head, jnp.zeros((LOCAL, QBLOCK), F32))
        grads_qkv[0, span, :] = turned_query.T * SCALE

    grads_qkv[1] = jnp.zeros((GROUP, LOCAL), F32)
    grads_qkv[2] = jnp.zeros((GROUP, LOCAL), F32)
    attend(0)
    attend(QBLOCK)
    out_scatter[1]()
    attend(2 * QBLOCK)
    out_scatter[2]()
    attend(3 * QBLOCK)

    def input_grad(index, sums):
        first = pl.multiple_of(index * QBLOCK, QBLOCK)
        span = pl.ds(first, QBLOCK)
        back = jnp.zeros((QBLOCK, WIDTH), F32)
        added_sums = []
        for c in range(3):
            pre = grads_qkv[c, span, :]
            if c < 2:
                pre = turned(pre, tables, first, -1.0)
            pre = pre.astype(BF16)
            added_sums.append(jnp.sum(pre.astype(F32), axis=0, keepdims=True))
            back = back + dot_t(pre, weights[c])
            turns[pl.ds(c * LOCAL, LOCAL), span] = pre.T
        parts[pl.ds(2 * index, 2)] = back.astype(BF16).reshape(2, ROWS, WIDTH)
        return sums + jnp.concatenate(added_sums, axis=0)

    bias_sum[...] = lax.fori_loop(
        0, GROUP // QBLOCK, input_grad, jnp.zeros((3, LOCAL), F32)
    )
    scatter[0]()

    def weight_grad(index, carry):
        columns = pl.ds(pl.multiple_of(index * 2 * ROWS, 2 * ROWS), 2 * ROWS)
        three = dot(turns[pl.ds(0, 3 * LOCAL), :], before[:, columns])
        last = dot(turns[pl.ds(3 * LOCAL, LOCAL), :], rows[:, :, columns].reshape(GROUP, 2 * ROWS))
        for side in range(2):
            lanes = slice(side * ROWS, (side + 1) * ROWS)
            grads[2 * index + side, pl.ds(0, 3 * LOCAL), :] = three[:, lanes].astype(BF16)
            grads[2 * index + side, pl.ds(3 * LOCAL, LOCAL), :] = last[:, lanes].astype(BF16)
        return carry

    lax.fori_loop(0, 8, weight_grad, 0)
    blocks[0]()
    out_scatter[3]()
    scatter[1]()
    blocks[1]()
    scatter[2]()
    blocks[2]()
    scatter[3]()
    blocks[3]()
    mail.finish()
    gmail.finish()
    omail.finish()
    wmail.finish()


def attention_backward(own, weights, tables, start, acts, attended, logs, first_rows, outs, collective):
    group = (TENSOR, ROWS, WIDTH)
    block = (4 * LOCAL, ROWS)
    landing = (sum(SCATTER_ROWS), WIDTH)
    return pl.pallas_call(
        attention_back_kernel,
        out_shape=(
            jax.ShapeDtypeStruct((ROWS, WIDTH), F32),
            jax.ShapeDtypeStruct((ROWS, WIDTH), F32),
            jax.ShapeDtypeStruct(block, F32),
            jax.ShapeDtypeStruct((3, LOCAL), F32),
        ),
        in_specs=vmem(7) + anywhere(2),
        out_specs=tuple(vmem(4)),
        scratch_shapes=[
            pltpu.VMEM(group, BF16),
            pltpu.VMEM((GROUP, WIDTH), BF16),
            pltpu.VMEM((GROUP, LOCAL), BF16),
            pltpu.VMEM((3, GROUP, LOCAL), F32),
            pltpu.VMEM((LOCAL, GROUP), BF16),
            pltpu.VMEM((4 * LOCAL, GROUP), BF16),
            pltpu.VMEM(group, BF16),
            pltpu.VMEM(group, BF16),
            pltpu.VMEM((16,) + block, BF16),
            pltpu.VMEM(landing, BF16),
            pltpu.VMEM(landing, BF16),
            pltpu.VMEM((BLOCK_MAILS,) + block, BF16),
            pltpu.VMEM(block, F32),
            *pairs(SCATTER_MAILS),
            *pairs(GATHER_MAILS),
            *pairs(SCATTER_MAILS),
            *pairs(BLOCK_MAILS),
            pltpu.SemaphoreType.DMA((3,)),
        ],
        compiler_params=params(collective),
        name="attention_backward",
    )(own, weights, tables, start, acts, attended, logs, first_rows, outs)


def norm_parts(values, gain, shift):
    centred = values - jnp.mean(values, axis=-1, keepdims=True)
    variance = jnp.mean(centred * centred, axis=-1, keepdims=True)
    rinv = lax.rsqrt(variance + EPS)
    normal = centred * rinv
    return (normal * gain + shift, normal, rinv)


def norm_back(incoming, normal, rinv, gain):
    scaled = incoming * gain
    inner = (
        scaled
        - jnp.mean(scaled, axis=-1, keepdims=True)
        - normal * jnp.mean(scaled * normal, axis=-1, keepdims=True)
    )
    return (rinv * inner, jnp.sum(incoming * normal, axis=0), jnp.sum(incoming, axis=0))


def places(group_ids):
    group = group_ids.shape[0]
    index = jnp.arange(group, dtype=jnp.int32)
    numbers = jnp.arange(DOCS, dtype=jnp.int32)
    before = (group_ids[None, :] >= 0) & (group_ids[None, :] < numbers[:, None])
    starts = jnp.sum(before.astype(jnp.int32), axis=1)
    offset = jnp.sum(jnp.where(group_ids[:, None] == numbers[None, :], starts[None, :], 0), axis=1)
    position = (index - offset).astype(F32)
    freq = jnp.power(10000.0, -2.0 * jnp.arange(ROT // 2, dtype=F32) / ROT)
    angle = position[:, None] * freq[None, :]
    cosine, sine = jnp.cos(angle), jnp.sin(angle)
    rest = HEAD_DIM - ROT
    none = jnp.zeros_like(sine)
    tables = jnp.stack(
        [
            jnp.concatenate([cosine, cosine, jnp.ones((group, rest), F32)], axis=1),
            jnp.concatenate([-sine, none, jnp.zeros((group, rest), F32)], axis=1),
            jnp.concatenate([none, sine, jnp.zeros((group, rest), F32)], axis=1),
        ]
    )
    return jnp.where(group_ids >= 0, offset, index), jnp.tile(tables, (1, 1, 2))


def body(
    tokens,
    doc_ids,
    qkv_weight,
    qkv_bias,
    out_weight,
    norm1_gain,
    norm1_shift,
    norm2_gain,
    norm2_shift,
    gate_up_weight,
    down_weight,
    cotangent,
):
    inputs = tokens.astype(F32)
    normed1, normal1, rinv1 = norm_parts(inputs, norm1_gain, norm1_shift)
    shard = jnp.concatenate([qkv_weight, out_weight.T[None]])
    rows1, id_rows, projections = gather_weights(
        normed1.astype(BF16), jnp.broadcast_to(doc_ids[None], (8, ROWS)), shard, 0
    )
    rows1 = rows1.reshape(GROUP, WIDTH)
    group_ids = jnp.swapaxes(id_rows[:, :, 0], 0, 1).reshape(GROUP)
    start, tables = places(group_ids)
    feed_shard = jnp.concatenate(
        [jnp.swapaxes(gate_up_weight, 1, 2).reshape(2 * UNITS, ROWS), down_weight]
    )
    branch, grad_rows, feed, acts, attended, logs = attention_forward(
        rows1, projections, qkv_bias, tables, start[:, None], cotangent, feed_shard, 1
    )
    mixed = inputs + branch
    normed2, normal2, rinv2 = norm_parts(mixed, norm2_gain, norm2_shift)
    grad_normed2, feed_out, feed_grad = feed_forward(normed2.astype(BF16), grad_rows, feed, 2)
    feed_grad = lax.psum_scatter(feed_grad, "dp", scatter_dimension=0, tiled=False).astype(F32)
    gate_up_shard = jnp.swapaxes(feed_grad[: 2 * UNITS].reshape(2, UNITS, ROWS), 1, 2)
    down_shard = feed_grad[2 * UNITS :]
    back2, gain2_grad, shift2_grad = norm_back(grad_normed2, normal2, rinv2, norm2_gain)
    grad_mixed = cotangent.astype(F32) + back2
    grad_normed1, feed_sum, weight_shard, bias_part = attention_backward(
        grad_mixed.astype(BF16),
        projections,
        tables,
        start[None, :],
        acts,
        attended,
        logs,
        rows1,
        feed_out,
        3,
    )
    layer_out = (mixed + feed_sum).astype(BF16)
    qkv_shard = jnp.swapaxes(weight_shard[: 3 * LOCAL].reshape(3, LOCAL, ROWS), 1, 2)
    out_shard = weight_shard[3 * LOCAL :]
    back1, gain1_grad, shift1_grad = norm_back(grad_normed1, normal1, rinv1, norm1_gain)
    token_grad = (grad_mixed + back1).astype(BF16)
    norms = jnp.concatenate([gain1_grad, shift1_grad, gain2_grad, shift2_grad, bias_part.reshape(-1)])
    sums = sum_all(jnp.pad(norms.reshape(-1, 128), ((0, 2), (0, 0))), 4)
    gain1_sum, shift1_sum, gain2_sum, shift2_sum = sums[:64].reshape(4, WIDTH)
    bias_grad = sums[64:70].reshape(3, LOCAL)
    return (
        layer_out,
        token_grad,
        qkv_shard,
        bias_grad,
        out_shard,
        gain1_sum,
        shift1_sum,
        gain2_sum,
        shift2_sum,
        gate_up_shard,
        down_shard,
    )


def solution(mesh):
    in_specs = (
        P(("dp", "tensor"), None),
        P(("dp", "tensor")),
        P(None, "dp", "tensor"),
        P(None, "tensor"),
        P("tensor", "dp"),
        P(),
        P(),
        P(),
        P(),
        P(None, "dp", "tensor"),
        P("tensor", "dp"),
        P(("dp", "tensor"), None),
    )
    out_specs = (
        P(("dp", "tensor"), None),
        P(("dp", "tensor"), None),
        P(None, "dp", "tensor"),
        P(None, "tensor"),
        P("tensor", "dp"),
        P(),
        P(),
        P(),
        P(),
        P(None, "dp", "tensor"),
        P("tensor", "dp"),
    )
    return jax.shard_map(body, mesh=mesh, in_specs=in_specs, out_specs=out_specs, check_vma=False)
```

time: 573 us -> 409 us (0.71)
  matrix products: 112 us -> 0 us
  local copies, waits for them, and re-layouts: 43.7 us -> 15.5 us
  other arithmetic: 44.8 us -> 18.3 us
  Pallas kernels: 347 us -> 353 us
    dot_general x24 -> x0, matrix products: 112 us -> none  [product(): return jnp.einsum(spec, left, right, preferred_element_type=F32)]
    pallas_call x7 -> x3, Pallas kernels: 262 us -> 291 us  [the longest x1 128 us: attention_backward(): pl.pallas_call(attention_back_kernel, out_shape=(jax.ShapeDtypeStruct((RO...]
    pallas_call x1, Pallas kernels: 66.1 us -> 42.4 us  [gather_weights(): pl.pallas_call(gather_weights_kernel, out_shape=(jax.ShapeDtypeStruct((TE...]
    unnamed x105 -> x31, local copies, waits for them, and re-layouts: 18.1 us -> 2.18 us
    concatenate x5 -> x1, other arithmetic: 9.71 us -> 0.83 us  [body(): jnp.concatenate([jnp.swapaxes(gate_up_weight, 1, 2).reshape(2 * UNITS, RO...]
    convert_element_type x6 -> x5, other arithmetic: 14.7 us -> 6.03 us  [the longest x1 2.12 us: body(): layer_out = (mixed + feed_sum).astype(BF16)]
    reshape x2, local copies, waits for them, and re-layouts: 9.64 us -> 1.52 us  [the longest x1 0.91 us: body(): weight_shard[:3 * LOCAL].reshape(3, LOCAL, ROWS)]
  transfers between devices with their start and end apart: 2 -> 1, of which waited for: 0 -> 0; matrix products, arithmetic and copies ran while one was open for 24% -> 4% of each run, Pallas kernels for 62% -> 37%
where the time goes in v2:
time: 409 us; the launch traced here: 401 us
  Pallas kernels  353 us (86%)
  other arithmetic  18.3 us (4%)
  local copies, waits for them, and re-layouts  15.5 us (4%)
  between operations  14.8 us (4%)
    pallas_call x1, Pallas kernels, attention_backward(): pl.pallas_call(attention_back_kernel, out_shape=(jax.ShapeDtypeStruct((RO...  128 us
    pallas_call x1, Pallas kernels, attention_forward(): pl.pallas_call(attention_kernel, out_shape=(jax.ShapeDtypeStruct((ROWS, W...  88.2 us
    pallas_call x1, Pallas kernels, feed_forward(): pl.pallas_call(feed_kernel, out_shape=(jax.ShapeDtypeStruct((ROWS, WIDTH)...  74.8 us
    pallas_call x1, Pallas kernels, gather_weights(): pl.pallas_call(gather_weights_kernel, out_shape=(jax.ShapeDtypeStruct((TE...  42.4 us
    pallas_call x1, Pallas kernels, sum_all(): pl.pallas_call(sum_kernel, out_shape=jax.ShapeDtypeStruct(values.shape, F...  19.8 us
  transfers between devices with their start and end apart: 1, of which 0 were waited for; matrix products, arithmetic and copies ran while one was open for 4% of the time, Pallas kernels for 37%

profile of v2, /device:TPU:0, one launch (start us, length us, event | category | flops | bytes accessed | tf_op | source)
XLA Modules:
  0.0 401.3 jit_solution(11419506871637284025)
XLA Ops:
  7.3 1.2 convert_reduce_fusion
  8.5 1.3 fusion.14
  9.9 0.9 copy.36
  10.8 1.7 pad_maximum_fusion.2.shard
  12.5 1.2 fusion.7.own
  14.3 42.4 %gather_weights.1 = (bf16[8,128,2048]{2,1,0:T(8,128)(2,1)}, s32[2,4,8,128]{3,2,1,0:T(8,128)}, bf16[4,2048,256]{2,1,0:T(8,128)(2,1)}) custom-call(bf16[128,2048]{1,0:T(8,128)(2,1)} %fusion.7.own, s32[8,128]{1,0:T(8,128)} %broadcast_in_dim.16.ids, bf16[4,128,256]{2,1,0:T(8,128)(2,1)} %pad_maximum_fusion.2.shard), custom_call_target="tpu_custom_call" | custom-call | tf_op jit(solution)/shard_map/gather_weights/pallas_call | solution.py:272
  56.7 0.8 slice.31
  59.2 1.6 copy.41.tables
  60.8 0.8 pad_maximum_fusion.1.shard
  61.7 0.9 iota_select_fusion.start
  62.5 88.2 %attention_forward.1 = (f32[128,2048]{1,0:T(8,128)}, bf16[8,128,2048]{2,1,0:T(8,128)(2,1)}, bf16[16,2112,128]{2,1,0:T(8,128)(2,1)}, bf16[3,1024,256]{2,1,0:T(8,1...) custom-call(bf16[1024,2048]{1,0:T(8,128)(2,1)} %bitcast.36, bf16[4,2048,256]{2,1,0:T(8,128)(2,1)} %get-tuple-element.28.weights, ...), custom_call_target="tpu_custom_call" | custom-call | tf_op jit(solution)/shard_map/attention_forward/pallas_call | solution.py:663
  150.8 1.4 fusion.18
  152.5 1.0 add_convert_fusion.1.own
  153.6 74.8 %feed_forward.1 = (f32[128,2048]{1,0:T(8,128)}, bf16[8,128,2048]{2,1,0:T(8,128)(2,1)}, bf16[16,2112,128]{2,1,0:T(8,128)(2,1)}) custom-call(bf16[128,2048]{1,0:T(8,128)(2,1)} %add_convert_fusion.1.own, bf16[8,128,2048]{2,1,0:T(8,128)(2,1)} %get-tuple-element.31.gathered, bf16[16,2112,128]{2,1,0:T(8,128)(2,1)} %get-tuple-element.32.feed), custom_call_target="tpu_custom_call" | custom-call | tf_op jit(solution)/shard_map/feed_forward/pallas_call | solution.py:784
  228.4 1.2 copy-done.1
  230.0 0.6 iota_select_fusion.1.start
  230.6 1.7 fusion.17
  232.3 127.5 %attention_backward.1 = (f32[128,2048]{1,0:T(8,128)}, f32[128,2048]{1,0:T(8,128)}, f32[1024,128]{1,0:T(8,128)}, f32[3,256]{1,0:T(4,128)}) custom-call(bf16[128,2048]{1,0:T(8,128)(2,1)} %get-tuple-element.51.own, bf16[4,2048,256]{2,1,0:T(8,128)(2,1)} %get-tuple-element.28.weights, f32[3,1024,128]{2,1,0:T(8,128)} %copy.41.tables, ...), custom_call_target="tpu_custom_call" | custom-call | tf_op jit(solution)/shard_map/attention_backward/pallas_call | solution.py:981
  359.8 1.7 slice.34
  361.5 1.0 slice.32
  362.5 0.7 reshape.175
  363.7 0.6 pad.4.values
  364.4 19.8 %sum_all.1 = f32[72,128]{1,0:T(8,128)} custom-call(f32[72,128]{1,0:T(8,128)} %pad.4.values), custom_call_target="tpu_custom_call" | custom-call | tf_op jit(solution)/shard_map/sum_all/pallas_call | solution.py:476
  384.1 0.7 slice.33
  384.8 0.6 reshape.177
  385.4 0.9 copy.44
  386.3 1.4 slice_bitcast_fusion.1
  387.8 2.1 add_convert_fusion
  389.9 1.3 fusion.12
  391.2 1.2 convert_element_type.46
  392.4 0.8 slice_bitcast_fusion
  393.1 0.9 slice.38
  (65 shorter events, 3.6 us)
Async XLA Ops:
  7.2 5.3 %copy-start = (bf16[128,2048]{1,0:T(8,128)(2,1)S(1)}, bf16[128,2048]{1,0:T(8,128)(2,1)}, u32[]{:S(2)}) copy-start(bf16[128,2048]{1,0:T(8,128)(2,1)} %param.12) | copy-start | bytes 1572868
  7.2 5.3 %copy-start.9 = (f32[2048]{0:T(1024)S(1)}, f32[2048]{0:T(1024)}, u32[]{:S(2)}) copy-start(f32[2048]{0:T(1024)} %param.17) | copy-start | bytes 24580
  7.2 5.3 %copy-start.10 = (f32[2048]{0:T(1024)S(1)}, f32[2048]{0:T(1024)}, u32[]{:S(2)}) copy-start(f32[2048]{0:T(1024)} %param.18) | copy-start | bytes 24580
  7.2 6.5 %copy-start.12 = (s32[128]{0:T(128)S(1)}, s32[128]{0:T(128)}, u32[]{:S(2)}) copy-start(s32[128]{0:T(128)} %param.13) | copy-start | bytes 1540
  7.2 384.0 %reduce-scatter.2.cloned.1.call-start = ((), (), s32[]{:S(2)}) async-start(), calls=%async_computation.1 | async-start | bytes 9191424 | tf_op jit(solution)/shard_map/reduce_scatter | solution.py:1089
  59.2 1.7 copy-start.6
  59.2 1.6 copy-start.7
  150.8 1.7 copy-start.8
  150.8 1.7 copy-start.11
  228.3 1.2 copy-start.1
  228.4 2.2 copy-start.5
  359.8 3.4 copy-start.2
  386.3 3.6 copy-start.3
  391.2 2.0 copy-start.4
Sparse Core Ops, SparseCore 0:
  228.5 132.1 reduce-scatter.1

commit v3 on v0

v3 whole, which is shorter than its diff:
```python
import jax
import jax.numpy as jnp
from jax import lax
from jax.experimental import pallas as pl
from jax.experimental.pallas import tpu as pltpu
from jax.sharding import PartitionSpec as P

HEAD_DIM = 64
ROT = 16
DOCS = 4
EPS = 1e-05
SCALE = HEAD_DIM ** (-0.5)

ROWS = 128
WIDTH = 2048
TENSOR = 8
GROUP = ROWS * TENSOR
HALF = ROWS // 2
HEADS_DEV = 4
LOCAL = HEADS_DEV * HEAD_DIM
QBLOCK = 256
UNITS = 704
LANES = 128
MESH = pl.DeviceIdType.MESH
BF16 = jnp.bfloat16
F32 = jnp.float32
VMEM_LIMIT = 62 * 2**20


class Around:
    def __init__(self):
        dp, tensor = lax.axis_index("dp"), lax.axis_index("tensor")
        y, z = tensor // 2, lax.rem(tensor, 2)
        up, down, far = lax.rem(y + 1, 4), lax.rem(y + 3, 4), lax.rem(y + 2, 4)
        other = 1 - z
        self.me, self.across = y * 2 + z, y * 2 + other
        self.up, self.down, self.far = up * 2 + z, down * 2 + z, far * 2 + z
        self.up_o, self.down_o, self.far_o = up * 2 + other, down * 2 + other, far * 2 + other
        self.y, self.z = y, z
        self.y_up, self.y_down, self.y_far = up, down, far
        self.to_up, self.to_down, self.to_across = (dp, self.up), (dp, self.down), (dp, self.across)
        self.to_rest = [(dp, slot) for slot in (self.far, self.up_o, self.down_o, self.far_o)]

    def peers(self):
        return [self.to_up, self.to_down, self.to_across]


class Ring:
    def __init__(self):
        dp, tensor = lax.axis_index("dp"), lax.axis_index("tensor")
        zh, x, core = dp // 8, lax.rem(dp // 2, 4), lax.rem(dp, 2)
        self.zh, self.x, self.core, self.dp, self.tensor = zh, x, core, dp, tensor
        self.xs = [lax.rem(x + step, 4) for step in range(4)]
        self.to_x = [(self.index(zh, self.xs[step], core), tensor) for step in range(4)]
        self.to_zh = (self.index(1 - zh, x, core), tensor)
        self.to_core = (self.index(zh, x, 1 - core), tensor)
        self.to_zh_core = (self.index(1 - zh, x, 1 - core), tensor)

    def index(self, zh, x, core):
        return zh * 8 + x * 2 + core

    def peers(self):
        return self.to_x[1:] + [self.to_zh, self.to_core]


def hail(peers):
    barrier = pltpu.get_barrier_semaphore()
    for peer in peers:
        pl.semaphore_signal(barrier, inc=1, device_id=peer, device_id_type=MESH)


def hear(peers):
    pl.semaphore_wait(pltpu.get_barrier_semaphore(), len(peers))


class Mail:
    def __init__(self, sends, receives):
        self.sends, self.receives = sends, receives
        self.out = []

    def copy(self, number, source, target, device):
        return pltpu.make_async_remote_copy(
            src_ref=source,
            dst_ref=target,
            send_sem=self.sends.at[number],
            recv_sem=self.receives.at[number],
            device_id=device,
            device_id_type=MESH,
        )

    def send(self, number, source, target, device):
        copy = self.copy(number, source, target, device)
        copy.start()
        self.out.append(copy)

    def landed(self, number, target, device):
        self.copy(number, target, target, device).wait_recv()

    def finish(self):
        for copy in self.out:
            copy.wait_send()
        self.out = []


MIDDLE = {48: 96, 32: 80}
GATHER_MAILS = 15


def gather_steps(around, mail, rows, top):
    a, middle = around, MIDDLE[top]

    def part(slot, first, last):
        return rows.at[slot, pl.ds(first, last - first)]

    def send(number, slot, first, last, device):
        mail.send(number, part(slot, first, last), part(slot, first, last), device)

    def got(number, slot, first, last):
        mail.landed(number, part(slot, first, last), a.to_up)

    def begin():
        send(0, a.me, 0, HALF, a.to_up)
        send(1, a.me, HALF, ROWS, a.to_down)
        send(2, a.me, top, ROWS, a.to_across)
        send(3, a.me, HALF, ROWS, a.to_up)
        send(4, a.me, 0, HALF, a.to_down)
        send(5, a.me, 0, top, a.to_across)

    def one():
        got(0, a.down, 0, HALF)
        send(6, a.down, 0, HALF, a.to_up)
        send(7, a.down, 0, top, a.to_across)
        got(1, a.up, HALF, ROWS)
        send(8, a.up, HALF, ROWS, a.to_down)
        got(2, a.across, top, ROWS)
        send(9, a.across, top, ROWS, a.to_up)
        send(10, a.across, top, ROWS, a.to_down)

    def two():
        got(4, a.up, 0, HALF)
        send(11, a.up, 0, top, a.to_across)
        got(3, a.down, HALF, ROWS)
        got(5, a.across, 0, top)

    def three():
        got(6, a.far, 0, HALF)
        send(12, a.far, 0, top, a.to_across)
        got(8, a.far, HALF, ROWS)

    def four():
        got(9, a.down_o, top, ROWS)
        send(13, a.down_o, top, middle, a.to_up)
        got(10, a.up_o, top, ROWS)
        send(14, a.up_o, middle, ROWS, a.to_down)

    def five():
        got(7, a.down_o, 0, top)
        got(11, a.up_o, 0, top)

    def six():
        got(13, a.far_o, top, middle)
        got(14, a.far_o, middle, ROWS)
        got(12, a.far_o, 0, top)

    return begin, one, two, three, four, five, six


def added(*terms):
    total = terms[0].astype(F32)
    for term in terms[1:]:
        total = total + term.astype(F32)
    return total


SCATTER_MAILS = 20


def scatter_boxes(top):
    middle = MIDDLE[top]
    last, inner, rest = ROWS - middle, middle - top, HALF - top
    counts = (last, inner, top, HALF, top, top, last, inner, HALF, top)
    counts += (top, inner, last, HALF, top, top, ROWS - top, rest, rest, rest, ROWS - top)
    return counts, tuple(sum(counts[:k]) for k in range(len(counts)))


def scatter_rows_needed(top):
    return sum(scatter_boxes(top)[0])


class Scatter:
    def __init__(self, around, mail, parts, land, top):
        self.a, self.mail, self.parts, self.land, self.top = around, mail, parts, land, top
        self.middle = MIDDLE[top]
        self.counts, self.firsts = scatter_boxes(top)

    def part(self, slot, first, last):
        return self.parts.at[slot, pl.ds(first, last - first)]

    def box(self, number):
        return self.land.at[pl.ds(self.firsts[number], self.counts[number])]

    def direct(self, number, slot, first, device):
        source = self.part(slot, first, first + self.counts[number])
        self.mail.send(number, source, self.box(number), device)

    def got(self, number):
        self.mail.landed(number, self.box(number), self.a.to_up)

    def fold(self, stage, slot, first, *others):
        terms = [self.part(slot, first, first + self.counts[stage])[...], self.box(stage)[...]]
        terms += [self.box(other)[...] for other in others]
        self.box(stage)[...] = added(*terms).astype(BF16)

    def from_far_o(self):
        a = self.a
        self.direct(0, a.far_o, self.middle, a.to_up)
        self.direct(1, a.far_o, self.top, a.to_down)
        self.direct(2, a.far_o, 0, a.to_across)

    def from_far(self):
        a = self.a
        self.direct(3, a.far, HALF, a.to_up)
        self.direct(17, a.far, self.top, a.to_down)

    def from_up_o(self):
        a = self.a
        self.direct(4, a.up_o, 0, a.to_across)
        self.direct(7, a.up_o, self.top, a.to_up)

    def from_down_o(self):
        a = self.a
        self.direct(5, a.down_o, 0, a.to_across)
        self.direct(6, a.down_o, self.middle, a.to_down)

    def from_up(self):
        self.direct(18, self.a.up, self.top, self.a.to_up)

    def from_down(self):
        self.direct(8, self.a.down, HALF, self.a.to_down)

    def from_across(self):
        self.direct(9, self.a.across, 0, self.a.to_across)

    def one(self):
        a, send, box = self.a, self.mail.send, self.box
        self.got(1)
        self.fold(1, a.down_o, self.top)
        send(11, box(1), box(11), a.to_down)
        self.got(0)
        self.fold(0, a.up_o, self.middle)
        send(12, box(0), box(12), a.to_up)
        self.got(2)
        self.fold(2, a.far, 0)
        send(10, box(2), box(10), a.to_down)
        self.got(3)
        self.fold(3, a.up, HALF)
        send(13, box(3), box(13), a.to_up)

    def two(self):
        a, send, box = self.a, self.mail.send, self.box
        self.got(17)
        self.fold(17, a.down, self.top)
        send(19, box(17), box(19), a.to_down)
        self.got(4)
        self.fold(4, a.up, 0)
        send(14, box(4), box(14), a.to_up)
        for number in (6, 7, 11, 12):
            self.got(number)
        inner, last = self.middle - self.top, ROWS - self.middle
        made = self.firsts[20]
        self.land[pl.ds(made, inner), :] = added(
            self.part(a.across, self.top, self.middle)[...], box(7)[...], box(11)[...]
        ).astype(BF16)
        self.land[pl.ds(made + inner, last), :] = added(
            self.part(a.across, self.middle, ROWS)[...], box(6)[...], box(12)[...]
        ).astype(BF16)
        send(16, box(20), box(16), a.to_across)
        self.got(5)
        self.got(10)
        self.fold(5, a.down, 0, 10)
        send(15, box(5), box(15), a.to_down)

    def three(self, total):
        a, top = self.a, self.top
        for number in (8, 9, 13, 14, 18, 19, 16, 15):
            self.got(number)

        def boxed(number, first, last):
            return self.land[pl.ds(self.firsts[number] + first, last - first), :]

        total[pl.ds(0, top), :] = added(
            self.part(a.me, 0, top)[...], *(self.box(k)[...] for k in (9, 14, 15))
        )
        total[pl.ds(top, HALF - top), :] = added(
            self.part(a.me, top, HALF)[...],
            self.box(18)[...],
            self.box(19)[...],
            boxed(16, 0, HALF - top),
        )
        total[pl.ds(HALF, HALF), :] = added(
            self.part(a.me, HALF, ROWS)[...],
            self.box(8)[...],
            self.box(13)[...],
            boxed(16, HALF - top, ROWS - top),
        )


def spread_steps(ring, mail, block):
    r = ring

    def share(number, zh, x, device):
        mail.send(number, block(zh, x, r.core), block(zh, x, r.core), device)

    def came(number, zh, x, core):
        mail.landed(number, block(zh, x, core), r.to_core)

    def begin():
        share(0, r.zh, r.x, r.to_zh)
        for step in (1, 3, 2):
            share(step, r.zh, r.x, r.to_x[step])
        share(7, r.zh, r.x, r.to_core)

    def one():
        came(0, 1 - r.zh, r.x, r.core)
        for step in (1, 3, 2):
            share(3 + step, 1 - r.zh, r.x, r.to_x[step])
        share(8, 1 - r.zh, r.x, r.to_core)

    def two():
        for step in (1, 3, 2):
            came(step, r.zh, r.xs[4 - step], r.core)
            share(8 + step, r.zh, r.xs[4 - step], r.to_core)

    def three():
        for step in (1, 3, 2):
            came(3 + step, 1 - r.zh, r.xs[4 - step], r.core)
            share(11 + step, 1 - r.zh, r.xs[4 - step], r.to_core)

    def four():
        sibling = 1 - r.core
        came(7, r.zh, r.x, sibling)
        came(8, 1 - r.zh, r.x, sibling)
        for step in (1, 3, 2):
            came(8 + step, r.zh, r.xs[4 - step], sibling)
            came(11 + step, 1 - r.zh, r.xs[4 - step], sibling)

    return begin, one, two, three, four


SPREAD_MAILS = 15
FOLDS = [(side, step) for step in (1, 3, 2, 0) for side in (1, 0)]


class Fold:
    def __init__(self, ring, mail, grads, own, land):
        self.r, self.mail, self.grads, self.own, self.land = ring, mail, grads, own, land

    def place(self, side, step):
        zh = 1 - self.r.zh if side else self.r.zh
        return zh * 4 + self.r.xs[step]

    def send(self, number):
        side, step = FOLDS[number]
        source = self.grads.at[self.place(side, step)]
        self.mail.send(number, source, self.land.at[number], self.r.to_x[step])

    def cross(self):
        for number in (0, 2, 4):
            self.mail.landed(number, self.land.at[number], self.r.to_core)
        self.land[0] = added(self.own(1), self.land[0], self.land[2], self.land[4]).astype(BF16)
        self.mail.send(6, self.land.at[0], self.land.at[6], self.r.to_zh)

    def near(self):
        for number in (1, 3, 5):
            self.mail.landed(number, self.land.at[number], self.r.to_core)

    def result(self):
        self.mail.landed(6, self.land.at[6], self.r.to_core)
        land = self.land
        return added(self.own(0), land[1], land[3], land[5], land[6])


FOLD_MAILS = 7

SUM_ROWS, SUM_NORMS = 72, 64
SUM_BOXES, SUM_MAILS = 14, 13


def sum_everywhere(a, r, mail, boxes, values):
    def stage(base, count, mine, sources, peers):
        view = pl.ds(0, count)
        for number, peer in enumerate(peers):
            mail.send(base + number, boxes.at[base + mine, view], boxes.at[base + mine, view], peer)
        for number, source in enumerate(sources):
            mail.landed(base + number, boxes.at[base + source, view], peers[0])
        result = boxes[base, view]
        for k in range(1, len(peers) + 1):
            result = result + boxes[base + k, view]
        return result

    boxes[r.x] = values
    first = stage(0, SUM_ROWS, r.x, [r.xs[3], r.xs[2], r.xs[1]], r.to_x[1:])
    place = r.zh * 2 + r.core
    boxes[4 + place] = first
    second = stage(
        4,
        SUM_ROWS,
        place,
        [(1 - r.zh) * 2 + r.core, r.zh * 2 + 1 - r.core, (1 - r.zh) * 2 + 1 - r.core],
        [r.to_zh, r.to_core, r.to_zh_core],
    )
    boxes[8 + a.y, pl.ds(0, SUM_NORMS)] = second[:SUM_NORMS]
    y_peers = [a.to_up, a.to_rest[0], a.to_down]
    third = stage(8, SUM_NORMS, a.y, [a.y_down, a.y_far, a.y_up], y_peers)
    boxes[12 + a.z, pl.ds(0, SUM_NORMS)] = third
    fourth = stage(12, SUM_NORMS, a.z, [1 - a.z], [a.to_across])
    return jnp.concatenate([fourth, second[SUM_NORMS:]], axis=0)


def dot(left, right):
    return lax.dot_general(left, right, (((1,), (0,)), ((), ())), preferred_element_type=F32)


def dot_t(left, right):
    return lax.dot_general(left, right, (((1,), (1,)), ((), ())), preferred_element_type=F32)


def normalized(values):
    centred = values - jnp.mean(values, axis=1, keepdims=True)
    variance = jnp.mean(centred * centred, axis=1, keepdims=True)
    rinv = lax.rsqrt(variance + EPS)
    return centred * rinv, rinv


def norm_back(incoming, normal, rinv, gain):
    scaled = incoming * gain
    inner = scaled - jnp.mean(scaled, axis=1, keepdims=True)
    inner = inner - normal * jnp.mean(scaled * normal, axis=1, keepdims=True)
    gain_grad = jnp.sum(incoming * normal, axis=0, keepdims=True)
    return rinv * inner, gain_grad, jnp.sum(incoming, axis=0, keepdims=True)


def turned(values, tables, first, sign):
    rows = pl.ds(first, values.shape[0])
    cosine, minus, plus = tables[0, rows], tables[1, rows], tables[2, rows]
    halves = []
    for lane in range(0, LOCAL, LANES):
        part = values[:, lane : lane + LANES]
        left = pltpu.roll(part, LANES - ROT // 2, 1)
        right = pltpu.roll(part, ROT // 2, 1)
        halves.append(part * cosine + sign * (left * minus + right * plus))
    return jnp.concatenate(halves, axis=1)


def head_lanes(head, rows):
    return lax.broadcasted_iota(jnp.int32, (rows, LOCAL), 1) // HEAD_DIM == head


def only(mask, values):
    return jnp.where(mask, values, jnp.zeros_like(values))


def place_rows(id_rows, frequency, tables, start_rows, start_lanes):
    ids = jnp.max(id_rows[...], axis=1)
    shape = (TENSOR, ROWS)
    index = lax.broadcasted_iota(jnp.int32, shape, 0) * ROWS
    index = (index + lax.broadcasted_iota(jnp.int32, shape, 1)).astype(F32)
    offset = jnp.zeros(shape, F32)
    for number in range(1, DOCS):
        before = ((ids >= 0) & (ids < number)).astype(F32)
        count = jnp.sum(jnp.sum(before, axis=1, keepdims=True), axis=0, keepdims=True)
        offset = jnp.where(ids == number, count, offset)
    start = jnp.where(ids >= 0, offset, index)
    position = index - offset

    def along(values):
        return jnp.concatenate([values[t : t + 1] for t in range(TENSOR)], axis=1)

    angle = frequency[:, :1] * along(position)
    cosine, sine = jnp.cos(angle), jnp.sin(angle)
    none = jnp.zeros_like(sine)
    rest = (HEAD_DIM - ROT) // 8
    columns = (
        [cosine, cosine] + [jnp.ones_like(sine)] * rest,
        [-sine, none] + [none] * rest,
        [none, sine] + [none] * rest,
    )
    for number, parts in enumerate(columns):
        tables[number] = jnp.concatenate(parts + parts, axis=0).T
    lanes = jnp.broadcast_to(along(start), (8, GROUP))
    start_lanes[...] = lanes
    start_rows[...] = jnp.concatenate([lanes] * (LANES // 8), axis=0).T


def vmem(count):
    return [pl.BlockSpec(memory_space=pltpu.VMEM)] * count


def anywhere(count):
    return [pl.BlockSpec(memory_space=pl.ANY)] * count


def pairs(count):
    return [pltpu.SemaphoreType.DMA((count,)), pltpu.SemaphoreType.DMA((count,))]


def params(collective):
    return pltpu.CompilerParams(
        collective_id=collective, has_side_effects=True, vmem_limit_bytes=VMEM_LIMIT
    )


TOP_ROWS, TOP_COTS, TOP_BRANCH = 48, 32, 48


def attention_kernel(
    tokens,
    ids,
    bias,
    out_shard,
    gain1,
    shift1,
    gain2,
    shift2,
    frequency,
    qkv_shard,
    gate_up,
    down,
    own_cots,
    normed2,
    mixed,
    tables,
    start_lanes,
    acts,
    attended,
    logs,
    rows_kept,
    weights_kept,
    cots,
    feed,
    rows,
    weights,
    id_rows,
    start_rows,
    parts,
    land,
    total,
    r_sends,
    r_receives,
    c_sends,
    c_receives,
    b_sends,
    b_receives,
    w_sends,
    w_receives,
    f_sends,
    f_receives,
    i_sends,
    i_receives,
    local,
):
    a, r = Around(), Ring()
    rmail, cmail, bmail = Mail(r_sends, r_receives), Mail(c_sends, c_receives), Mail(b_sends, b_receives)
    wmail, fmail, imail = Mail(w_sends, w_receives), Mail(f_sends, f_receives), Mail(i_sends, i_receives)
    peers = a.peers() + a.to_rest + r.peers()
    hail(peers)

    def weight_block(zh, x, core):
        first = pl.multiple_of(r.index(zh, x, core) * ROWS, ROWS)
        return weights.at[:, pl.ds(first, ROWS), :]

    def feed_block(zh, x, core):
        return feed.at[r.index(zh, x, core)]

    mine = pl.multiple_of(r.dp * ROWS, ROWS)
    copies = [
        pltpu.make_async_copy(qkv_shard, weights.at[pl.ds(0, 3), pl.ds(mine, ROWS)], local.at[0]),
        pltpu.make_async_copy(gate_up, feed.at[r.dp, pl.ds(0, 2 * UNITS)], local.at[1]),
        pltpu.make_async_copy(down, feed.at[r.dp, pl.ds(2 * UNITS, UNITS)], local.at[2]),
        pltpu.make_async_copy(own_cots, cots.at[a.me], local.at[3]),
    ]
    for copy in copies:
        copy.start()
    id_rows[a.me] = jnp.broadcast_to(ids[...], (8, ROWS))
    weights[3, pl.ds(mine, ROWS), :] = out_shard[...].T
    normal, _ = normalized(tokens[...].astype(F32))
    rows[a.me] = (normal * gain1[...] + shift1[...]).astype(BF16)
    hear(peers)

    group = [
        (0, a.to_up, a.down),
        (1, a.to_down, a.up),
        (2, a.to_across, a.across),
        (3, a.to_rest[0], a.far),
        (4, a.to_rest[1], a.down_o),
        (5, a.to_rest[2], a.up_o),
        (6, a.to_rest[3], a.far_o),
    ]
    for number, device, _ in group:
        imail.send(number, id_rows.at[a.me], id_rows.at[a.me], device)
    gather = gather_steps(a, rmail, rows, TOP_ROWS)
    others = gather_steps(a, cmail, cots, TOP_COTS)
    spread = spread_steps(r, wmail, weight_block)
    feeds = spread_steps(r, fmail, feed_block)
    scatter = Scatter(a, bmail, parts, land, TOP_BRANCH)
    gather[0]()
    for copy in copies:
        copy.wait()
    spread[0]()
    for number, _, slot in group:
        imail.landed(number, id_rows.at[slot], a.to_up)
    place_rows(id_rows, frequency, tables, start_rows, start_lanes)
    spread[1]()
    gather[1]()
    gather[2]()
    spread[2]()
    spread[3]()
    gather[3]()
    feeds[0]()
    gather[4]()
    others[0]()
    spread[4]()

    def project(y):
        first = pl.multiple_of(y * QBLOCK, QBLOCK)
        chunk = rows[pl.ds(2 * y, 2)].reshape(QBLOCK, WIDTH)
        for c in range(3):
            pre = dot(chunk, weights[c]) + bias[pl.ds(c, 1), :]
            if c < 2:
                pre = turned(pre, tables, first, 1.0)
            acts[c, pl.ds(first, QBLOCK), :] = pre.astype(BF16)

    project(a.y)
    gather[5]()
    project(a.y_down)
    project(a.y_up)
    gather[6]()
    project(a.y_far)
    keeps = [
        pltpu.make_async_copy(rows, rows_kept, local.at[4]),
        pltpu.make_async_copy(weights, weights_kept, local.at[5]),
    ]
    for keep in keeps:
        keep.start()

    def attend(first):
        count = first + QBLOCK
        query = acts[0, pl.ds(first, QBLOCK), :] * BF16(SCALE)
        row = first + lax.broadcasted_iota(jnp.int32, (QBLOCK, count), 0)
        column = lax.broadcasted_iota(jnp.int32, (QBLOCK, count), 1)
        start = start_rows[pl.ds(first, QBLOCK), pl.ds(0, 1)]
        allow = (column <= row) & (column.astype(F32) >= start)
        lane = lax.broadcasted_iota(jnp.int32, (QBLOCK, LANES), 1)

        def one_head(head, carry):
            out, log = carry
            masked = only(head_lanes(head, QBLOCK), query)
            scores = dot_t(masked, acts[1, pl.ds(0, count), :])
            scores = jnp.where(allow, scores, -1e30)
            highest = jnp.max(scores, axis=1, keepdims=True)
            expon = jnp.exp(scores - highest)
            sums = jnp.sum(expon, axis=1, keepdims=True)
            values = only(head_lanes(head, count), acts[2, pl.ds(0, count), :])
            out = out + dot(expon.astype(BF16), values) / sums
            log = jnp.where(lane == head, highest + jnp.log(sums), log)
            return out, log

        out, log = lax.fori_loop(
            0,
            HEADS_DEV,
            one_head,
            (jnp.zeros((QBLOCK, LOCAL), F32), jnp.zeros((QBLOCK, LANES), F32)),
        )
        out = out.astype(BF16)
        attended[pl.ds(first, QBLOCK), :] = out
        logs[:, pl.ds(first, QBLOCK)] = log.T[:8]
        branch = dot_t(out, weights[3]).astype(BF16)
        parts[first // ROWS] = branch[:ROWS]
        parts[first // ROWS + 1] = branch[ROWS:]

    attend(0)
    others[1]()
    attend(QBLOCK)
    others[2]()
    attend(2 * QBLOCK)
    others[3]()
    feeds[1]()
    attend(3 * QBLOCK)
    scatter.from_far_o()
    scatter.from_far()
    scatter.from_up_o()
    scatter.from_down_o()
    scatter.from_up()
    scatter.from_down()
    scatter.from_across()
    others[4]()
    feeds[2]()
    scatter.one()
    scatter.two()
    feeds[3]()
    others[5]()
    others[6]()
    scatter.three(total)
    after = tokens[...].astype(F32) + total[...]
    mixed[...] = after
    normal, _ = normalized(after)
    normed2[...] = (normal * gain2[...] + shift2[...]).astype(BF16)
    feeds[4]()
    for mail in (rmail, cmail, bmail, wmail, fmail, imail):
        mail.finish()
    for keep in keeps:
        keep.wait()


def attention_forward(tokens, ids, bias, out_shard, norms, frequency, qkv_shard, gate_up, down, cots):
    group = (TENSOR, ROWS, WIDTH)
    weights = (4, WIDTH, LOCAL)
    return pl.pallas_call(
        attention_kernel,
        out_shape=(
            jax.ShapeDtypeStruct((ROWS, WIDTH), BF16),
            jax.ShapeDtypeStruct((ROWS, WIDTH), F32),
            jax.ShapeDtypeStruct((3, GROUP, LANES), F32),
            jax.ShapeDtypeStruct((8, GROUP), F32),
            jax.ShapeDtypeStruct((3, GROUP, LOCAL), BF16),
            jax.ShapeDtypeStruct((GROUP, LOCAL), BF16),
            jax.ShapeDtypeStruct((8, GROUP), F32),
            jax.ShapeDtypeStruct(group, BF16),
            jax.ShapeDtypeStruct(weights, BF16),
            jax.ShapeDtypeStruct(group, BF16),
            jax.ShapeDtypeStruct((16, 3 * UNITS, ROWS), BF16),
        ),
        in_specs=vmem(9) + anywhere(4),
        out_specs=tuple(vmem(7) + anywhere(4)),
        scratch_shapes=[
            pltpu.VMEM(group, BF16),
            pltpu.VMEM(weights, BF16),
            pltpu.VMEM((TENSOR, 8, ROWS), jnp.int32),
            pltpu.VMEM((GROUP, LANES), F32),
            pltpu.VMEM(group, BF16),
            pltpu.VMEM((scatter_rows_needed(TOP_BRANCH), WIDTH), BF16),
            pltpu.VMEM((ROWS, WIDTH), F32),
            *pairs(GATHER_MAILS),
            *pairs(GATHER_MAILS),
            *pairs(SCATTER_MAILS),
            *pairs(SPREAD_MAILS),
            *pairs(SPREAD_MAILS),
            *pairs(7),
            pltpu.SemaphoreType.DMA((6,)),
        ],
        compiler_params=params(0),
        name="attention_forward",
    )(tokens, ids, bias, out_shard, *norms, frequency, qkv_shard, gate_up, down, cots)


TOP_FEED = 48


def feed_kernel(
    own,
    mixed,
    own_cots,
    gain2,
    cots_in,
    feed,
    grad_mixed,
    branch_grad,
    norm_grads,
    halves,
    outs_kept,
    rows,
    cots,
    weights,
    parts,
    outs,
    acts,
    grads,
    land,
    core_land,
    total,
    g_sends,
    g_receives,
    s_sends,
    s_receives,
    w_sends,
    w_receives,
    w_local,
    local,
):
    a, r = Around(), Ring()
    gmail, mail, wmail = Mail(g_sends, g_receives), Mail(s_sends, s_receives), Mail(w_sends, w_receives)
    peers = a.peers() + [r.to_core]
    hail(peers)
    loads = [
        pltpu.make_async_copy(feed.at[n], weights.at[:, pl.ds(n * ROWS, ROWS)], w_local.at[n])
        for n in range(16)
    ]
    keep = pltpu.make_async_copy(cots_in, cots, local.at[0])
    for copy in loads + [keep]:
        copy.start()
    rows[a.me] = own[...]
    hear(peers)
    gather = gather_steps(a, gmail, rows, TOP_FEED)
    scatter = Scatter(a, mail, parts, land, TOP_FEED)
    gather[0]()
    for copy in loads + [keep]:
        copy.wait()

    def pair(*slots):
        x = jnp.concatenate([rows[slot] for slot in slots], axis=0)
        given = jnp.concatenate([cots[slot] for slot in slots], axis=0)
        gate = dot_t(x, weights[pl.ds(0, UNITS), :])
        upward = dot_t(x, weights[pl.ds(UNITS, UNITS), :])
        grad_hidden = dot_t(given, weights[pl.ds(2 * UNITS, UNITS), :])
        sigma = jax.nn.sigmoid(gate)
        silu = gate * sigma
        hidden = (silu * upward).astype(BF16)
        grad_gate = (grad_hidden * upward * (sigma + silu * (1.0 - sigma))).astype(BF16)
        grad_up = (grad_hidden * silu).astype(BF16)
        back = dot(grad_gate, weights[pl.ds(0, UNITS), :])
        back = (back + dot(grad_up, weights[pl.ds(UNITS, UNITS), :])).astype(BF16)
        for number, slot in enumerate(slots):
            parts[slot] = back[number * ROWS : (number + 1) * ROWS]
        return hidden, grad_gate, grad_up

    def rest(kept, *slots):
        hidden, grad_gate, grad_up = kept
        out = dot(hidden, weights[pl.ds(2 * UNITS, UNITS), :]).astype(BF16)
        for number, slot in enumerate(slots):
            chunk = slice(number * ROWS, (number + 1) * ROWS)
            outs[slot] = out[chunk]
            lanes = pl.ds(pl.multiple_of(slot * ROWS, ROWS), ROWS)
            acts[pl.ds(0, UNITS), lanes] = grad_gate[chunk].T
            acts[pl.ds(UNITS, UNITS), lanes] = grad_up[chunk].T
            acts[pl.ds(2 * UNITS, UNITS), lanes] = hidden[chunk].T

    gather[1]()
    gather[2]()
    rest(pair(a.me, a.across), a.me, a.across)
    gather[3]()
    kept = pair(a.down, a.up)
    gather[4]()
    rest(kept, a.down, a.up)
    gather[5]()
    scatter.from_across()
    scatter.from_up()
    scatter.from_down()
    kept = pair(a.far, a.down_o)
    scatter.from_far()
    scatter.from_down_o()
    gather[6]()
    last = pair(a.far_o, a.up_o)
    scatter.from_far_o()
    scatter.from_up_o()
    rest(kept, a.far, a.down_o)
    rest(last, a.far_o, a.up_o)
    outs_copy = pltpu.make_async_copy(outs, outs_kept, local.at[1])
    outs_copy.start()
    scatter.one()

    def to_sibling(index):
        return wmail.copy(index, grads.at[index, 1 - r.core], core_land.at[index], r.to_core)

    def weight_grad(index, carry):
        columns = pl.ds(pl.multiple_of(index * 2 * ROWS, 2 * ROWS), 2 * ROWS)
        both = dot(acts[pl.ds(0, 2 * UNITS), :], rows[:, :, columns].reshape(GROUP, 2 * ROWS))
        low = dot(acts[pl.ds(2 * UNITS, UNITS), :], cots[:, :, columns].reshape(GROUP, 2 * ROWS))
        for core in range(2):
            lanes = slice(core * ROWS, (core + 1) * ROWS)
            grads[index, core, pl.ds(0, 2 * UNITS), :] = both[:, lanes].astype(BF16)
            grads[index, core, pl.ds(2 * UNITS, UNITS), :] = low[:, lanes].astype(BF16)
        to_sibling(index).start()
        return carry

    def core_sum(index, carry):
        to_sibling(index).wait()
        core_land[index] = added(grads[index, r.core], core_land[index]).astype(BF16)
        return carry

    lax.fori_loop(0, 4, weight_grad, 0)
    scatter.two()
    lax.fori_loop(4, 8, weight_grad, 0)
    lax.fori_loop(0, 8, core_sum, 0)
    halves_copy = pltpu.make_async_copy(core_land, halves, local.at[2])
    halves_copy.start()
    scatter.three(total)
    normal, rinv = normalized(mixed[...])
    back, gain_grad, shift_grad = norm_back(total[...], normal, rinv, gain2[...])
    back = own_cots[...].astype(F32) + back
    grad_mixed[...] = back
    branch_grad[...] = back.astype(BF16)
    norm_grads[...] = jnp.concatenate([gain_grad, shift_grad], axis=0)
    gmail.finish()
    mail.finish()
    outs_copy.wait()
    halves_copy.wait()


def feed_forward(own, mixed, own_cots, gain2, cots, feed):
    group = (TENSOR, ROWS, WIDTH)
    blocks = (8, 3 * UNITS, ROWS)
    return pl.pallas_call(
        feed_kernel,
        out_shape=(
            jax.ShapeDtypeStruct((ROWS, WIDTH), F32),
            jax.ShapeDtypeStruct((ROWS, WIDTH), BF16),
            jax.ShapeDtypeStruct((2, WIDTH), F32),
            jax.ShapeDtypeStruct(blocks, BF16),
            jax.ShapeDtypeStruct(group, BF16),
        ),
        in_specs=vmem(4) + anywhere(2),
        out_specs=tuple(vmem(3) + anywhere(2)),
        scratch_shapes=[
            pltpu.VMEM(group, BF16),
            pltpu.VMEM(group, BF16),
            pltpu.VMEM((3 * UNITS, WIDTH), BF16),
            pltpu.VMEM(group, BF16),
            pltpu.VMEM(group, BF16),
            pltpu.VMEM((3 * UNITS, GROUP), BF16),
            pltpu.VMEM((8, 2, 3 * UNITS, ROWS), BF16),
            pltpu.VMEM((scatter_rows_needed(TOP_FEED), WIDTH), BF16),
            pltpu.VMEM(blocks, BF16),
            pltpu.VMEM((ROWS, WIDTH), F32),
            *pairs(GATHER_MAILS),
            *pairs(SCATTER_MAILS),
            *pairs(8),
            pltpu.SemaphoreType.DMA((16,)),
            pltpu.SemaphoreType.DMA((3,)),
        ],
        compiler_params=params(1),
        name="feed_forward",
    )(own, mixed, own_cots, gain2, cots, feed)


TOP_GRADS, TOP_OUTS, TOP_BACK = 48, 32, 48


def attention_back_kernel(
    own,
    grad_mixed,
    mixed,
    tokens,
    gain1,
    norm2_grads,
    tables,
    start_lanes,
    acts,
    attended,
    logs,
    weights,
    halves,
    first_rows,
    outs,
    layer_out,
    token_grad,
    qkv_grad,
    out_grad,
    gate_up_grad,
    down_grad,
    sums,
    rows,
    before,
    grad_out,
    grads_qkv,
    keys_turned,
    turns,
    parts,
    out_parts,
    grads,
    land,
    out_land,
    core_land,
    w_land,
    f_land,
    own_halves,
    total,
    boxes,
    g_sends,
    g_receives,
    s_sends,
    s_receives,
    o_sends,
    o_receives,
    k_sends,
    k_receives,
    w_sends,
    w_receives,
    f_sends,
    f_receives,
    a_sends,
    a_receives,
    local,
):
    a, r = Around(), Ring()
    gmail, mail, omail = Mail(g_sends, g_receives), Mail(s_sends, s_receives), Mail(o_sends, o_receives)
    kmail, wmail, fmail = Mail(k_sends, k_receives), Mail(w_sends, w_receives), Mail(f_sends, f_receives)
    amail = Mail(a_sends, a_receives)
    peers = a.peers() + a.to_rest[:1] + r.peers() + [r.to_zh_core]
    hail(peers)
    loads = [
        pltpu.make_async_copy(first_rows, before, local.at[0]),
        pltpu.make_async_copy(outs, out_parts, local.at[1]),
        pltpu.make_async_copy(halves.at[r.zh * 4 + r.x], own_halves.at[0], local.at[2]),
        pltpu.make_async_copy(halves.at[(1 - r.zh) * 4 + r.x], own_halves.at[1], local.at[3]),
    ]
    for copy in loads:
        copy.start()
    rows[a.me] = own[...]
    hear(peers)
    gather = gather_steps(a, gmail, rows, TOP_GRADS)
    out_scatter = Scatter(a, omail, out_parts, out_land, TOP_OUTS)
    scatter = Scatter(a, mail, parts, land, TOP_BACK)
    feed_fold = Fold(r, fmail, halves, lambda side: own_halves[side], f_land)
    fold = Fold(r, wmail, core_land, lambda side: core_land[fold.place(side, 0)], w_land)
    gather[0]()
    for number in range(6):
        feed_fold.send(number)
    keys_turned[...] = acts[1].T
    turns[pl.ds(3 * LOCAL, LOCAL), :] = attended[...].T
    for copy in loads:
        copy.wait()
    gather[1]()
    gather[2]()
    gather[3]()
    gather[4]()

    def back_project(y):
        chunk = rows[pl.ds(2 * y, 2)].reshape(QBLOCK, WIDTH)
        first = pl.multiple_of(y * QBLOCK, QBLOCK)
        grad_out[pl.ds(first, QBLOCK), :] = dot(chunk, weights[3]).astype(BF16)

    out_scatter.from_far_o()
    out_scatter.from_far()
    out_scatter.from_up_o()
    out_scatter.from_down_o()
    out_scatter.from_up()
    out_scatter.from_down()
    out_scatter.from_across()
    back_project(a.y)
    gather[5]()
    back_project(a.y_up)
    back_project(a.y_down)
    gather[6]()
    back_project(a.y_far)

    def attend(first):
        count = first + QBLOCK
        span = pl.ds(first, QBLOCK)
        query = acts[0, span, :] * BF16(SCALE)
        given = grad_out[span, :]
        row = lax.broadcasted_iota(jnp.int32, (count, QBLOCK), 0)
        column = first + lax.broadcasted_iota(jnp.int32, (count, QBLOCK), 1)
        allow = (row <= column) & (row.astype(F32) >= start_lanes[pl.ds(0, 1), span])
        overlap = given.astype(F32) * attended[span, :].astype(F32)
        lane = lax.broadcasted_iota(jnp.int32, (QBLOCK, LANES), 1)
        inner = jnp.zeros((QBLOCK, LANES), F32)
        for head in range(HEADS_DEV):
            summed = jnp.sum(only(head_lanes(head, QBLOCK), overlap), axis=1, keepdims=True)
            inner = jnp.where(lane == head, summed, inner)
        inner = inner.T[:8]
        head_row = lax.broadcasted_iota(jnp.int32, (8, QBLOCK), 0)
        head_rows = lax.broadcasted_iota(jnp.int32, (LOCAL, count), 0) // HEAD_DIM

        def one_head(head, turned_query):
            mask = head_lanes(head, QBLOCK)
            masked, masked_given = only(mask, query), only(mask, given)
            log = jnp.sum(only(head_row == head, logs[:, span]), axis=0, keepdims=True)
            mean = jnp.sum(only(head_row == head, inner), axis=0, keepdims=True)
            scores = dot_t(acts[1, pl.ds(0, count), :], masked)
            probs = only(allow, jnp.exp(scores - log))
            grad_probs = dot_t(acts[2, pl.ds(0, count), :], masked_given)
            grad_scores = (probs * (grad_probs - mean)).astype(BF16)
            grads_qkv[2, pl.ds(0, count), :] += dot(probs.astype(BF16), masked_given)
            grads_qkv[1, pl.ds(0, count), :] += dot(grad_scores, masked)
            keys = only(head_rows == head, keys_turned[:, pl.ds(0, count)])
            return turned_query + dot(keys, grad_scores)

        turned_query = lax.fori_loop(0, HEADS_DEV, one_head, jnp.zeros((LOCAL, QBLOCK), F32))
        grads_qkv[0, span, :] = turned_query.T * SCALE

    grads_qkv[1] = jnp.zeros((GROUP, LOCAL), F32)
    grads_qkv[2] = jnp.zeros((GROUP, LOCAL), F32)
    attend(0)
    attend(QBLOCK)
    out_scatter.one()
    attend(2 * QBLOCK)
    out_scatter.two()
    feed_fold.cross()
    attend(3 * QBLOCK)

    def input_grad(y, sums_so_far):
        first = pl.multiple_of(y * QBLOCK, QBLOCK)
        span = pl.ds(first, QBLOCK)
        back = jnp.zeros((QBLOCK, WIDTH), F32)
        new = []
        for c in range(3):
            pre = grads_qkv[c, span, :]
            if c < 2:
                pre = turned(pre, tables, first, -1.0)
            pre = pre.astype(BF16)
            new.append(jnp.sum(pre.astype(F32), axis=0, keepdims=True))
            back = back + dot_t(pre, weights[c])
            turns[pl.ds(c * LOCAL, LOCAL), span] = pre.T
        parts[pl.ds(2 * y, 2)] = back.astype(BF16).reshape(2, ROWS, WIDTH)
        return sums_so_far + jnp.concatenate(new, axis=0)

    bias_sums = input_grad(a.y_far, jnp.zeros((3, LOCAL), F32))
    scatter.from_far_o()
    scatter.from_far()
    bias_sums = input_grad(a.y_up, bias_sums)
    scatter.from_up_o()
    scatter.from_up()
    bias_sums = input_grad(a.y_down, bias_sums)
    scatter.from_down_o()
    scatter.from_down()
    bias_sums = input_grad(a.y, bias_sums)
    scatter.from_across()

    def to_sibling(index):
        return kmail.copy(index, grads.at[index, 1 - r.core], core_land.at[index], r.to_core)

    def weight_grad(index, carry):
        columns = pl.ds(pl.multiple_of(index * 2 * ROWS, 2 * ROWS), 2 * ROWS)
        three = dot(
            turns[pl.ds(0, 3 * LOCAL), :], before[:, :, columns].reshape(GROUP, 2 * ROWS)
        )
        last = dot(turns[pl.ds(3 * LOCAL, LOCAL), :], rows[:, :, columns].reshape(GROUP, 2 * ROWS))
        for core in range(2):
            lanes = slice(core * ROWS, (core + 1) * ROWS)
            grads[index, core, pl.ds(0, 3 * LOCAL), :] = three[:, lanes].astype(BF16)
            grads[index, core, pl.ds(3 * LOCAL, LOCAL), :] = last[:, lanes].astype(BF16)
        to_sibling(index).start()
        return carry

    def core_sum(index, carry):
        to_sibling(index).wait()
        core_land[index] = added(grads[index, r.core], core_land[index]).astype(BF16)
        return carry

    lax.fori_loop(0, 8, weight_grad, 0)
    scatter.one()
    lax.fori_loop(0, 8, core_sum, 0)
    for number in range(6):
        fold.send(number)
    feed_fold.near()
    feed_sum = feed_fold.result()
    gate_up_grad[...] = feed_sum[: 2 * UNITS]
    down_grad[...] = feed_sum[2 * UNITS :]
    scatter.two()
    out_scatter.three(total)
    layer_out[...] = (mixed[...] + total[...]).astype(BF16)
    fold.cross()
    fold.near()
    scatter.three(total)
    normal, rinv = normalized(tokens[...].astype(F32))
    back, gain_grad, shift_grad = norm_back(total[...], normal, rinv, gain1[...])
    token_grad[...] = (grad_mixed[...] + back).astype(BF16)
    values = jnp.concatenate([gain_grad, shift_grad, norm2_grads[...]], axis=0)
    values = jnp.concatenate([values[:, k : k + LANES] for k in range(0, WIDTH, LANES)], axis=0)
    biases = jnp.concatenate([bias_sums[:, k : k + LANES] for k in range(0, LOCAL, LANES)], axis=0)
    values = jnp.concatenate([values, biases, jnp.zeros((2, LANES), F32)], axis=0)
    sums[...] = sum_everywhere(a, r, amail, boxes, values)
    shard = fold.result()
    for c in range(3):
        qkv_grad[c] = shard[c * LOCAL : (c + 1) * LOCAL].T
    out_grad[...] = shard[3 * LOCAL :]
    for some in (gmail, mail, omail, kmail, wmail, fmail, amail):
        some.finish()


def attention_backward(*operands):
    group = (TENSOR, ROWS, WIDTH)
    block, feed_block = (4 * LOCAL, ROWS), (3 * UNITS, ROWS)
    return pl.pallas_call(
        attention_back_kernel,
        out_shape=(
            jax.ShapeDtypeStruct((ROWS, WIDTH), BF16),
            jax.ShapeDtypeStruct((ROWS, WIDTH), BF16),
            jax.ShapeDtypeStruct((3, ROWS, LOCAL), F32),
            jax.ShapeDtypeStruct((LOCAL, ROWS), F32),
            jax.ShapeDtypeStruct((2 * UNITS, ROWS), F32),
            jax.ShapeDtypeStruct((UNITS, ROWS), F32),
            jax.ShapeDtypeStruct((SUM_ROWS, LANES), F32),
        ),
        in_specs=vmem(12) + anywhere(3),
        out_specs=tuple(vmem(7)),
        scratch_shapes=[
            pltpu.VMEM(group, BF16),
            pltpu.VMEM(group, BF16),
            pltpu.VMEM((GROUP, LOCAL), BF16),
            pltpu.VMEM((3, GROUP, LOCAL), F32),
            pltpu.VMEM((LOCAL, GROUP), BF16),
            pltpu.VMEM((4 * LOCAL, GROUP), BF16),
            pltpu.VMEM(group, BF16),
            pltpu.VMEM(group, BF16),
            pltpu.VMEM((8, 2) + block, BF16),
            pltpu.VMEM((scatter_rows_needed(TOP_BACK), WIDTH), BF16),
            pltpu.VMEM((scatter_rows_needed(TOP_OUTS), WIDTH), BF16),
            pltpu.VMEM((8,) + block, BF16),
            pltpu.VMEM((FOLD_MAILS,) + block, BF16),
            pltpu.VMEM((FOLD_MAILS,) + feed_block, BF16),
            pltpu.VMEM((2,) + feed_block, BF16),
            pltpu.VMEM((ROWS, WIDTH), F32),
            pltpu.VMEM((SUM_BOXES, SUM_ROWS, LANES), F32),
            *pairs(GATHER_MAILS),
            *pairs(SCATTER_MAILS),
            *pairs(SCATTER_MAILS),
            *pairs(8),
            *pairs(FOLD_MAILS),
            *pairs(FOLD_MAILS),
            *pairs(SUM_MAILS),
            pltpu.SemaphoreType.DMA((4,)),
        ],
        compiler_params=params(2),
        name="attention_backward",
    )(*operands)


def body(
    tokens,
    doc_ids,
    qkv_weight,
    qkv_bias,
    out_weight,
    norm1_gain,
    norm1_shift,
    norm2_gain,
    norm2_shift,
    gate_up_weight,
    down_weight,
    cotangent,
):
    norms = [item[None] for item in (norm1_gain, norm1_shift, norm2_gain, norm2_shift)]
    frequency = jnp.power(10000.0, -2.0 * jnp.arange(ROT // 2, dtype=F32) / ROT)
    frequency = jnp.broadcast_to(frequency[:, None], (ROT // 2, LANES))
    gate_up = jnp.swapaxes(gate_up_weight, 1, 2).reshape(2 * UNITS, ROWS)
    normed2, mixed, tables, start, acts, attended, logs, rows, weights, cots, feed = attention_forward(
        tokens,
        doc_ids[None],
        qkv_bias,
        out_weight,
        norms,
        frequency,
        qkv_weight,
        gate_up,
        down_weight,
        cotangent,
    )
    grad_mixed, branch_grad, norm2_grads, halves, outs = feed_forward(
        normed2, mixed, cotangent, norms[2], cots, feed
    )
    layer_out, token_grad, qkv_grad, out_grad, gate_up_grad, down_grad, sums = attention_backward(
        branch_grad,
        grad_mixed,
        mixed,
        tokens,
        norms[0],
        norm2_grads,
        tables,
        start,
        acts,
        attended,
        logs,
        weights,
        halves,
        rows,
        outs,
    )
    norm_sums = jnp.swapaxes(sums[:SUM_NORMS].reshape(WIDTH // LANES, 4, LANES), 0, 1)
    gain1_sum, shift1_sum, gain2_sum, shift2_sum = norm_sums.reshape(4, WIDTH)
    biases = sums[SUM_NORMS : SUM_NORMS + 6].reshape(LOCAL // LANES, 3, LANES)
    return (
        layer_out,
        token_grad,
        qkv_grad,
        jnp.swapaxes(biases, 0, 1).reshape(3, LOCAL),
        out_grad,
        gain1_sum,
        shift1_sum,
        gain2_sum,
        shift2_sum,
        jnp.swapaxes(gate_up_grad.reshape(2, UNITS, ROWS), 1, 2),
        down_grad,
    )


def solution(mesh):
    in_specs = (
        P(("dp", "tensor"), None),
        P(("dp", "tensor")),
        P(None, "dp", "tensor"),
        P(None, "tensor"),
        P("tensor", "dp"),
        P(),
        P(),
        P(),
        P(),
        P(None, "dp", "tensor"),
        P("tensor", "dp"),
        P(("dp", "tensor"), None),
    )
    out_specs = (
        P(("dp", "tensor"), None),
        P(("dp", "tensor"), None),
        P(None, "dp", "tensor"),
        P(None, "tensor"),
        P("tensor", "dp"),
        P(),
        P(),
        P(),
        P(),
        P(None, "dp", "tensor"),
        P("tensor", "dp"),
    )
    return jax.shard_map(body, mesh=mesh, in_specs=in_specs, out_specs=out_specs, check_vma=False)
```

time: 1350 us -> 359 us (0.27)
  waiting for transfers between devices: 978 us -> 0 us
  Pallas kernels: 0 us -> 338 us
  matrix products: 129 us -> 0 us
  blocking collectives: 101 us -> 0 us
  local copies, waits for them, and re-layouts: 66.2 us -> 13.2 us
  other arithmetic: 44.7 us -> 0.01 us
  between operations: 15.2 us -> 1.12 us
    all_gather x8 -> x0, waiting for transfers between devices: 476 us -> none  [the longest x1 90.6 us: body(): lax.all_gather(normed1.astype(jnp.bfloat16), 'tensor', axis=0, tiled=True)]
    pallas_call x0 -> x3, Pallas kernels: none -> 338 us  [the longest x1 140 us: attention_forward(): pl.pallas_call(attention_kernel, out_shape=(jax.ShapeDtypeStruct((ROWS, W...]
    reduce_scatter x4 -> x0, waiting for transfers between devices: 281 us -> none  [the longest x1 92.9 us: body(): lax.psum_scatter(jnp.einsum('ctf,cdf->td', picked, gate_up_full, preferre...]
    unnamed x20 -> x0, waiting for transfers between devices: 221 us -> none
    dot_general x24 -> x0, matrix products: 129 us -> none  [the longest x2 16.3 us: body(): jnp.einsum('qhd,khd->hqk', grad_block, values_all, preferred_element_type...]
    psum x1 -> x0, blocking collectives: 82 us -> none  [body(): lax.psum((gain1_grad, shift1_grad, gain2_grad, shift2_grad, bias_full), (...]
    unnamed x126 -> x8, local copies, waits for them, and re-layouts: 61.9 us -> 9.85 us
    convert_element_type x10 -> x0, other arithmetic: 22.3 us -> none  [the longest x1 8.84 us: body(): grad_scores = (probs * (grad_probs - inner)).astype(jnp.bfloat16)]
  transfers between devices with their start and end apart: 16 -> 0, of which waited for: 15 -> 0; matrix products, arithmetic and copies ran while one was open for 15% -> 0% of each run, Pallas kernels for 0% -> 0%
where the time goes in v3:
time: 359 us; the launch traced here: 352 us
  Pallas kernels  338 us (94%)
  local copies, waits for them, and re-layouts  13.2 us (4%)
    pallas_call x1, Pallas kernels, attention_forward(): pl.pallas_call(attention_kernel, out_shape=(jax.ShapeDtypeStruct((ROWS, W...  140 us
    pallas_call x1, Pallas kernels, attention_backward(): pl.pallas_call(attention_back_kernel, out_shape=(jax.ShapeDtypeStruct((RO...  129 us
    pallas_call x1, Pallas kernels, feed_forward(): pl.pallas_call(feed_kernel, out_shape=(jax.ShapeDtypeStruct((ROWS, WIDTH)...  68.8 us
    unnamed x8, local copies, waits for them, and re-layouts  9.85 us

profile of v3, /device:TPU:0, one launch (start us, length us, event | category | flops | bytes accessed | tf_op | source)
XLA Modules:
  0.0 352.1 jit_solution(10217147315530886939)
XLA Ops:
  0.7 0.7 broadcast_in_dim.26.frequency
  1.3 139.5 %attention_forward.1 = (bf16[128,2048]{1,0:T(8,128)(2,1)}, f32[128,2048]{1,0:T(8,128)}, f32[3,1024,128]{2,1,0:T(8,128)}, f32[8,1024]{1,0:T(8,128)}, bf16[3,1024,...) custom-call(bf16[128,2048]{1,0:T(8,128)(2,1)} %tokens.3, ...), custom_call_target="tpu_custom_call" | custom-call | tf_op jit(solution)/shard_map/attention_forward/pallas_call | solution.py:718
  140.9 68.8 %feed_forward.1 = (f32[128,2048]{1,0:T(8,128)}, bf16[128,2048]{1,0:T(8,128)(2,1)}, f32[2,2048]{1,0:T(2,128)}, bf16[8,2112,128]{2,1,0:T(8,128)(2,1)}, bf16[8,128,2048]{2,1,0:T(8,128)(2,1)}) custom-call(bf16[128,2048]{1,0:T(8,128)(2,1)} %get-tuple-element.34.own, f32[128,2048]{1,0:T(8,128)} %get-tuple-element.35.mixed, bf16[128,2048]{1,0:T(8,128)(2,1)} %own_cots.3, ...), custom_call_target="tpu_custom_call" | custom-call | tf_op jit(solution)/shard_map/feed_forward/pallas_call | solution.py:902
  209.7 129.3 %attention_backward.1 = (bf16[128,2048]{1,0:T(8,128)(2,1)}, bf16[128,2048]{1,0:T(8,128)(2,1)}, f32[3,128,256]{2,1,0:T(8,128)}, f32[256,128]{1,0:T(8,128)}, f32[1...) custom-call(bf16[128,2048]{1,0:T(8,128)(2,1)} %get-tuple-element.38.own, ...), custom_call_target="tpu_custom_call" | custom-call | tf_op jit(solution)/shard_map/attention_backward/pallas_call | solution.py:1174
  339.1 0.0 copy-start
  339.1 0.7 slice.10
  339.8 0.8 slice.11
  340.6 0.6 reshape.52
  341.2 0.6 fusion
  341.8 1.9 copy.30
  343.7 1.9 copy.31
  345.5 1.8 copy.32
  347.3 1.6 copy.33
  348.9 2.0 copy.34
  350.9 0.0 copy-done
  350.9 0.7 copy.35
  (1 shorter events, 0.0 us)
Async XLA Ops:
  339.1 11.8 %copy-start = (f32[704,128]{1,0:T(8,128)S(1)}, f32[704,128]{1,0:T(8,128)}, u32[]{:S(2)}) copy-start(f32[704,128]{1,0:T(8,128)} %get-tuple-element.82) | copy-start | bytes 1081348

commit v4 on v3

v4 whole, which is shorter than its diff:
```python
from functools import partial

import jax
import jax.numpy as jnp
from jax import lax
from jax.experimental import pallas as pl
from jax.experimental.pallas import tpu as pltpu
from jax.sharding import PartitionSpec as P

HEAD_DIM = 64
ROT = 16
DOCS = 4
EPS = 1e-05
SCALE = HEAD_DIM ** (-0.5)

ROWS = 128
WIDTH = 2048
TENSOR = 8
GROUP = ROWS * TENSOR
HALF = ROWS // 2
HEADS_DEV = 4
LOCAL = HEADS_DEV * HEAD_DIM
QBLOCK = 256
UNITS = 704
LANES = 128
MESH = pl.DeviceIdType.MESH
BF16 = jnp.bfloat16
F32 = jnp.float32
VMEM_LIMIT = 62 * 2**20


class Around:
    def __init__(self):
        dp, tensor = lax.axis_index("dp"), lax.axis_index("tensor")
        y, z = tensor // 2, lax.rem(tensor, 2)
        up, down, far = lax.rem(y + 1, 4), lax.rem(y + 3, 4), lax.rem(y + 2, 4)
        other = 1 - z
        self.me, self.across = y * 2 + z, y * 2 + other
        self.up, self.down, self.far = up * 2 + z, down * 2 + z, far * 2 + z
        self.up_o, self.down_o, self.far_o = up * 2 + other, down * 2 + other, far * 2 + other
        self.y, self.z = y, z
        self.y_up, self.y_down, self.y_far = up, down, far
        self.to_up, self.to_down, self.to_across = (dp, self.up), (dp, self.down), (dp, self.across)
        self.to_rest = [(dp, slot) for slot in (self.far, self.up_o, self.down_o, self.far_o)]

    def peers(self):
        return [self.to_up, self.to_down, self.to_across]


class Ring:
    def __init__(self):
        dp, tensor = lax.axis_index("dp"), lax.axis_index("tensor")
        zh, x, core = dp // 8, lax.rem(dp // 2, 4), lax.rem(dp, 2)
        self.zh, self.x, self.core, self.dp, self.tensor = zh, x, core, dp, tensor
        self.xs = [lax.rem(x + step, 4) for step in range(4)]
        self.to_x = [(self.index(zh, self.xs[step], core), tensor) for step in range(4)]
        self.to_zh = (self.index(1 - zh, x, core), tensor)
        self.to_core = (self.index(zh, x, 1 - core), tensor)
        self.to_zh_core = (self.index(1 - zh, x, 1 - core), tensor)

    def index(self, zh, x, core):
        return zh * 8 + x * 2 + core

    def peers(self):
        return self.to_x[1:] + [self.to_zh, self.to_core]


def hail(peers):
    barrier = pltpu.get_barrier_semaphore()
    for peer in peers:
        pl.semaphore_signal(barrier, inc=1, device_id=peer, device_id_type=MESH)


def hear(peers):
    pl.semaphore_wait(pltpu.get_barrier_semaphore(), len(peers))


class Mail:
    def __init__(self, sends, receives):
        self.sends, self.receives = sends, receives
        self.out = []

    def copy(self, number, source, target, device):
        return pltpu.make_async_remote_copy(
            src_ref=source,
            dst_ref=target,
            send_sem=self.sends.at[number],
            recv_sem=self.receives.at[number],
            device_id=device,
            device_id_type=MESH,
        )

    def send(self, number, source, target, device):
        copy = self.copy(number, source, target, device)
        copy.start()
        self.out.append(copy)

    def landed(self, number, target, device):
        self.copy(number, target, target, device).wait_recv()

    def finish(self):
        for copy in self.out:
            copy.wait_send()
        self.out = []


MIDDLE = {64: 96, 48: 96, 32: 80}
GATHER_MAILS = 17


class Gather:
    def __init__(self, around, mail, rows, top, own=None):
        a, middle = around, MIDDLE[top]
        self.mail, self.rows, self.own = mail, rows, own
        self.messages = [
            (a.to_up, a.me, 0, HALF, a.down),
            (a.to_down, a.me, HALF, ROWS, a.up),
            (a.to_across, a.me, top, ROWS, a.across),
            (a.to_up, a.me, HALF, ROWS, a.down),
            (a.to_down, a.me, 0, HALF, a.up),
            (a.to_across, a.me, 0, top, a.across),
            (a.to_up, a.down, 0, HALF, a.far),
            (a.to_across, a.down, 0, top, a.down_o),
            (a.to_down, a.up, HALF, ROWS, a.far),
            (a.to_up, a.across, top, middle, a.down_o),
            (a.to_down, a.across, middle, ROWS, a.up_o),
            (a.to_across, a.up, 0, top, a.up_o),
            (a.to_across, a.far, 0, top, a.far_o),
            (a.to_up, a.down_o, top, middle, a.far_o),
            (a.to_down, a.up_o, middle, ROWS, a.far_o),
            (a.to_up, a.across, middle, ROWS, a.down_o),
            (a.to_down, a.across, top, middle, a.up_o),
        ]

    def part(self, slot, first, last):
        return self.rows.at[slot, pl.ds(first, last - first)]

    def send(self, *numbers):
        for number in numbers:
            device, slot, first, last, _ = self.messages[number]
            target = source = self.part(slot, first, last)
            if number < 6 and self.own is not None:
                source = self.own.at[pl.ds(first, last - first)]
            self.mail.send(number, source, target, device)

    def step(self, number):
        return partial(self.on, number)

    def on(self, number):
        device, _, first, last, slot = self.messages[number]
        self.mail.landed(number, self.part(slot, first, last), device)
        followers = {0: (6, 7), 1: (8,), 2: (9, 10, 15, 16), 4: (11,), 6: (12,), 9: (13,), 10: (14,)}
        self.send(*followers.get(number, ()))


def added(*terms):
    total = terms[0].astype(F32)
    for term in terms[1:]:
        total = total + term.astype(F32)
    return total


SCATTER_MAILS = 21


def scatter_boxes(top):
    middle = MIDDLE[top]
    last, inner, rest = ROWS - middle, middle - top, HALF - top
    counts = (last, inner, top, HALF, top, top, last, inner, HALF, top)
    counts += (top, inner, last, HALF, top, top, inner, rest, rest, rest, last, inner, last)
    order = [*range(17), 20, 17, 18, 19, 21, 22]
    firsts = [0] * len(counts)
    for before, number in zip(order, order[1:]):
        firsts[number] = firsts[before] + counts[before]
    return counts, tuple(firsts)


def scatter_rows_needed(top):
    return sum(scatter_boxes(top)[0])


class Scatter:
    def __init__(self, around, mail, parts, land, top):
        self.a, self.mail, self.parts, self.land, self.top = around, mail, parts, land, top
        self.middle = MIDDLE[top]
        self.counts, self.firsts = scatter_boxes(top)

    def part(self, slot, first, last):
        return self.parts.at[slot, pl.ds(first, last - first)]

    def box(self, number):
        return self.land.at[pl.ds(self.firsts[number], self.counts[number])]

    def got(self, number):
        self.mail.landed(number, self.box(number), self.a.to_up)

    def fold(self, stage, slot, first, *others):
        terms = [self.part(slot, first, first + self.counts[stage])[...], self.box(stage)[...]]
        terms += [self.box(other)[...] for other in others]
        self.box(stage)[...] = added(*terms).astype(BF16)

    def direct(self, *numbers):
        a, top, middle = self.a, self.top, self.middle
        messages = {
            0: (a.far_o, middle, a.to_up),
            1: (a.far_o, top, a.to_down),
            2: (a.far_o, 0, a.to_across),
            3: (a.far, HALF, a.to_up),
            17: (a.far, top, a.to_down),
            4: (a.up_o, 0, a.to_across),
            7: (a.up_o, top, a.to_up),
            5: (a.down_o, 0, a.to_across),
            6: (a.down_o, middle, a.to_down),
            18: (a.up, top, a.to_up),
            8: (a.down, HALF, a.to_down),
            9: (a.across, 0, a.to_across),
        }
        for number in numbers:
            slot, first, device = messages[number]
            source = self.part(slot, first, first + self.counts[number])
            self.mail.send(number, source, self.box(number), device)

    def from_far_pair(self):
        self.direct(0, 1, 2, 3, 17)

    def from_up_pair(self):
        self.direct(7, 4, 18)

    def from_down_pair(self):
        self.direct(6, 5, 8)

    def from_across(self):
        self.direct(9)

    def direct_up(self):
        self.direct(0, 3, 7, 18)

    def direct_down(self):
        self.direct(1, 17, 6, 8)

    def direct_across(self):
        self.direct(2, 4, 5, 9)

    def step(self, number):
        return partial(self.on, number)

    def on(self, number):
        a, box = self.a, self.box
        follower, slot, first, device, *others = {
            1: (11, a.down_o, self.top, a.to_down),
            0: (12, a.up_o, self.middle, a.to_up),
            2: (10, a.far, 0, a.to_down),
            3: (13, a.up, HALF, a.to_up),
            17: (19, a.down, self.top, a.to_down),
            4: (14, a.up, 0, a.to_up),
            5: (15, a.down, 0, a.to_down, 10),
        }[number]
        for other in (number, *others):
            self.got(other)
        self.fold(number, slot, first, *others)
        self.mail.send(follower, box(number), box(follower), device)

    def over(self, number, made, first, *landed):
        for other in landed:
            self.got(other)
        own = self.part(self.a.across, first, first + self.counts[number])
        terms = [own[...]] + [self.box(other)[...] for other in landed]
        self.box(made)[...] = added(*terms).astype(BF16)
        self.mail.send(number, self.box(made), self.box(number), self.a.to_across)

    def over_inner(self):
        self.over(16, 21, self.top, 7, 11)

    def over_last(self):
        self.over(20, 22, self.middle, 6, 12)

    def all_direct(self):
        self.direct(0, 1, 2, 3, 17, 7, 4, 6, 5, 18, 8, 9)

    def finish(self, total):
        a, top = self.a, self.top
        for number in (8, 9, 13, 14, 18, 19, 16, 20, 15):
            self.got(number)

        def boxed(number, first, last):
            return self.land[pl.ds(self.firsts[number] + first, last - first), :]

        total[pl.ds(0, top), :] = added(
            self.part(a.me, 0, top)[...], *(self.box(k)[...] for k in (9, 14, 15))
        )
        total[pl.ds(top, HALF - top), :] = added(
            self.part(a.me, top, HALF)[...],
            self.box(18)[...],
            self.box(19)[...],
            boxed(16, 0, HALF - top),
        )
        total[pl.ds(HALF, HALF), :] = added(
            self.part(a.me, HALF, ROWS)[...],
            self.box(8)[...],
            self.box(13)[...],
            boxed(16, HALF - top, ROWS - top),
        )


class Spread:
    def __init__(self, ring, mail, block, own_shard=None):
        r = self.r = ring
        self.mail, self.block, self.own = mail, block, own_shard
        own, cross = (r.zh, r.x), (1 - r.zh, r.x)
        self.messages = [(r.to_zh, own, cross)]
        self.messages += [(r.to_x[k], own, (r.zh, r.xs[4 - k])) for k in (1, 2, 3)]
        self.messages += [(r.to_x[k], cross, (1 - r.zh, r.xs[4 - k])) for k in (1, 2, 3)]
        self.messages += [(r.to_core, own, own), (r.to_core, cross, cross)]
        self.messages += [(r.to_core, self.messages[k][2], self.messages[k][2]) for k in range(1, 7)]

    def send(self, number):
        device, place, _ = self.messages[number]
        block = self.block(*place, self.r.core)
        source = self.own if self.own is not None and number in (0, 1, 2, 3, 7) else block
        self.mail.send(number, source, block, device)

    def step(self, number):
        return partial(self.on, number)

    def begin(self):
        for number in (0, 1, 3, 2, 7):
            self.send(number)

    def on(self, number):
        device, _, place = self.messages[number]
        core = self.r.core if number < 7 else 1 - self.r.core
        self.mail.landed(number, self.block(*place, core), device)
        if number == 0:
            for follower in (4, 6, 5, 8):
                self.send(follower)
        elif number < 7:
            self.send(number + 8)

    def finish(self):
        for number in range(7, SPREAD_MAILS):
            self.on(number)


SPREAD_MAILS = 15
FOLDS = [(side, step) for step in (1, 3, 2, 0) for side in (1, 0)]


class Fold:
    def __init__(self, ring, mail, grads, own, land):
        self.r, self.mail, self.grads, self.own, self.land = ring, mail, grads, own, land

    def place(self, side, step):
        zh = 1 - self.r.zh if side else self.r.zh
        return zh * 4 + self.r.xs[step]

    def send(self, *numbers):
        for number in numbers:
            side, step = FOLDS[number]
            source = self.grads.at[self.place(side, step)]
            self.mail.send(number, source, self.land.at[number], self.r.to_x[step])

    def cross(self):
        for number in (0, 2, 4):
            self.mail.landed(number, self.land.at[number], self.r.to_core)
        self.land[0] = added(self.own(1), self.land[0], self.land[2], self.land[4]).astype(BF16)
        self.mail.send(6, self.land.at[0], self.land.at[6], self.r.to_zh)

    def near(self):
        for number in (1, 3, 5):
            self.mail.landed(number, self.land.at[number], self.r.to_core)

    def result(self):
        self.mail.landed(6, self.land.at[6], self.r.to_core)
        land = self.land
        return added(self.own(0), land[1], land[3], land[5], land[6])


FOLD_MAILS = 7

EARLY_ROWS, NORM_ROWS = 40, 32
SUM_BOXES, SUM_MAILS = 14, 13


class EverySum:
    def __init__(self, a, r, mail, boxes, rows, norms):
        self.norms, self.mail, self.boxes = norms, mail, boxes
        crossed = 1 - r.zh
        place = r.zh * 2 + r.core
        z_sources = [crossed * 2 + r.core, r.zh * 2 + 1 - r.core, crossed * 2 + 1 - r.core]
        z_peers = [r.to_zh, r.to_core, r.to_zh_core]
        y_peers = [a.to_up, a.to_rest[0], a.to_down]
        self.stages = [
            (0, rows, r.x, [r.xs[3], r.xs[2], r.xs[1]], r.to_x[1:]),
            (4, rows, place, z_sources, z_peers),
            (8, norms, a.y, [a.y_down, a.y_far, a.y_up], y_peers),
            (12, norms, a.z, [1 - a.z], [a.to_across]),
        ]

    def give(self, stage, values):
        base, count, mine, _, peers = self.stages[stage]
        view = pl.ds(0, count)
        self.boxes[base + mine, view] = values
        for number, peer in enumerate(peers):
            box = self.boxes.at[base + mine, view]
            self.mail.send(base + number, box, box, peer)

    def take(self, stage):
        base, count, _, sources, peers = self.stages[stage]
        view = pl.ds(0, count)
        for number, source in enumerate(sources):
            self.mail.landed(base + number, self.boxes.at[base + source, view], peers[0])
        result = self.boxes[base, view]
        for k in range(1, len(peers) + 1):
            result = result + self.boxes[base + k, view]
        return result

    def first(self, values):
        self.give(0, values)

    def second(self):
        self.give(1, self.take(0))

    def third(self):
        self.over_dp = self.take(1)
        self.give(2, self.over_dp[: self.norms])

    def fourth(self):
        self.give(3, self.take(2))

    def result(self):
        total = self.take(3)
        if self.norms == self.over_dp.shape[0]:
            return total
        return jnp.concatenate([total, self.over_dp[self.norms :]], axis=0)


def dot(left, right):
    return lax.dot_general(left, right, (((1,), (0,)), ((), ())), preferred_element_type=F32)


def dot_t(left, right):
    return lax.dot_general(left, right, (((1,), (1,)), ((), ())), preferred_element_type=F32)


def normalized(values):
    centred = values - jnp.mean(values, axis=1, keepdims=True)
    variance = jnp.mean(centred * centred, axis=1, keepdims=True)
    rinv = lax.rsqrt(variance + EPS)
    return centred * rinv, rinv


def norm_back(incoming, normal, rinv, gain):
    scaled = incoming * gain
    inner = scaled - jnp.mean(scaled, axis=1, keepdims=True)
    inner = inner - normal * jnp.mean(scaled * normal, axis=1, keepdims=True)
    gain_grad = jnp.sum(incoming * normal, axis=0, keepdims=True)
    return rinv * inner, gain_grad, jnp.sum(incoming, axis=0, keepdims=True)


def turned(values, tables, first, sign):
    rows = pl.ds(first, values.shape[0])
    cosine, minus, plus = tables[0, rows], tables[1, rows], tables[2, rows]
    halves = []
    for lane in range(0, LOCAL, LANES):
        part = values[:, lane : lane + LANES]
        left = pltpu.roll(part, LANES - ROT // 2, 1)
        right = pltpu.roll(part, ROT // 2, 1)
        halves.append(part * cosine + sign * (left * minus + right * plus))
    return jnp.concatenate(halves, axis=1)


def head_lanes(head, rows):
    return lax.broadcasted_iota(jnp.int32, (rows, LOCAL), 1) // HEAD_DIM == head


def only(mask, values):
    return jnp.where(mask, values, jnp.zeros_like(values))


def place_rows(id_rows, frequency, tables, start_rows, start_lanes):
    ids = jnp.max(id_rows[...], axis=1)
    shape = (TENSOR, ROWS)
    index = lax.broadcasted_iota(jnp.int32, shape, 0) * ROWS
    index = (index + lax.broadcasted_iota(jnp.int32, shape, 1)).astype(F32)
    offset = jnp.zeros(shape, F32)
    for number in range(1, DOCS):
        before = ((ids >= 0) & (ids < number)).astype(F32)
        count = jnp.sum(jnp.sum(before, axis=1, keepdims=True), axis=0, keepdims=True)
        offset = jnp.where(ids == number, count, offset)
    start = jnp.where(ids >= 0, offset, index)
    position = index - offset

    def along(values):
        return jnp.concatenate([values[t : t + 1] for t in range(TENSOR)], axis=1)

    angle = frequency[:, :1] * along(position)
    cosine, sine = jnp.cos(angle), jnp.sin(angle)
    none = jnp.zeros_like(sine)
    rest = (HEAD_DIM - ROT) // 8
    columns = (
        [cosine, cosine] + [jnp.ones_like(sine)] * rest,
        [-sine, none] + [none] * rest,
        [none, sine] + [none] * rest,
    )
    for number, parts in enumerate(columns):
        tables[number] = jnp.concatenate(parts + parts, axis=0).T
    lanes = jnp.broadcast_to(along(start), (8, GROUP))
    start_lanes[...] = lanes
    start_rows[...] = jnp.concatenate([lanes] * (LANES // 8), axis=0).T


def vmem(count):
    return [pl.BlockSpec(memory_space=pltpu.VMEM)] * count


def anywhere(count):
    return [pl.BlockSpec(memory_space=pl.ANY)] * count


def pairs(count):
    return [pltpu.SemaphoreType.DMA((count,)), pltpu.SemaphoreType.DMA((count,))]


def params(collective):
    return pltpu.CompilerParams(
        collective_id=collective, has_side_effects=True, vmem_limit_bytes=VMEM_LIMIT
    )


TOP_ROWS, TOP_COTS, TOP_BRANCH = 48, 32, 48


def attention_kernel(
    tokens,
    ids,
    bias,
    out_shard,
    gain1,
    shift1,
    gain2,
    shift2,
    frequency,
    qkv_shard,
    gate_up,
    down,
    own_cots,
    normed2,
    start_lanes,
    logs,
    mixed_kept,
    tables_kept,
    acts_kept,
    attended_kept,
    rows_kept,
    weights_kept,
    cots,
    feed,
    rows,
    weights,
    feed_own,
    cots_own,
    tables,
    acts,
    attended,
    mixed,
    id_rows,
    start_rows,
    parts,
    land,
    total,
    r_sends,
    r_receives,
    c_sends,
    c_receives,
    b_sends,
    b_receives,
    w_sends,
    w_receives,
    f_sends,
    f_receives,
    i_sends,
    i_receives,
    local,
):
    a, r = Around(), Ring()
    rmail, cmail, bmail = Mail(r_sends, r_receives), Mail(c_sends, c_receives), Mail(b_sends, b_receives)
    wmail, fmail, imail = Mail(w_sends, w_receives), Mail(f_sends, f_receives), Mail(i_sends, i_receives)
    peers = a.peers() + a.to_rest + r.peers()
    hail(peers)

    def weight_block(zh, x, core):
        first = pl.multiple_of(r.index(zh, x, core) * ROWS, ROWS)
        return weights.at[:, pl.ds(first, ROWS), :]

    mine = pl.multiple_of(r.dp * ROWS, ROWS)
    loads = [
        pltpu.make_async_copy(qkv_shard, weights.at[pl.ds(0, 3), pl.ds(mine, ROWS)], local.at[0]),
        pltpu.make_async_copy(gate_up, feed_own.at[pl.ds(0, 2 * UNITS)], local.at[1]),
        pltpu.make_async_copy(down, feed_own.at[pl.ds(2 * UNITS, UNITS)], local.at[2]),
        pltpu.make_async_copy(own_cots, cots_own, local.at[3]),
    ]
    for copy in loads:
        copy.start()
    id_rows[a.me] = jnp.broadcast_to(ids[...], (8, ROWS))
    weights[3, pl.ds(mine, ROWS), :] = out_shard[...].T
    normal, _ = normalized(tokens[...].astype(F32))
    rows[a.me] = (normal * gain1[...] + shift1[...]).astype(BF16)
    hear(peers)

    group = [
        (0, a.to_up, a.down),
        (1, a.to_down, a.up),
        (2, a.to_across, a.across),
        (3, a.to_rest[0], a.far),
        (4, a.to_rest[1], a.down_o),
        (5, a.to_rest[2], a.up_o),
        (6, a.to_rest[3], a.far_o),
    ]
    gather = Gather(a, rmail, rows, TOP_ROWS)
    others = Gather(a, cmail, cots, TOP_COTS, cots_own)
    spread = Spread(r, wmail, weight_block)
    feeds = Spread(r, fmail, lambda zh, x, core: feed.at[r.index(zh, x, core)], feed_own)
    scatter = Scatter(a, bmail, parts, land, TOP_BRANCH)
    started = []

    def keep(source, target, number):
        copy = pltpu.make_async_copy(source, target, local.at[number])
        copy.start()
        started.append(copy)

    def begin():
        for number, device, _ in group:
            imail.send(number, id_rows.at[a.me], id_rows.at[a.me], device)
        for number in (0, 1, 2):
            gather.send(number)
        loads[0].wait()
        spread.begin()
        for number in (3, 4, 5):
            gather.send(number)
        for copy in loads[1:]:
            copy.wait()
        keep(feed_own, feed.at[r.dp], 4)
        keep(cots_own, cots.at[a.me], 5)

    def place():
        for number, _, slot in group:
            imail.landed(number, id_rows.at[slot], a.to_up)
        place_rows(id_rows, frequency, tables, start_rows, start_lanes)
        keep(tables, tables_kept, 6)

    def P(y):
        return partial(project, y)

    def project(y):
        first = pl.multiple_of(y * QBLOCK, QBLOCK)
        chunk = rows[pl.ds(2 * y, 2)].reshape(QBLOCK, WIDTH)
        for c in range(3):
            pre = dot(chunk, weights[c]) + bias[pl.ds(c, 1), :]
            if c < 2:
                pre = turned(pre, tables, first, 1.0)
            acts[c, pl.ds(first, QBLOCK), :] = pre.astype(BF16)

    state = {}

    def A(q, *heads):
        return partial(attend, q * QBLOCK, heads)

    def attend(first, heads):
        count = first + QBLOCK
        query = acts[0, pl.ds(first, QBLOCK), :] * BF16(SCALE)
        row = first + lax.broadcasted_iota(jnp.int32, (QBLOCK, count), 0)
        column = lax.broadcasted_iota(jnp.int32, (QBLOCK, count), 1)
        start = start_rows[pl.ds(first, QBLOCK), pl.ds(0, 1)]
        allow = (column <= row) & (column.astype(F32) >= start)
        lane = lax.broadcasted_iota(jnp.int32, (QBLOCK, LANES), 1)

        def one_head(head, carry):
            out, log = carry
            masked = only(head_lanes(head, QBLOCK), query)
            scores = dot_t(masked, acts[1, pl.ds(0, count), :])
            scores = jnp.where(allow, scores, -1e30)
            highest = jnp.max(scores, axis=1, keepdims=True)
            expon = jnp.exp(scores - highest)
            sums = jnp.sum(expon, axis=1, keepdims=True)
            values = only(head_lanes(head, count), acts[2, pl.ds(0, count), :])
            out = out + dot(expon.astype(BF16), values) / sums
            log = jnp.where(lane == head, highest + jnp.log(sums), log)
            return out, log

        zeros = (jnp.zeros((QBLOCK, LOCAL), F32), jnp.zeros((QBLOCK, LANES), F32))
        carry = lax.fori_loop(*heads, one_head, state.pop("attend", zeros))
        if heads[1] < HEADS_DEV:
            state["attend"] = carry
            return
        out = carry[0].astype(BF16)
        attended[pl.ds(first, QBLOCK), :] = out
        logs[:, pl.ds(first, QBLOCK)] = carry[1].T[:8]
        branch = dot_t(out, weights[3]).astype(BF16)
        parts[first // ROWS] = branch[:ROWS]
        parts[first // ROWS + 1] = branch[ROWS:]

    def branch_sums():
        keep(rows, rows_kept, 7)
        keep(weights, weights_kept, 8)
        keep(acts, acts_kept, 9)
        keep(attended, attended_kept, 10)
        scatter.all_direct()

    def second_norm():
        scatter.finish(total)
        after = tokens[...].astype(F32) + total[...]
        mixed[...] = after
        keep(mixed, mixed_kept, 11)
        normal, _ = normalized(after)
        normed2[...] = (normal * gain2[...] + shift2[...]).astype(BF16)

    R, C, B, w, f = gather.step, others.step, scatter.step, spread.step, feeds.step
    C_up, C_down, C_across = (partial(others.send, *two) for two in ((0, 3), (1, 4), (2, 5)))
    for step in (
        begin, place, R(0), R(1), w(1), w(3), R(2), R(3), R(4), w(2), w(0), R(6), R(8), C_across,
        R(5), feeds.begin, R(10), C_down, w(4), w(6), R(9), C_up, R(7), R(15), R(16), R(11), R(14),
        w(5), R(13), R(12), spread.finish, P(a.y_down), P(a.y_far), C(1), P(a.y), P(a.y_up),
        A(0, 0, 4), A(1, 0, 2), C(4), C(2), f(1), f(3), A(1, 2, 4), A(2, 0, 1), A(2, 1, 2), C(5),
        A(2, 2, 3), A(2, 3, 4), C(9), A(3, 0, 1), A(3, 1, 2), A(3, 2, 3), C(10), C(15), A(3, 3, 4),
        branch_sums, f(2), C(3), C(8), C(0), C(16), C(13), f(0), C(11), B(0), C(14), B(2), B(1),
        B(3), B(17), B(4), f(4), f(6), C(6), B(5), C(7), scatter.over_last, C(12),
        scatter.over_inner, f(5), feeds.finish, second_norm,
    ):
        step()
    for mail in (rmail, cmail, bmail, wmail, fmail, imail):
        mail.finish()
    for copy in started:
        copy.wait()


def attention_forward(tokens, ids, bias, out_shard, norms, frequency, qkv_shard, gate_up, down, cots):
    group = (TENSOR, ROWS, WIDTH)
    weights = (4, WIDTH, LOCAL)
    tables, acts = (3, GROUP, LANES), (3, GROUP, LOCAL)
    return pl.pallas_call(
        attention_kernel,
        out_shape=(
            jax.ShapeDtypeStruct((ROWS, WIDTH), BF16),
            jax.ShapeDtypeStruct((8, GROUP), F32),
            jax.ShapeDtypeStruct((8, GROUP), F32),
            jax.ShapeDtypeStruct((ROWS, WIDTH), F32),
            jax.ShapeDtypeStruct(tables, F32),
            jax.ShapeDtypeStruct(acts, BF16),
            jax.ShapeDtypeStruct((GROUP, LOCAL), BF16),
            jax.ShapeDtypeStruct(group, BF16),
            jax.ShapeDtypeStruct(weights, BF16),
            jax.ShapeDtypeStruct(group, BF16),
            jax.ShapeDtypeStruct((16, 3 * UNITS, ROWS), BF16),
        ),
        in_specs=vmem(9) + anywhere(4),
        out_specs=tuple(vmem(3) + anywhere(8)),
        scratch_shapes=[
            pltpu.VMEM(group, BF16),
            pltpu.VMEM(weights, BF16),
            pltpu.VMEM((3 * UNITS, ROWS), BF16),
            pltpu.VMEM((ROWS, WIDTH), BF16),
            pltpu.VMEM(tables, F32),
            pltpu.VMEM(acts, BF16),
            pltpu.VMEM((GROUP, LOCAL), BF16),
            pltpu.VMEM((ROWS, WIDTH), F32),
            pltpu.VMEM((TENSOR, 8, ROWS), jnp.int32),
            pltpu.VMEM((GROUP, LANES), F32),
            pltpu.VMEM(group, BF16),
            pltpu.VMEM((scatter_rows_needed(TOP_BRANCH), WIDTH), BF16),
            pltpu.VMEM((ROWS, WIDTH), F32),
            *pairs(GATHER_MAILS),
            *pairs(GATHER_MAILS),
            *pairs(SCATTER_MAILS),
            *pairs(SPREAD_MAILS),
            *pairs(SPREAD_MAILS),
            *pairs(7),
            pltpu.SemaphoreType.DMA((12,)),
        ],
        compiler_params=params(0),
        name="attention_forward",
    )(tokens, ids, bias, out_shard, *norms, frequency, qkv_shard, gate_up, down, cots)


TOP_FEED, TOP_FEED_BACK = 64, 48

def feed_kernel(
    gain2,
    own,
    mixed_in,
    cots_own,
    cots_in,
    feed,
    grad_mixed,
    branch_grad,
    norm_grads,
    halves,
    outs_kept,
    rows,
    cots,
    weights,
    parts,
    outs,
    acts,
    grads,
    land,
    core_land,
    mixed,
    own_cots,
    total,
    g_sends,
    g_receives,
    s_sends,
    s_receives,
    w_sends,
    w_receives,
    w_local,
    local,
):
    a, r = Around(), Ring()
    gmail, mail, wmail = Mail(g_sends, g_receives), Mail(s_sends, s_receives), Mail(w_sends, w_receives)
    peers = a.peers() + [r.to_core]
    hail(peers)
    first_load = pltpu.make_async_copy(own, rows.at[a.me], local.at[0])
    loads = [
        pltpu.make_async_copy(feed.at[n], weights.at[:, pl.ds(n * ROWS, ROWS)], w_local.at[n])
        for n in range(16)
    ]
    loads.append(pltpu.make_async_copy(cots_in, cots, local.at[1]))
    late_loads = [
        pltpu.make_async_copy(mixed_in, mixed, local.at[2]),
        pltpu.make_async_copy(cots_own, own_cots, local.at[3]),
    ]
    for copy in [first_load] + loads + late_loads:
        copy.start()
    first_load.wait()
    hear(peers)
    gather = Gather(a, gmail, rows, TOP_FEED)
    scatter = Scatter(a, mail, parts, land, TOP_FEED_BACK)
    started = []

    def keep(source, target, number):
        copy = pltpu.make_async_copy(source, target, local.at[number])
        copy.start()
        started.append(copy)

    def load():
        for copy in loads:
            copy.wait()

    state = {}

    def pair(index, *slots):
        x = jnp.concatenate([rows[slot] for slot in slots], axis=0)
        given = jnp.concatenate([cots[slot] for slot in slots], axis=0)
        gate = dot_t(x, weights[pl.ds(0, UNITS), :])
        upward = dot_t(x, weights[pl.ds(UNITS, UNITS), :])
        grad_hidden = dot_t(given, weights[pl.ds(2 * UNITS, UNITS), :])
        sigma = jax.nn.sigmoid(gate)
        silu = gate * sigma
        hidden = (silu * upward).astype(BF16)
        grad_gate = (grad_hidden * upward * (sigma + silu * (1.0 - sigma))).astype(BF16)
        grad_up = (grad_hidden * silu).astype(BF16)
        state[index] = hidden, grad_gate, grad_up

    def pair_back(index, *slots):
        _, grad_gate, grad_up = state[index]
        back = dot(grad_gate, weights[pl.ds(0, UNITS), :])
        back = (back + dot(grad_up, weights[pl.ds(UNITS, UNITS), :])).astype(BF16)
        for number, slot in enumerate(slots):
            parts[slot] = back[number * ROWS : (number + 1) * ROWS]

    def rest(index, *slots):
        hidden, grad_gate, grad_up = state[index]
        out = dot(hidden, weights[pl.ds(2 * UNITS, UNITS), :]).astype(BF16)
        for number, slot in enumerate(slots):
            chunk = slice(number * ROWS, (number + 1) * ROWS)
            outs[slot] = out[chunk]
            lanes = pl.ds(pl.multiple_of(slot * ROWS, ROWS), ROWS)
            acts[pl.ds(0, UNITS), lanes] = grad_gate[chunk].T
            acts[pl.ds(UNITS, UNITS), lanes] = grad_up[chunk].T
            acts[pl.ds(2 * UNITS, UNITS), lanes] = hidden[chunk].T

    def to_sibling(index):
        return wmail.copy(index, grads.at[index, 1 - r.core], core_land.at[index], r.to_core)

    def weight_grad(index, carry):
        columns = pl.ds(pl.multiple_of(index * 2 * ROWS, 2 * ROWS), 2 * ROWS)
        both = dot(acts[pl.ds(0, 2 * UNITS), :], rows[:, :, columns].reshape(GROUP, 2 * ROWS))
        low = dot(acts[pl.ds(2 * UNITS, UNITS), :], cots[:, :, columns].reshape(GROUP, 2 * ROWS))
        for core in range(2):
            lanes = slice(core * ROWS, (core + 1) * ROWS)
            grads[index, core, pl.ds(0, 2 * UNITS), :] = both[:, lanes].astype(BF16)
            grads[index, core, pl.ds(2 * UNITS, UNITS), :] = low[:, lanes].astype(BF16)
        to_sibling(index).start()
        return carry

    def core_sum(index, carry):
        to_sibling(index).wait()
        core_land[index] = added(grads[index, r.core], core_land[index]).astype(BF16)
        return carry

    def core_sums(first, last):
        lax.fori_loop(first, last, core_sum, 0)
        keep(core_land.at[pl.ds(first, last - first)], halves.at[pl.ds(first, last - first)], 4 + first // 4)

    def keep_outs():
        keep(outs, outs_kept, 6)

    def norm():
        for copy in late_loads:
            copy.wait()
        scatter.finish(total)
        normal, rinv = normalized(mixed[...])
        back, gain_grad, shift_grad = norm_back(total[...], normal, rinv, gain2[...])
        back = own_cots[...].astype(F32) + back
        grad_mixed[...] = back
        branch_grad[...] = back.astype(BF16)
        norm_grads[...] = jnp.concatenate([gain_grad, shift_grad], axis=0)

    couples = [(a.me, a.across), (a.down, a.up), (a.far, a.down_o), (a.far_o, a.up_o)]
    directs = [(9,), (18, 8), (3, 17, 6, 5), (0, 1, 2, 7, 4)]
    G, S = gather.step, scatter.step

    def P(index):
        return partial(pair, index, *couples[index])

    def Q(index):
        return partial(pair_back, index, *couples[index])

    def T(index):
        return partial(rest, index, *couples[index])

    def D(index):
        return partial(scatter.direct, *directs[index])

    def W(index):
        return partial(lax.fori_loop, 2 * index, 2 * index + 2, weight_grad, 0)

    def K(index):
        return partial(core_sums, 4 * index, 4 * index + 4)

    for step in (
        partial(gather.send, *range(6)), load, G(0), G(2), G(1), G(3), G(4), P(1), T(1), G(10),
        Q(1), D(1), G(5), P(0), G(16), G(6), G(7), Q(0), D(0), T(0), G(9), G(15), G(8), P(2), T(2),
        G(14), Q(2), D(2), G(13), G(11), G(12), P(3), Q(3), D(3), T(3), S(17), keep_outs, W(0),
        S(3), W(1), S(0), W(2), S(1), W(3), S(2), K(0), S(4), scatter.over_inner, K(1),
        scatter.over_last, S(5), norm,
    ):
        step()
    gmail.finish()
    mail.finish()
    for copy in started:
        copy.wait()


def feed_forward(gain2, own, mixed, own_cots, cots, feed):
    group = (TENSOR, ROWS, WIDTH)
    blocks = (8, 3 * UNITS, ROWS)
    return pl.pallas_call(
        feed_kernel,
        out_shape=(
            jax.ShapeDtypeStruct((ROWS, WIDTH), F32),
            jax.ShapeDtypeStruct((ROWS, WIDTH), BF16),
            jax.ShapeDtypeStruct((2, WIDTH), F32),
            jax.ShapeDtypeStruct(blocks, BF16),
            jax.ShapeDtypeStruct(group, BF16),
        ),
        in_specs=vmem(1) + anywhere(5),
        out_specs=tuple(vmem(3) + anywhere(2)),
        scratch_shapes=[
            pltpu.VMEM(group, BF16),
            pltpu.VMEM(group, BF16),
            pltpu.VMEM((3 * UNITS, WIDTH), BF16),
            pltpu.VMEM(group, BF16),
            pltpu.VMEM(group, BF16),
            pltpu.VMEM((3 * UNITS, GROUP), BF16),
            pltpu.VMEM((8, 2, 3 * UNITS, ROWS), BF16),
            pltpu.VMEM((scatter_rows_needed(TOP_FEED_BACK), WIDTH), BF16),
            pltpu.VMEM(blocks, BF16),
            pltpu.VMEM((ROWS, WIDTH), F32),
            pltpu.VMEM((ROWS, WIDTH), BF16),
            pltpu.VMEM((ROWS, WIDTH), F32),
            *pairs(GATHER_MAILS),
            *pairs(SCATTER_MAILS),
            *pairs(8),
            pltpu.SemaphoreType.DMA((16,)),
            pltpu.SemaphoreType.DMA((7,)),
        ],
        compiler_params=params(1),
        name="feed_forward",
    )(gain2, own, mixed, own_cots, cots, feed)


TOP_GRADS, TOP_OUTS, TOP_BACK = 48, 32, 48

def attention_back_kernel(
    gain1,
    norm2_grads,
    own,
    grad_mixed_in,
    mixed_in,
    tokens_in,
    tables_in,
    start_in,
    acts_in,
    attended_in,
    logs_in,
    weights_in,
    halves,
    first_rows,
    outs,
    layer_out,
    token_grad,
    qkv_grad,
    out_grad,
    gate_up_grad,
    down_grad,
    early_out,
    late_out,
    grad_mixed,
    mixed,
    tokens,
    tables,
    start_lanes,
    acts,
    attended,
    logs,
    weights,
    rows,
    before,
    grad_out,
    grads_qkv,
    keys_turned,
    turns,
    parts,
    out_parts,
    grads,
    land,
    out_land,
    core_land,
    w_land,
    f_land,
    own_halves,
    total,
    boxes,
    late_boxes,
    g_sends,
    g_receives,
    s_sends,
    s_receives,
    o_sends,
    o_receives,
    k_sends,
    k_receives,
    w_sends,
    w_receives,
    f_sends,
    f_receives,
    a_sends,
    a_receives,
    l_sends,
    l_receives,
    local,
):
    a, r = Around(), Ring()
    gmail, mail, omail = Mail(g_sends, g_receives), Mail(s_sends, s_receives), Mail(o_sends, o_receives)
    kmail, wmail, fmail = Mail(k_sends, k_receives), Mail(w_sends, w_receives), Mail(f_sends, f_receives)
    amail, lmail = Mail(a_sends, a_receives), Mail(l_sends, l_receives)
    peers = a.peers() + a.to_rest[:1] + r.peers() + [r.to_zh_core]
    hail(peers)
    loads = {}
    for number, (name, source, target) in enumerate(
        (
            ("own", own, rows.at[a.me]),
            ("acts", acts_in, acts),
            ("attended", attended_in, attended),
            ("outs", outs, out_parts),
            ("weights", weights_in, weights),
            ("logs", logs_in, logs),
            ("start", start_in, start_lanes),
            ("half", halves.at[r.zh * 4 + r.x], own_halves.at[0]),
            ("other", halves.at[(1 - r.zh) * 4 + r.x], own_halves.at[1]),
            ("tables", tables_in, tables),
            ("before", first_rows, before),
            ("mixed", mixed_in, mixed),
            ("tokens", tokens_in, tokens),
            ("grad_mixed", grad_mixed_in, grad_mixed),
        )
    ):
        loads[name] = pltpu.make_async_copy(source, target, local.at[number])
        loads[name].start()

    def loaded(*names):
        for name in names:
            loads.pop(name).wait()

    loaded("own")
    hear(peers)
    gather = Gather(a, gmail, rows, TOP_GRADS)
    out_scatter = Scatter(a, omail, out_parts, out_land, TOP_OUTS)
    scatter = Scatter(a, mail, parts, land, TOP_BACK)
    early = EverySum(a, r, amail, boxes, EARLY_ROWS, NORM_ROWS)
    late = EverySum(a, r, lmail, late_boxes, NORM_ROWS, NORM_ROWS)
    feed_fold = Fold(r, fmail, halves, lambda side: own_halves[side], f_land)
    fold = Fold(r, wmail, core_land, lambda side: core_land[fold.place(side, 0)], w_land)

    def turn():
        loaded("acts", "attended")
        keys_turned[...] = acts[1].T
        turns[pl.ds(3 * LOCAL, LOCAL), :] = attended[...].T
        grads_qkv[1] = jnp.zeros((GROUP, LOCAL), F32)
        grads_qkv[2] = jnp.zeros((GROUP, LOCAL), F32)
        loaded("outs", "weights", "logs", "start")

    def back_project(y):
        chunk = rows[pl.ds(2 * y, 2)].reshape(QBLOCK, WIDTH)
        first = pl.multiple_of(y * QBLOCK, QBLOCK)
        grad_out[pl.ds(first, QBLOCK), :] = dot(chunk, weights[3]).astype(BF16)

    state = {}

    def attend(first, heads):
        count = first + QBLOCK
        span = pl.ds(first, QBLOCK)
        query = acts[0, span, :] * BF16(SCALE)
        given = grad_out[span, :]
        row = lax.broadcasted_iota(jnp.int32, (count, QBLOCK), 0)
        column = first + lax.broadcasted_iota(jnp.int32, (count, QBLOCK), 1)
        allow = (row <= column) & (row.astype(F32) >= start_lanes[pl.ds(0, 1), span])
        overlap = given.astype(F32) * attended[span, :].astype(F32)
        lane = lax.broadcasted_iota(jnp.int32, (QBLOCK, LANES), 1)
        inner = jnp.zeros((QBLOCK, LANES), F32)
        for head in range(*heads):
            summed = jnp.sum(only(head_lanes(head, QBLOCK), overlap), axis=1, keepdims=True)
            inner = jnp.where(lane == head, summed, inner)
        inner = inner.T[:8]
        head_row = lax.broadcasted_iota(jnp.int32, (8, QBLOCK), 0)
        head_rows = lax.broadcasted_iota(jnp.int32, (LOCAL, count), 0) // HEAD_DIM

        def one_head(head, turned_query):
            mask = head_lanes(head, QBLOCK)
            masked, masked_given = only(mask, query), only(mask, given)
            log = jnp.sum(only(head_row == head, logs[:, span]), axis=0, keepdims=True)
            mean = jnp.sum(only(head_row == head, inner), axis=0, keepdims=True)
            scores = dot_t(acts[1, pl.ds(0, count), :], masked)
            probs = only(allow, jnp.exp(scores - log))
            grad_probs = dot_t(acts[2, pl.ds(0, count), :], masked_given)
            grad_scores = (probs * (grad_probs - mean)).astype(BF16)
            grads_qkv[2, pl.ds(0, count), :] += dot(probs.astype(BF16), masked_given)
            grads_qkv[1, pl.ds(0, count), :] += dot(grad_scores, masked)
            keys = only(head_rows == head, keys_turned[:, pl.ds(0, count)])
            return turned_query + dot(keys, grad_scores)

        so_far = state.pop("attend", jnp.zeros((LOCAL, QBLOCK), F32))
        so_far = lax.fori_loop(*heads, one_head, so_far)
        if heads[1] < HEADS_DEV:
            state["attend"] = so_far
        else:
            grads_qkv[0, span, :] = so_far.T * SCALE

    def input_grad(y):
        if "tables" in loads:
            loaded("tables")
        first = pl.multiple_of(y * QBLOCK, QBLOCK)
        span = pl.ds(first, QBLOCK)
        back = jnp.zeros((QBLOCK, WIDTH), F32)
        new = []
        for c in range(3):
            pre = grads_qkv[c, span, :]
            if c < 2:
                pre = turned(pre, tables, first, -1.0)
            pre = pre.astype(BF16)
            new.append(jnp.sum(pre.astype(F32), axis=0, keepdims=True))
            back = back + dot_t(pre, weights[c])
            turns[pl.ds(c * LOCAL, LOCAL), span] = pre.T
        parts[pl.ds(2 * y, 2)] = back.astype(BF16).reshape(2, ROWS, WIDTH)
        state["bias"] = state.get("bias", 0.0) + jnp.concatenate(new, axis=0)

    def to_sibling(index):
        return kmail.copy(index, grads.at[index, 1 - r.core], core_land.at[index], r.to_core)

    def weight_grad(index, carry):
        columns = pl.ds(pl.multiple_of(index * 2 * ROWS, 2 * ROWS), 2 * ROWS)
        three = dot(
            turns[pl.ds(0, 3 * LOCAL), :], before[:, :, columns].reshape(GROUP, 2 * ROWS)
        )
        last = dot(turns[pl.ds(3 * LOCAL, LOCAL), :], rows[:, :, columns].reshape(GROUP, 2 * ROWS))
        for core in range(2):
            lanes = slice(core * ROWS, (core + 1) * ROWS)
            grads[index, core, pl.ds(0, 3 * LOCAL), :] = three[:, lanes].astype(BF16)
            grads[index, core, pl.ds(3 * LOCAL, LOCAL), :] = last[:, lanes].astype(BF16)
        to_sibling(index).start()
        return carry

    def weight_grads(first):
        if "before" in loads:
            loaded("before")
        lax.fori_loop(first, first + 2, weight_grad, 0)

    def core_sum(index, carry):
        to_sibling(index).wait()
        core_land[index] = added(grads[index, r.core], core_land[index]).astype(BF16)
        return carry

    def feed_cross():
        loaded("other")
        feed_fold.cross()

    def feed_result():
        loaded("half")
        feed_fold.near()
        feed_sum = feed_fold.result()
        gate_up_grad[...] = feed_sum[: 2 * UNITS]
        down_grad[...] = feed_sum[2 * UNITS :]

    def weight_result():
        fold.near()
        shard = fold.result()
        for c in range(3):
            qkv_grad[c] = shard[c * LOCAL : (c + 1) * LOCAL].T
        out_grad[...] = shard[3 * LOCAL :]

    def layer_result():
        loaded("mixed")
        out_scatter.finish(total)
        layer_out[...] = (mixed[...] + total[...]).astype(BF16)

    def norm():
        loaded("tokens", "grad_mixed")
        scatter.finish(total)
        normal, rinv = normalized(tokens[...].astype(F32))
        back, gain_grad, shift_grad = norm_back(total[...], normal, rinv, gain1[...])
        late.first(by_lanes(gain_grad, shift_grad))
        token_grad[...] = (grad_mixed[...] + back).astype(BF16)

    def by_lanes(*values):
        values = jnp.concatenate(values, axis=0)
        width = values.shape[1]
        return jnp.concatenate([values[:, k : k + LANES] for k in range(0, width, LANES)], axis=0)

    def early_sums():
        spare = jnp.zeros((EARLY_ROWS - NORM_ROWS - 3 * LOCAL // LANES, LANES), F32)
        parts_now = [by_lanes(norm2_grads[...]), by_lanes(state["bias"]), spare]
        early.first(jnp.concatenate(parts_now, axis=0))

    def early_result():
        early_out[...] = early.result()

    def late_result():
        late_out[...] = late.result()

    G, O, S = gather.step, out_scatter.step, scatter.step

    def P(y):
        return partial(back_project, y)

    def A(q, *heads):
        return partial(attend, q * QBLOCK, heads)

    def I(y):
        return partial(input_grad, y)

    def W(index):
        return partial(weight_grads, 2 * index)

    def K(index):
        return partial(lax.fori_loop, 4 * index, 4 * index + 4, core_sum, 0)

    for step in (
        partial(gather.send, *range(6)), partial(feed_fold.send, *range(6)), turn, G(0), G(1), G(2),
        G(3), G(4), G(5), P(a.y), G(7), G(6), out_scatter.direct_across, G(8), G(10), G(11),
        out_scatter.direct_down, G(9), out_scatter.direct_up, G(15), G(16), G(12), P(a.y_down),
        P(a.y_up), G(14), O(2), G(13), P(a.y_far), A(0, 0, 4), A(1, 0, 2), A(1, 2, 4), O(0),
        A(2, 0, 1), O(17), A(2, 1, 2), A(2, 2, 3), feed_cross, O(4), A(2, 3, 4), O(3), A(3, 0, 1),
        A(3, 1, 2), A(3, 2, 3), A(3, 3, 4), I(a.y_far), scatter.from_far_pair, I(a.y_up),
        scatter.from_up_pair, I(a.y_down), scatter.from_down_pair, I(a.y), O(5),
        scatter.from_across, W(0), out_scatter.over_last, W(1), W(2), S(1), W(3), S(17), S(2), K(0),
        feed_result, O(1), K(1), S(4), partial(fold.send, *range(6)), early_sums, S(0), S(3),
        scatter.over_inner, S(5), scatter.over_last, fold.cross, out_scatter.over_inner, norm,
        early.second, weight_result, late.second, layer_result, early.third, late.third,
        early.fourth, late.fourth, early_result, late_result,
    ):
        step()
    for some in (gmail, mail, omail, kmail, wmail, fmail, amail, lmail):
        some.finish()


def attention_backward(*operands):
    group = (TENSOR, ROWS, WIDTH)
    block, feed_block = (4 * LOCAL, ROWS), (3 * UNITS, ROWS)
    return pl.pallas_call(
        attention_back_kernel,
        out_shape=(
            jax.ShapeDtypeStruct((ROWS, WIDTH), BF16),
            jax.ShapeDtypeStruct((ROWS, WIDTH), BF16),
            jax.ShapeDtypeStruct((3, ROWS, LOCAL), F32),
            jax.ShapeDtypeStruct((LOCAL, ROWS), F32),
            jax.ShapeDtypeStruct((2 * UNITS, ROWS), F32),
            jax.ShapeDtypeStruct((UNITS, ROWS), F32),
            jax.ShapeDtypeStruct((EARLY_ROWS, LANES), F32),
            jax.ShapeDtypeStruct((NORM_ROWS, LANES), F32),
        ),
        in_specs=vmem(2) + anywhere(13),
        out_specs=tuple(vmem(8)),
        scratch_shapes=[
            pltpu.VMEM((ROWS, WIDTH), F32),
            pltpu.VMEM((ROWS, WIDTH), F32),
            pltpu.VMEM((ROWS, WIDTH), BF16),
            pltpu.VMEM((3, GROUP, LANES), F32),
            pltpu.VMEM((8, GROUP), F32),
            pltpu.VMEM((3, GROUP, LOCAL), BF16),
            pltpu.VMEM((GROUP, LOCAL), BF16),
            pltpu.VMEM((8, GROUP), F32),
            pltpu.VMEM((4, WIDTH, LOCAL), BF16),
            pltpu.VMEM(group, BF16),
            pltpu.VMEM(group, BF16),
            pltpu.VMEM((GROUP, LOCAL), BF16),
            pltpu.VMEM((3, GROUP, LOCAL), F32),
            pltpu.VMEM((LOCAL, GROUP), BF16),
            pltpu.VMEM((4 * LOCAL, GROUP), BF16),
            pltpu.VMEM(group, BF16),
            pltpu.VMEM(group, BF16),
            pltpu.VMEM((8, 2) + block, BF16),
            pltpu.VMEM((scatter_rows_needed(TOP_BACK), WIDTH), BF16),
            pltpu.VMEM((scatter_rows_needed(TOP_OUTS), WIDTH), BF16),
            pltpu.VMEM((8,) + block, BF16),
            pltpu.VMEM((FOLD_MAILS,) + block, BF16),
            pltpu.VMEM((FOLD_MAILS,) + feed_block, BF16),
            pltpu.VMEM((2,) + feed_block, BF16),
            pltpu.VMEM((ROWS, WIDTH), F32),
            pltpu.VMEM((SUM_BOXES, EARLY_ROWS, LANES), F32),
            pltpu.VMEM((SUM_BOXES, NORM_ROWS, LANES), F32),
            *pairs(GATHER_MAILS),
            *pairs(SCATTER_MAILS),
            *pairs(SCATTER_MAILS),
            *pairs(8),
            *pairs(FOLD_MAILS),
            *pairs(FOLD_MAILS),
            *pairs(SUM_MAILS),
            *pairs(SUM_MAILS),
            pltpu.SemaphoreType.DMA((14,)),
        ],
        compiler_params=params(2),
        name="attention_backward",
    )(*operands)


def results_kernel(
    layer_in, token_in, qkv_in, out_in, gate_up_in, down_in, early, late, layer, token, qkv, out, gate_up, down, *norms
):
    bias = norms[4]
    for source, target in (
        (layer_in, layer),
        (token_in, token),
        (qkv_in, qkv),
        (out_in, out),
        (gate_up_in, gate_up),
        (down_in, down),
    ):
        target[...] = source[...]
    for k in range(WIDTH // LANES):
        for number in range(2):
            norms[number][pl.ds(k, 1), :] = late[pl.ds(2 * k + number, 1), :]
            norms[2 + number][pl.ds(k, 1), :] = early[pl.ds(2 * k + number, 1), :]
    for k in range(LOCAL // LANES):
        bias[:, pl.ds(k * LANES, LANES)] = early[pl.ds(NORM_ROWS + 3 * k, 3), :]


def results(*values):
    shapes = [jax.ShapeDtypeStruct(item.shape, item.dtype) for item in values[:6]]
    shapes += [jax.ShapeDtypeStruct((WIDTH // LANES, LANES), F32)] * 4
    shapes.append(jax.ShapeDtypeStruct((3, LOCAL), F32))
    return pl.pallas_call(
        results_kernel,
        out_shape=tuple(shapes),
        in_specs=vmem(8),
        out_specs=tuple(vmem(len(shapes))),
        name="results",
    )(*values)


def body(
    tokens,
    doc_ids,
    qkv_weight,
    qkv_bias,
    out_weight,
    norm1_gain,
    norm1_shift,
    norm2_gain,
    norm2_shift,
    gate_up_weight,
    down_weight,
    cotangent,
):
    norms = [item[None] for item in (norm1_gain, norm1_shift, norm2_gain, norm2_shift)]
    frequency = jnp.power(10000.0, -2.0 * jnp.arange(ROT // 2, dtype=F32) / ROT)
    frequency = jnp.broadcast_to(frequency[:, None], (ROT // 2, LANES))
    gate_up = jnp.swapaxes(gate_up_weight, 1, 2).reshape(2 * UNITS, ROWS)
    normed2, start, logs, mixed, tables, acts, attended, rows, weights, cots, feed = attention_forward(
        tokens,
        doc_ids[None],
        qkv_bias,
        out_weight,
        norms,
        frequency,
        qkv_weight,
        gate_up,
        down_weight,
        cotangent,
    )
    grad_mixed, branch_grad, norm2_grads, halves, outs = feed_forward(
        norms[2], normed2, mixed, cotangent, cots, feed
    )
    backward = attention_backward(
        norms[0],
        norm2_grads,
        branch_grad,
        grad_mixed,
        mixed,
        tokens,
        tables,
        start,
        acts,
        attended,
        logs,
        weights,
        halves,
        rows,
        outs,
    )
    layer_out, token_grad, qkv_grad, out_grad, gate_up_grad, down_grad, *sums = results(*backward)
    return (
        layer_out,
        token_grad,
        qkv_grad,
        sums[4],
        out_grad,
        sums[0].reshape(WIDTH),
        sums[1].reshape(WIDTH),
        sums[2].reshape(WIDTH),
        sums[3].reshape(WIDTH),
        jnp.swapaxes(gate_up_grad.reshape(2, UNITS, ROWS), 1, 2),
        down_grad,
    )


def solution(mesh):
    in_specs = (
        P(("dp", "tensor"), None),
        P(("dp", "tensor")),
        P(None, "dp", "tensor"),
        P(None, "tensor"),
        P("tensor", "dp"),
        P(),
        P(),
        P(),
        P(),
        P(None, "dp", "tensor"),
        P("tensor", "dp"),
        P(("dp", "tensor"), None),
    )
    out_specs = (
        P(("dp", "tensor"), None),
        P(("dp", "tensor"), None),
        P(None, "dp", "tensor"),
        P(None, "tensor"),
        P("tensor", "dp"),
        P(),
        P(),
        P(),
        P(),
        P(None, "dp", "tensor"),
        P("tensor", "dp"),
    )
    return jax.shard_map(body, mesh=mesh, in_specs=in_specs, out_specs=out_specs, check_vma=False)
```

time: 359 us -> 288 us (0.80)
  the two profiles are of different devices: /device:TPU:0 before, /device:TPU:34 now
where the time goes in v4:
time: 288 us; the launch traced here: 283 us
  Pallas kernels  281 us (98%)
    pallas_call x1, Pallas kernels, attention_backward(): pl.pallas_call(attention_back_kernel, out_shape=(jax.ShapeDtypeStruct((RO...  111 us
    pallas_call x1, Pallas kernels, attention_forward(): pl.pallas_call(attention_kernel, out_shape=(jax.ShapeDtypeStruct((ROWS, W...  97.1 us
    pallas_call x1, Pallas kernels, feed_forward(): pl.pallas_call(feed_kernel, out_shape=(jax.ShapeDtypeStruct((ROWS, WIDTH)...  69.6 us

profile of v4, /device:TPU:34, one launch (start us, length us, event | category | flops | bytes accessed | tf_op | source)
XLA Modules:
  0.0 282.8 jit_solution(11393278066989902783)
XLA Ops:
  0.7 0.7 broadcast_in_dim.26.frequency
  1.3 97.1 %attention_forward.1 = (bf16[128,2048]{1,0:T(8,128)(2,1)}, f32[8,1024]{1,0:T(8,128)}, f32[8,1024]{1,0:T(8,128)}, f32[128,2048]{1,0:T(8,128)}, f32[3,1024,128]{2,...) custom-call(bf16[128,2048]{1,0:T(8,128)(2,1)} %tokens_in.1, ...), custom_call_target="tpu_custom_call" | custom-call | tf_op jit(solution)/shard_map/attention_forward/pallas_call | solution.py:740
  98.4 69.6 %feed_forward.1 = (f32[128,2048]{1,0:T(8,128)}, bf16[128,2048]{1,0:T(8,128)(2,1)}, f32[2,2048]{1,0:T(2,128)}, bf16[8,2112,128]{2,1,0:T(8,128)(2,1)}, bf16[8,128,2048]{2,1,0:T(8,128)(2,1)}) custom-call(f32[1,2048]{1,0:T(1,128)} %bitcast.17, bf16[128,2048]{1,0:T(8,128)(2,1)} %get-tuple-element.46.own, f32[128,2048]{1,0:T(8,128)} %get-tuple-element.47.mixed_in, ...), custom_call_target="tpu_custom_call" | custom-call | tf_op jit(solution)/shard_map/feed_forward/pallas_call | solution.py:959
  168.0 111.0 %attention_backward.1 = (bf16[128,2048]{1,0:T(8,128)(2,1)}, bf16[128,2048]{1,0:T(8,128)(2,1)}, f32[3,128,256]{2,1,0:T(8,128)}, f32[256,128]{1,0:T(8,128)}, f32[1...) custom-call(f32[1,2048]{1,0:T(1,128)} %bitcast.19, ...), custom_call_target="tpu_custom_call" | custom-call | tf_op jit(solution)/shard_map/attention_backward/pallas_call | solution.py:1291
  279.0 3.3 %results.1 = (bf16[128,2048]{1,0:T(8,128)(2,1)}, bf16[128,2048]{1,0:T(8,128)(2,1)}, f32[3,128,256]{2,1,0:T(8,128)}, f32[256,128]{1,0:T(8,128)}, f32[1408,128]{1,...) custom-call(bf16[128,2048]{1,0:T(8,128)(2,1)} %get-tuple-element.62., ...), custom_call_target="tpu_custom_call" | custom-call | tf_op jit(solution)/shard_map/results/pallas_call | solution.py:1373
  (1 shorter events, 0.0 us)

commit v5 on v4

--- a/solution.py
+++ b/solution.py
@@ -2,6 +2,7 @@
 
 import jax
 import jax.numpy as jnp
+import numpy as np
 from jax import lax
 from jax.experimental import pallas as pl
 from jax.experimental.pallas import tpu as pltpu
@@ -184,6 +185,7 @@
         self.a, self.mail, self.parts, self.land, self.top = around, mail, parts, land, top
         self.middle = MIDDLE[top]
         self.counts, self.firsts = scatter_boxes(top)
+        self.crossed = False
 
     def part(self, slot, first, last):
         return self.parts.at[slot, pl.ds(first, last - first)]
@@ -277,14 +279,16 @@
     def all_direct(self):
         self.direct(0, 1, 2, 3, 17, 7, 4, 6, 5, 18, 8, 9)
 
-    def finish(self, total):
+    def boxed(self, number, first, last):
+        return self.land[pl.ds(self.firsts[number] + first, last - first), :]
+
+    def finish_top(self, total):
         a, top = self.a, self.top
-        for number in (8, 9, 13, 14, 18, 19, 16, 20, 15):
+        for number in (9, 14, 15, 18, 19):
             self.got(number)
-
-        def boxed(number, first, last):
-            return self.land[pl.ds(self.firsts[number] + first, last - first), :]
-
+        if not self.crossed:
+            self.got(16)
+            self.crossed = True
         total[pl.ds(0, top), :] = added(
             self.part(a.me, 0, top)[...], *(self.box(k)[...] for k in (9, 14, 15))
         )
@@ -292,13 +296,20 @@
             self.part(a.me, top, HALF)[...],
             self.box(18)[...],
             self.box(19)[...],
-            boxed(16, 0, HALF - top),
+            self.boxed(16, 0, HALF - top),
         )
+
+    def finish_low(self, total):
+        for number in (8, 13, 20):
+            self.got(number)
+        if not self.crossed:
+            self.got(16)
+            self.crossed = True
         total[pl.ds(HALF, HALF), :] = added(
-            self.part(a.me, HALF, ROWS)[...],
+            self.part(self.a.me, HALF, ROWS)[...],
             self.box(8)[...],
             self.box(13)[...],
-            boxed(16, HALF - top, ROWS - top),
+            self.boxed(16, HALF - self.top, ROWS - self.top),
         )
 
 
@@ -377,24 +388,13 @@
 
 FOLD_MAILS = 7
 
-EARLY_ROWS, NORM_ROWS = 40, 32
+SUM_ROWS, NORM_ROWS = 72, 64
 SUM_BOXES, SUM_MAILS = 14, 13
 
 
 class EverySum:
-    def __init__(self, a, r, mail, boxes, rows, norms):
-        self.norms, self.mail, self.boxes = norms, mail, boxes
-        crossed = 1 - r.zh
-        place = r.zh * 2 + r.core
-        z_sources = [crossed * 2 + r.core, r.zh * 2 + 1 - r.core, crossed * 2 + 1 - r.core]
-        z_peers = [r.to_zh, r.to_core, r.to_zh_core]
-        y_peers = [a.to_up, a.to_rest[0], a.to_down]
-        self.stages = [
-            (0, rows, r.x, [r.xs[3], r.xs[2], r.xs[1]], r.to_x[1:]),
-            (4, rows, place, z_sources, z_peers),
-            (8, norms, a.y, [a.y_down, a.y_far, a.y_up], y_peers),
-            (12, norms, a.z, [1 - a.z], [a.to_across]),
-        ]
+    def __init__(self, mail, boxes, stages):
+        self.mail, self.boxes, self.stages = mail, boxes, stages
 
     def give(self, stage, values):
         base, count, mine, _, peers = self.stages[stage]
@@ -421,17 +421,24 @@
         self.give(1, self.take(0))
 
     def third(self):
-        self.over_dp = self.take(1)
-        self.give(2, self.over_dp[: self.norms])
+        self.kept = self.take(1)
+        self.give(2, self.kept[: self.stages[2][1]])
 
     def fourth(self):
         self.give(3, self.take(2))
 
-    def result(self):
-        total = self.take(3)
-        if self.norms == self.over_dp.shape[0]:
-            return total
-        return jnp.concatenate([total, self.over_dp[self.norms :]], axis=0)
+
+def sum_stages(a, r):
+    crossed = 1 - r.zh
+    place = r.zh * 2 + r.core
+    sources = [crossed * 2 + r.core, r.zh * 2 + 1 - r.core, crossed * 2 + 1 - r.core]
+    y_sources, y_peers = [a.y_down, a.y_far, a.y_up], [a.to_up, a.to_rest[0], a.to_down]
+    return [
+        (0, SUM_ROWS, r.x, [r.xs[3], r.xs[2], r.xs[1]], r.to_x[1:]),
+        (4, SUM_ROWS, place, sources, [r.to_zh, r.to_core, r.to_zh_core]),
+        (8, NORM_ROWS, a.y, y_sources, y_peers),
+        (12, NORM_ROWS, a.z, [1 - a.z], [a.to_across]),
+    ]
 
 
 def dot(left, right):
@@ -449,12 +456,14 @@
     return centred * rinv, rinv
 
 
+def norm_sums(incoming, normal):
+    return jnp.sum(incoming * normal, axis=0, keepdims=True), jnp.sum(incoming, axis=0, keepdims=True)
+
+
 def norm_back(incoming, normal, rinv, gain):
     scaled = incoming * gain
     inner = scaled - jnp.mean(scaled, axis=1, keepdims=True)
-    inner = inner - normal * jnp.mean(scaled * normal, axis=1, keepdims=True)
-    gain_grad = jnp.sum(incoming * normal, axis=0, keepdims=True)
-    return rinv * inner, gain_grad, jnp.sum(incoming, axis=0, keepdims=True)
+    return rinv * (inner - normal * jnp.mean(scaled * normal, axis=1, keepdims=True))
 
 
 def turned(values, tables, first, sign):
@@ -706,25 +715,33 @@
         keep(attended, attended_kept, 10)
         scatter.all_direct()
 
-    def second_norm():
-        scatter.finish(total)
-        after = tokens[...].astype(F32) + total[...]
-        mixed[...] = after
-        keep(mixed, mixed_kept, 11)
+    def norm_half(first, number):
+        half = pl.ds(first, HALF)
+        after = tokens[half, :].astype(F32) + total[half, :]
+        mixed[half, :] = after
+        keep(mixed.at[half], mixed_kept.at[half], number)
         normal, _ = normalized(after)
-        normed2[...] = (normal * gain2[...] + shift2[...]).astype(BF16)
+        normed2[half, :] = (normal * gain2[...] + shift2[...]).astype(BF16)
+
+    def norm_top():
+        scatter.finish_top(total)
+        norm_half(0, 11)
+
+    def norm_low():
+        scatter.finish_low(total)
+        norm_half(HALF, 12)
 
     R, C, B, w, f = gather.step, others.step, scatter.step, spread.step, feeds.step
     C_up, C_down, C_across = (partial(others.send, *two) for two in ((0, 3), (1, 4), (2, 5)))
     for step in (
         begin, place, R(0), R(1), w(1), w(3), R(2), R(3), R(4), w(2), w(0), R(6), R(8), C_across,
-        R(5), feeds.begin, R(10), C_down, w(4), w(6), R(9), C_up, R(7), R(15), R(16), R(11), R(14),
-        w(5), R(13), R(12), spread.finish, P(a.y_down), P(a.y_far), C(1), P(a.y), P(a.y_up),
-        A(0, 0, 4), A(1, 0, 2), C(4), C(2), f(1), f(3), A(1, 2, 4), A(2, 0, 1), A(2, 1, 2), C(5),
-        A(2, 2, 3), A(2, 3, 4), C(9), A(3, 0, 1), A(3, 1, 2), A(3, 2, 3), C(10), C(15), A(3, 3, 4),
-        branch_sums, f(2), C(3), C(8), C(0), C(16), C(13), f(0), C(11), B(0), C(14), B(2), B(1),
-        B(3), B(17), B(4), f(4), f(6), C(6), B(5), C(7), scatter.over_last, C(12),
-        scatter.over_inner, f(5), feeds.finish, second_norm,
+        R(5), feeds.begin, R(10), C_down, R(9), C_up, R(7), w(4), w(6), R(15), R(16), R(11), R(14),
+        w(5), R(13), R(12), spread.finish, P(a.y_down), P(a.y_far), C(1), P(a.y), C(0), P(a.y_up),
+        A(0, 0, 4), A(1, 0, 2), f(1), C(2), f(3), C(3), A(1, 2, 4), C(5), A(2, 0, 1), A(2, 1, 2),
+        C(8), A(2, 2, 3), C(6), A(2, 3, 4), A(3, 0, 1), C(10), A(3, 1, 2), C(9), A(3, 2, 3), f(2),
+        A(3, 3, 4), branch_sums, C(16), C(15), f(0), C(4), C(7), C(14), C(13), C(12), B(0), B(1),
+        B(17), B(2), B(3), B(4), f(4), f(6), scatter.over_last, scatter.over_inner, C(11), f(5),
+        B(5), feeds.finish, norm_low, norm_top,
     ):
         step()
     for mail in (rmail, cmail, bmail, wmail, fmail, imail):
@@ -774,7 +791,7 @@
             *pairs(SPREAD_MAILS),
             *pairs(SPREAD_MAILS),
             *pairs(7),
-            pltpu.SemaphoreType.DMA((12,)),
+            pltpu.SemaphoreType.DMA((13,)),
         ],
         compiler_params=params(0),
         name="attention_forward",
@@ -790,9 +807,9 @@
     cots_own,
     cots_in,
     feed,
-    grad_mixed,
     branch_grad,
     norm_grads,
+    grad_mixed_kept,
     halves,
     outs_kept,
     rows,
@@ -807,6 +824,7 @@
     mixed,
     own_cots,
     total,
+    grad_mixed,
     g_sends,
     g_receives,
     s_sends,
@@ -906,16 +924,31 @@
     def keep_outs():
         keep(outs, outs_kept, 6)
 
-    def norm():
+    def second_norm():
         for copy in late_loads:
             copy.wait()
-        scatter.finish(total)
-        normal, rinv = normalized(mixed[...])
-        back, gain_grad, shift_grad = norm_back(total[...], normal, rinv, gain2[...])
-        back = own_cots[...].astype(F32) + back
-        grad_mixed[...] = back
-        branch_grad[...] = back.astype(BF16)
-        norm_grads[...] = jnp.concatenate([gain_grad, shift_grad], axis=0)
+        mixed[...], state["rinv"] = normalized(mixed[...])
+
+    def norm_half(first, number):
+        half = pl.ds(first, HALF)
+        incoming, normal = total[half, :], mixed[half, :]
+        rinv = state["rinv"][first : first + HALF]
+        back = norm_back(incoming, normal, rinv, gain2[...])
+        back = own_cots[half, :].astype(F32) + back
+        grad_mixed[half, :] = back
+        keep(grad_mixed.at[half], grad_mixed_kept.at[half], number)
+        branch_grad[half, :] = back.astype(BF16)
+        sums = jnp.concatenate(norm_sums(incoming, normal), axis=0)
+        norm_grads[...] = sums + norm_grads[...] if "summed" in state else sums
+        state["summed"] = True
+
+    def norm_top():
+        scatter.finish_top(total)
+        norm_half(0, 7)
+
+    def norm_low():
+        scatter.finish_low(total)
+        norm_half(HALF, 8)
 
     couples = [(a.me, a.across), (a.down, a.up), (a.far, a.down_o), (a.far_o, a.up_o)]
     directs = [(9,), (18, 8), (3, 17, 6, 5), (0, 1, 2, 7, 4)]
@@ -940,11 +973,11 @@
         return partial(core_sums, 4 * index, 4 * index + 4)
 
     for step in (
-        partial(gather.send, *range(6)), load, G(0), G(2), G(1), G(3), G(4), P(1), T(1), G(10),
-        Q(1), D(1), G(5), P(0), G(16), G(6), G(7), Q(0), D(0), T(0), G(9), G(15), G(8), P(2), T(2),
-        G(14), Q(2), D(2), G(13), G(11), G(12), P(3), Q(3), D(3), T(3), S(17), keep_outs, W(0),
-        S(3), W(1), S(0), W(2), S(1), W(3), S(2), K(0), S(4), scatter.over_inner, K(1),
-        scatter.over_last, S(5), norm,
+        partial(gather.send, *range(6)), load, G(0), G(1), G(2), second_norm, G(3), G(4), G(5),
+        P(1), T(1), P(0), G(6), G(7), Q(0), D(0), G(8), T(0), G(9), G(10), Q(1), D(1), G(15), G(16),
+        G(11), P(2), Q(2), D(2), G(14), G(13), T(2), G(12), P(3), Q(3), D(3), S(17), T(3),
+        keep_outs, W(0), S(0), W(1), S(1), W(2), S(2), S(3), W(3), scatter.over_last, S(4), K(0),
+        scatter.over_inner, K(1), S(5), norm_low, norm_top,
     ):
         step()
     gmail.finish()
@@ -959,14 +992,14 @@
     return pl.pallas_call(
         feed_kernel,
         out_shape=(
-            jax.ShapeDtypeStruct((ROWS, WIDTH), F32),
             jax.ShapeDtypeStruct((ROWS, WIDTH), BF16),
             jax.ShapeDtypeStruct((2, WIDTH), F32),
+            jax.ShapeDtypeStruct((ROWS, WIDTH), F32),
             jax.ShapeDtypeStruct(blocks, BF16),
             jax.ShapeDtypeStruct(group, BF16),
         ),
         in_specs=vmem(1) + anywhere(5),
-        out_specs=tuple(vmem(3) + anywhere(2)),
+        out_specs=tuple(vmem(2) + anywhere(3)),
         scratch_shapes=[
             pltpu.VMEM(group, BF16),
             pltpu.VMEM(group, BF16),
@@ -980,11 +1013,12 @@
             pltpu.VMEM((ROWS, WIDTH), F32),
             pltpu.VMEM((ROWS, WIDTH), BF16),
             pltpu.VMEM((ROWS, WIDTH), F32),
+            pltpu.VMEM((ROWS, WIDTH), F32),
             *pairs(GATHER_MAILS),
             *pairs(SCATTER_MAILS),
             *pairs(8),
             pltpu.SemaphoreType.DMA((16,)),
-            pltpu.SemaphoreType.DMA((7,)),
+            pltpu.SemaphoreType.DMA((9,)),
         ],
         compiler_params=params(1),
         name="feed_forward",
@@ -995,6 +1029,7 @@
 
 def attention_back_kernel(
     gain1,
+    shift1,
     norm2_grads,
     own,
     grad_mixed_in,
@@ -1015,8 +1050,7 @@
     out_grad,
     gate_up_grad,
     down_grad,
-    early_out,
-    late_out,
+    sums,
     grad_mixed,
     mixed,
     tokens,
@@ -1043,7 +1077,6 @@
     own_halves,
     total,
     boxes,
-    late_boxes,
     g_sends,
     g_receives,
     s_sends,
@@ -1058,14 +1091,12 @@
     f_receives,
     a_sends,
     a_receives,
-    l_sends,
-    l_receives,
     local,
 ):
     a, r = Around(), Ring()
     gmail, mail, omail = Mail(g_sends, g_receives), Mail(s_sends, s_receives), Mail(o_sends, o_receives)
     kmail, wmail, fmail = Mail(k_sends, k_receives), Mail(w_sends, w_receives), Mail(f_sends, f_receives)
-    amail, lmail = Mail(a_sends, a_receives), Mail(l_sends, l_receives)
+    amail = Mail(a_sends, a_receives)
     peers = a.peers() + a.to_rest[:1] + r.peers() + [r.to_zh_core]
     hail(peers)
     loads = {}
@@ -1099,8 +1130,7 @@
     gather = Gather(a, gmail, rows, TOP_GRADS)
     out_scatter = Scatter(a, omail, out_parts, out_land, TOP_OUTS)
     scatter = Scatter(a, mail, parts, land, TOP_BACK)
-    early = EverySum(a, r, amail, boxes, EARLY_ROWS, NORM_ROWS)
-    late = EverySum(a, r, lmail, late_boxes, NORM_ROWS, NORM_ROWS)
+    every = EverySum(amail, boxes, sum_stages(a, r))
     feed_fold = Fold(r, fmail, halves, lambda side: own_halves[side], f_land)
     fold = Fold(r, wmail, core_land, lambda side: core_land[fold.place(side, 0)], w_land)
 
@@ -1160,7 +1190,7 @@
 
     def input_grad(y):
         if "tables" in loads:
-            loaded("tables")
+            loaded("tables", "before")
         first = pl.multiple_of(y * QBLOCK, QBLOCK)
         span = pl.ds(first, QBLOCK)
         back = jnp.zeros((QBLOCK, WIDTH), F32)
@@ -1193,8 +1223,6 @@
         return carry
 
     def weight_grads(first):
-        if "before" in loads:
-            loaded("before")
         lax.fori_loop(first, first + 2, weight_grad, 0)
 
     def core_sum(index, carry):
@@ -1222,32 +1250,48 @@
 
     def layer_result():
         loaded("mixed")
-        out_scatter.finish(total)
+        out_scatter.finish_top(total)
+        out_scatter.finish_low(total)
         layer_out[...] = (mixed[...] + total[...]).astype(BF16)
 
-    def norm():
+    def first_norm():
         loaded("tokens", "grad_mixed")
-        scatter.finish(total)
-        normal, rinv = normalized(tokens[...].astype(F32))
-        back, gain_grad, shift_grad = norm_back(total[...], normal, rinv, gain1[...])
-        late.first(by_lanes(gain_grad, shift_grad))
-        token_grad[...] = (grad_mixed[...] + back).astype(BF16)
+        mixed[...], state["rinv"] = normalized(tokens[...].astype(F32))
+
+    def norm_half(first):
+        half = pl.ds(first, HALF)
+        rinv = state["rinv"][first : first + HALF]
+        back = norm_back(total[half, :], mixed[half, :], rinv, gain1[...])
+        token_grad[half, :] = (grad_mixed[half, :] + back).astype(BF16)
+
+    def norm_top():
+        scatter.finish_top(total)
+        norm_half(0)
+
+    def norm_low():
+        scatter.finish_low(total)
+        norm_half(HALF)
+
+    def norm1_sums(y):
+        part = parts[pl.ds(2 * y, 2)].reshape(QBLOCK, WIDTH).astype(F32)
+        scaled = before[pl.ds(2 * y, 2)].reshape(QBLOCK, WIDTH).astype(F32) - shift1[...]
+        sums = jnp.concatenate(norm_sums(part, scaled), axis=0)
+        state["norm1"] = sums + state["norm1"] if "norm1" in state else sums
 
     def by_lanes(*values):
         values = jnp.concatenate(values, axis=0)
         width = values.shape[1]
         return jnp.concatenate([values[:, k : k + LANES] for k in range(0, width, LANES)], axis=0)
 
-    def early_sums():
-        spare = jnp.zeros((EARLY_ROWS - NORM_ROWS - 3 * LOCAL // LANES, LANES), F32)
-        parts_now = [by_lanes(norm2_grads[...]), by_lanes(state["bias"]), spare]
-        early.first(jnp.concatenate(parts_now, axis=0))
-
-    def early_result():
-        early_out[...] = early.result()
-
-    def late_result():
-        late_out[...] = late.result()
+    def first_sums():
+        norm1 = state["norm1"]
+        norms = by_lanes(norm1[:1] / gain1[...], norm1[1:], norm2_grads[...])
+        spare = jnp.zeros((SUM_ROWS - NORM_ROWS - 3 * LOCAL // LANES, LANES), F32)
+        every.first(jnp.concatenate([norms, by_lanes(state["bias"]), spare], axis=0))
+
+    def last_sums():
+        sums[pl.ds(0, NORM_ROWS), :] = every.take(3)
+        sums[pl.ds(NORM_ROWS, SUM_ROWS - NORM_ROWS), :] = every.kept[NORM_ROWS:]
 
     G, O, S = gather.step, out_scatter.step, scatter.step
 
@@ -1260,6 +1304,9 @@
     def I(y):
         return partial(input_grad, y)
 
+    def N(y):
+        return partial(norm1_sums, y)
+
     def W(index):
         return partial(weight_grads, 2 * index)
 
@@ -1268,20 +1315,20 @@
 
     for step in (
         partial(gather.send, *range(6)), partial(feed_fold.send, *range(6)), turn, G(0), G(1), G(2),
-        G(3), G(4), G(5), P(a.y), G(7), G(6), out_scatter.direct_across, G(8), G(10), G(11),
+        G(3), G(4), G(5), P(a.y), G(7), G(6), G(8), out_scatter.direct_across, G(10), G(11),
         out_scatter.direct_down, G(9), out_scatter.direct_up, G(15), G(16), G(12), P(a.y_down),
-        P(a.y_up), G(14), O(2), G(13), P(a.y_far), A(0, 0, 4), A(1, 0, 2), A(1, 2, 4), O(0),
-        A(2, 0, 1), O(17), A(2, 1, 2), A(2, 2, 3), feed_cross, O(4), A(2, 3, 4), O(3), A(3, 0, 1),
-        A(3, 1, 2), A(3, 2, 3), A(3, 3, 4), I(a.y_far), scatter.from_far_pair, I(a.y_up),
-        scatter.from_up_pair, I(a.y_down), scatter.from_down_pair, I(a.y), O(5),
-        scatter.from_across, W(0), out_scatter.over_last, W(1), W(2), S(1), W(3), S(17), S(2), K(0),
-        feed_result, O(1), K(1), S(4), partial(fold.send, *range(6)), early_sums, S(0), S(3),
-        scatter.over_inner, S(5), scatter.over_last, fold.cross, out_scatter.over_inner, norm,
-        early.second, weight_result, late.second, layer_result, early.third, late.third,
-        early.fourth, late.fourth, early_result, late_result,
+        P(a.y_up), G(14), O(2), G(13), P(a.y_far), A(0, 0, 4), A(1, 0, 2), O(1), O(4), A(1, 2, 4),
+        O(0), O(17), A(2, 0, 1), A(2, 1, 2), feed_cross, A(2, 2, 3), A(2, 3, 4), A(3, 0, 1),
+        A(3, 1, 2), A(3, 2, 3), A(3, 3, 4), I(a.y_far), I(a.y_up), I(a.y_down), I(a.y),
+        scatter.from_across, O(5), scatter.from_down_pair, N(a.y), W(0), out_scatter.over_inner,
+        scatter.from_up_pair, N(a.y_up), W(1), scatter.from_far_pair, W(2), W(3),
+        out_scatter.over_last, N(a.y_down), N(a.y_far), first_sums, K(0), K(1),
+        partial(fold.send, *range(6)), S(0), feed_result, O(3), every.second, S(4), S(3), S(1),
+        S(17), scatter.over_last, S(2), scatter.over_inner, layer_result, every.third, first_norm,
+        S(5), fold.cross, norm_low, every.fourth, norm_top, weight_result, last_sums,
     ):
         step()
-    for some in (gmail, mail, omail, kmail, wmail, fmail, amail, lmail):
+    for some in (gmail, mail, omail, kmail, wmail, fmail, amail):
         some.finish()
 
 
@@ -1297,11 +1344,10 @@
             jax.ShapeDtypeStruct((LOCAL, ROWS), F32),
             jax.ShapeDtypeStruct((2 * UNITS, ROWS), F32),
             jax.ShapeDtypeStruct((UNITS, ROWS), F32),
-            jax.ShapeDtypeStruct((EARLY_ROWS, LANES), F32),
-            jax.ShapeDtypeStruct((NORM_ROWS, LANES), F32),
+            jax.ShapeDtypeStruct((SUM_ROWS, LANES), F32),
         ),
-        in_specs=vmem(2) + anywhere(13),
-        out_specs=tuple(vmem(8)),
+        in_specs=vmem(3) + anywhere(13),
+        out_specs=tuple(vmem(7)),
         scratch_shapes=[
             pltpu.VMEM((ROWS, WIDTH), F32),
             pltpu.VMEM((ROWS, WIDTH), F32),
@@ -1328,8 +1374,7 @@
             pltpu.VMEM((FOLD_MAILS,) + feed_block, BF16),
             pltpu.VMEM((2,) + feed_block, BF16),
             pltpu.VMEM((ROWS, WIDTH), F32),
-            pltpu.VMEM((SUM_BOXES, EARLY_ROWS, LANES), F32),
-            pltpu.VMEM((SUM_BOXES, NORM_ROWS, LANES), F32),
+            pltpu.VMEM((SUM_BOXES, SUM_ROWS, LANES), F32),
             *pairs(GATHER_MAILS),
             *pairs(SCATTER_MAILS),
             *pairs(SCATTER_MAILS),
@@ -1337,7 +1382,6 @@
             *pairs(FOLD_MAILS),
             *pairs(FOLD_MAILS),
             *pairs(SUM_MAILS),
-            *pairs(SUM_MAILS),
             pltpu.SemaphoreType.DMA((14,)),
         ],
         compiler_params=params(2),
@@ -1346,7 +1390,7 @@
 
 
 def results_kernel(
-    layer_in, token_in, qkv_in, out_in, gate_up_in, down_in, early, late, layer, token, qkv, out, gate_up, down, *norms
+    layer_in, token_in, qkv_in, out_in, gate_up_in, down_in, sums, layer, token, qkv, out, gate_up, down, *norms
 ):
     bias = norms[4]
     for source, target in (
@@ -1359,11 +1403,10 @@
     ):
         target[...] = source[...]
     for k in range(WIDTH // LANES):
-        for number in range(2):
-            norms[number][pl.ds(k, 1), :] = late[pl.ds(2 * k + number, 1), :]
-            norms[2 + number][pl.ds(k, 1), :] = early[pl.ds(2 * k + number, 1), :]
+        for number in range(4):
+            norms[number][pl.ds(k, 1), :] = sums[pl.ds(4 * k + number, 1), :]
     for k in range(LOCAL // LANES):
-        bias[:, pl.ds(k * LANES, LANES)] = early[pl.ds(NORM_ROWS + 3 * k, 3), :]
+        bias[:, pl.ds(k * LANES, LANES)] = sums[pl.ds(NORM_ROWS + 3 * k, 3), :]
 
 
 def results(*values):
@@ -1373,7 +1416,7 @@
     return pl.pallas_call(
         results_kernel,
         out_shape=tuple(shapes),
-        in_specs=vmem(8),
+        in_specs=vmem(7),
         out_specs=tuple(vmem(len(shapes))),
         name="results",
     )(*values)
@@ -1394,8 +1437,8 @@
     cotangent,
 ):
     norms = [item[None] for item in (norm1_gain, norm1_shift, norm2_gain, norm2_shift)]
-    frequency = jnp.power(10000.0, -2.0 * jnp.arange(ROT // 2, dtype=F32) / ROT)
-    frequency = jnp.broadcast_to(frequency[:, None], (ROT // 2, LANES))
+    frequency = np.power(10000.0, -2.0 * np.arange(ROT // 2) / ROT).astype(np.float32)
+    frequency = jnp.asarray(np.tile(frequency[:, None], (1, LANES)))
     gate_up = jnp.swapaxes(gate_up_weight, 1, 2).reshape(2 * UNITS, ROWS)
     normed2, start, logs, mixed, tables, acts, attended, rows, weights, cots, feed = attention_forward(
         tokens,
@@ -1409,11 +1452,12 @@
         down_weight,
         cotangent,
     )
-    grad_mixed, branch_grad, norm2_grads, halves, outs = feed_forward(
+    branch_grad, norm2_grads, grad_mixed, halves, outs = feed_forward(
         norms[2], normed2, mixed, cotangent, cots, feed
     )
     backward = attention_backward(
         norms[0],
+        norms[1],
         norm2_grads,
         branch_grad,
         grad_mixed,

time: 288 us -> 277 us (0.962)
  the two profiles are of different devices: /device:TPU:34 before, /device:TPU:4 now
where the time goes in v5:
time: 277 us; the launch traced here: 272 us
  Pallas kernels  271 us (98%)
    pallas_call x1, Pallas kernels, attention_backward(): pl.pallas_call(attention_back_kernel, out_shape=(jax.ShapeDtypeStruct((RO...  101 us
    pallas_call x1, Pallas kernels, attention_forward(): pl.pallas_call(attention_kernel, out_shape=(jax.ShapeDtypeStruct((ROWS, W...  97.9 us
    pallas_call x1, Pallas kernels, feed_forward(): pl.pallas_call(feed_kernel, out_shape=(jax.ShapeDtypeStruct((ROWS, WIDTH)...  68.2 us

profile of v5, /device:TPU:4, one launch (start us, length us, event | category | flops | bytes accessed | tf_op | source)
XLA Modules:
  0.0 271.7 jit_solution(1905753958348754070)
XLA Ops:
  0.6 97.9 %attention_forward.1 = (bf16[128,2048]{1,0:T(8,128)(2,1)}, f32[8,1024]{1,0:T(8,128)}, f32[8,1024]{1,0:T(8,128)}, f32[128,2048]{1,0:T(8,128)}, f32[3,1024,128]{2,...) custom-call(bf16[128,2048]{1,0:T(8,128)(2,1)} %tokens_in.1, ...), custom_call_target="tpu_custom_call" | custom-call | tf_op jit(solution)/shard_map/attention_forward/pallas_call | solution.py:757
  98.6 68.2 %feed_forward.1 = (bf16[128,2048]{1,0:T(8,128)(2,1)}, f32[2,2048]{1,0:T(2,128)}, f32[128,2048]{1,0:T(8,128)}, bf16[8,2112,128]{2,1,0:T(8,128)(2,1)}, bf16[8,128,2048]{2,1,0:T(8,128)(2,1)}) custom-call(f32[1,2048]{1,0:T(1,128)} %bitcast.17, bf16[128,2048]{1,0:T(8,128)(2,1)} %get-tuple-element.45.own, f32[128,2048]{1,0:T(8,128)} %get-tuple-element.46.mixed_in, ...), custom_call_target="tpu_custom_call" | custom-call | tf_op jit(solution)/shard_map/feed_forward/pallas_call | solution.py:992
  166.8 101.2 %attention_backward.1 = (bf16[128,2048]{1,0:T(8,128)(2,1)}, bf16[128,2048]{1,0:T(8,128)(2,1)}, f32[3,128,256]{2,1,0:T(8,128)}, f32[256,128]{1,0:T(8,128)}, f32[1...) custom-call(f32[1,2048]{1,0:T(1,128)} %bitcast.19, f32[1,2048]{1,0:T(1,128)} %bitcast.21, ...), custom_call_target="tpu_custom_call" | custom-call | tf_op jit(solution)/shard_map/attention_backward/pallas_call | solution.py:1338
  268.0 3.3 %results.1 = (bf16[128,2048]{1,0:T(8,128)(2,1)}, bf16[128,2048]{1,0:T(8,128)(2,1)}, f32[3,128,256]{2,1,0:T(8,128)}, f32[256,128]{1,0:T(8,128)}, f32[1408,128]{1,...) custom-call(bf16[128,2048]{1,0:T(8,128)(2,1)} %get-tuple-element.61., ...), custom_call_target="tpu_custom_call" | custom-call | tf_op jit(solution)/shard_map/results/pallas_call | solution.py:1416

commit v6 on v5

--- a/solution.py
+++ b/solution.py
@@ -553,9 +553,9 @@
     gate_up,
     down,
     own_cots,
-    normed2,
     start_lanes,
     logs,
+    normed2_kept,
     mixed_kept,
     tables_kept,
     acts_kept,
@@ -572,6 +572,7 @@
     acts,
     attended,
     mixed,
+    normed2,
     id_rows,
     start_rows,
     parts,
@@ -611,9 +612,13 @@
     for copy in loads:
         copy.start()
     id_rows[a.me] = jnp.broadcast_to(ids[...], (8, ROWS))
-    weights[3, pl.ds(mine, ROWS), :] = out_shard[...].T
-    normal, _ = normalized(tokens[...].astype(F32))
-    rows[a.me] = (normal * gain1[...] + shift1[...]).astype(BF16)
+
+    def first_norm(first):
+        half = pl.ds(first, HALF)
+        normal, _ = normalized(tokens[half, :].astype(F32))
+        rows[a.me, half] = (normal * gain1[...] + shift1[...]).astype(BF16)
+
+    first_norm(0)
     hear(peers)
 
     group = [
@@ -638,14 +643,15 @@
         started.append(copy)
 
     def begin():
+        gather.send(0)
         for number, device, _ in group:
             imail.send(number, id_rows.at[a.me], id_rows.at[a.me], device)
-        for number in (0, 1, 2):
-            gather.send(number)
+        first_norm(HALF)
+        gather.send(1, 2)
+        weights[3, pl.ds(mine, ROWS), :] = out_shard[...].T
         loads[0].wait()
         spread.begin()
-        for number in (3, 4, 5):
-            gather.send(number)
+        gather.send(3, 4, 5)
         for copy in loads[1:]:
             copy.wait()
         keep(feed_own, feed.at[r.dp], 4)
@@ -722,6 +728,7 @@
         keep(mixed.at[half], mixed_kept.at[half], number)
         normal, _ = normalized(after)
         normed2[half, :] = (normal * gain2[...] + shift2[...]).astype(BF16)
+        keep(normed2.at[half], normed2_kept.at[half], number + 2)
 
     def norm_top():
         scatter.finish_top(total)
@@ -734,14 +741,14 @@
     R, C, B, w, f = gather.step, others.step, scatter.step, spread.step, feeds.step
     C_up, C_down, C_across = (partial(others.send, *two) for two in ((0, 3), (1, 4), (2, 5)))
     for step in (
-        begin, place, R(0), R(1), w(1), w(3), R(2), R(3), R(4), w(2), w(0), R(6), R(8), C_across,
-        R(5), feeds.begin, R(10), C_down, R(9), C_up, R(7), w(4), w(6), R(15), R(16), R(11), R(14),
-        w(5), R(13), R(12), spread.finish, P(a.y_down), P(a.y_far), C(1), P(a.y), C(0), P(a.y_up),
-        A(0, 0, 4), A(1, 0, 2), f(1), C(2), f(3), C(3), A(1, 2, 4), C(5), A(2, 0, 1), A(2, 1, 2),
-        C(8), A(2, 2, 3), C(6), A(2, 3, 4), A(3, 0, 1), C(10), A(3, 1, 2), C(9), A(3, 2, 3), f(2),
-        A(3, 3, 4), branch_sums, C(16), C(15), f(0), C(4), C(7), C(14), C(13), C(12), B(0), B(1),
-        B(17), B(2), B(3), B(4), f(4), f(6), scatter.over_last, scatter.over_inner, C(11), f(5),
-        B(5), feeds.finish, norm_low, norm_top,
+        begin, R(0), place, R(1), R(2), w(3), w(1), R(3), R(4), w(2), w(0), R(6), C_across,
+        feeds.begin, R(8), R(5), R(10), C_down, R(9), C_up, R(7), w(4), w(6), R(15), R(16), R(11),
+        R(14), R(13), w(5), R(12), spread.finish, P(a.y_down), P(a.y_far), C(1), C(0), P(a.y),
+        P(a.y_up), A(0, 0, 4), A(1, 0, 2), C(2), C(3), f(1), f(3), A(1, 2, 4), C(5), A(2, 0, 1),
+        A(2, 1, 2), A(2, 2, 3), C(6), C(8), A(2, 3, 4), A(3, 0, 1), A(3, 1, 2), C(10), C(9),
+        A(3, 2, 3), f(2), A(3, 3, 4), branch_sums, C(15), C(16), C(4), f(0), C(7), C(14), C(13),
+        C(12), B(0), B(1), B(17), B(2), B(3), B(4), f(4), f(6), scatter.over_last,
+        scatter.over_inner, C(11), f(5), B(5), feeds.finish, norm_low, norm_top,
     ):
         step()
     for mail in (rmail, cmail, bmail, wmail, fmail, imail):
@@ -757,9 +764,9 @@
     return pl.pallas_call(
         attention_kernel,
         out_shape=(
-            jax.ShapeDtypeStruct((ROWS, WIDTH), BF16),
             jax.ShapeDtypeStruct((8, GROUP), F32),
             jax.ShapeDtypeStruct((8, GROUP), F32),
+            jax.ShapeDtypeStruct((ROWS, WIDTH), BF16),
             jax.ShapeDtypeStruct((ROWS, WIDTH), F32),
             jax.ShapeDtypeStruct(tables, F32),
             jax.ShapeDtypeStruct(acts, BF16),
@@ -770,7 +777,7 @@
             jax.ShapeDtypeStruct((16, 3 * UNITS, ROWS), BF16),
         ),
         in_specs=vmem(9) + anywhere(4),
-        out_specs=tuple(vmem(3) + anywhere(8)),
+        out_specs=tuple(vmem(2) + anywhere(9)),
         scratch_shapes=[
             pltpu.VMEM(group, BF16),
             pltpu.VMEM(weights, BF16),
@@ -780,6 +787,7 @@
             pltpu.VMEM(acts, BF16),
             pltpu.VMEM((GROUP, LOCAL), BF16),
             pltpu.VMEM((ROWS, WIDTH), F32),
+            pltpu.VMEM((ROWS, WIDTH), BF16),
             pltpu.VMEM((TENSOR, 8, ROWS), jnp.int32),
             pltpu.VMEM((GROUP, LANES), F32),
             pltpu.VMEM(group, BF16),
@@ -791,7 +799,7 @@
             *pairs(SPREAD_MAILS),
             *pairs(SPREAD_MAILS),
             *pairs(7),
-            pltpu.SemaphoreType.DMA((13,)),
+            pltpu.SemaphoreType.DMA((15,)),
         ],
         compiler_params=params(0),
         name="attention_forward",
@@ -807,8 +815,8 @@
     cots_own,
     cots_in,
     feed,
-    branch_grad,
     norm_grads,
+    branch_grad_kept,
     grad_mixed_kept,
     halves,
     outs_kept,
@@ -825,6 +833,7 @@
     own_cots,
     total,
     grad_mixed,
+    branch_grad,
     g_sends,
     g_receives,
     s_sends,
@@ -850,9 +859,8 @@
     ]
     for copy in [first_load] + loads + late_loads:
         copy.start()
-    first_load.wait()
     hear(peers)
-    gather = Gather(a, gmail, rows, TOP_FEED)
+    gather = Gather(a, gmail, rows, TOP_FEED, own)
     scatter = Scatter(a, mail, parts, land, TOP_FEED_BACK)
     started = []
 
@@ -862,7 +870,7 @@
         started.append(copy)
 
     def load():
-        for copy in loads:
+        for copy in [first_load] + loads:
             copy.wait()
 
     state = {}
@@ -938,6 +946,7 @@
         grad_mixed[half, :] = back
         keep(grad_mixed.at[half], grad_mixed_kept.at[half], number)
         branch_grad[half, :] = back.astype(BF16)
+        keep(branch_grad.at[half], branch_grad_kept.at[half], number + 2)
         sums = jnp.concatenate(norm_sums(incoming, normal), axis=0)
         norm_grads[...] = sums + norm_grads[...] if "summed" in state else sums
         state["summed"] = True
@@ -992,14 +1001,14 @@
     return pl.pallas_call(
         feed_kernel,
         out_shape=(
+            jax.ShapeDtypeStruct((2, WIDTH), F32),
             jax.ShapeDtypeStruct((ROWS, WIDTH), BF16),
-            jax.ShapeDtypeStruct((2, WIDTH), F32),
             jax.ShapeDtypeStruct((ROWS, WIDTH), F32),
             jax.ShapeDtypeStruct(blocks, BF16),
             jax.ShapeDtypeStruct(group, BF16),
         ),
         in_specs=vmem(1) + anywhere(5),
-        out_specs=tuple(vmem(2) + anywhere(3)),
+        out_specs=tuple(vmem(1) + anywhere(4)),
         scratch_shapes=[
             pltpu.VMEM(group, BF16),
             pltpu.VMEM(group, BF16),
@@ -1014,11 +1023,12 @@
             pltpu.VMEM((ROWS, WIDTH), BF16),
             pltpu.VMEM((ROWS, WIDTH), F32),
             pltpu.VMEM((ROWS, WIDTH), F32),
+            pltpu.VMEM((ROWS, WIDTH), BF16),
             *pairs(GATHER_MAILS),
             *pairs(SCATTER_MAILS),
             *pairs(8),
             pltpu.SemaphoreType.DMA((16,)),
-            pltpu.SemaphoreType.DMA((9,)),
+            pltpu.SemaphoreType.DMA((11,)),
         ],
         compiler_params=params(1),
         name="feed_forward",
@@ -1044,13 +1054,18 @@
     halves,
     first_rows,
     outs,
+    sums,
+    layer_kept,
+    token_kept,
+    qkv_kept,
+    out_kept,
+    gate_up_kept,
+    down_kept,
     layer_out,
     token_grad,
     qkv_grad,
     out_grad,
-    gate_up_grad,
-    down_grad,
-    sums,
+    feed_grad,
     grad_mixed,
     mixed,
     tokens,
@@ -1121,13 +1136,19 @@
         loads[name] = pltpu.make_async_copy(source, target, local.at[number])
         loads[name].start()
 
+    started = []
+
+    def keep(source, target, number):
+        copy = pltpu.make_async_copy(source, target, local.at[number])
+        copy.start()
+        started.append(copy)
+
     def loaded(*names):
         for name in names:
             loads.pop(name).wait()
 
-    loaded("own")
     hear(peers)
-    gather = Gather(a, gmail, rows, TOP_GRADS)
+    gather = Gather(a, gmail, rows, TOP_GRADS, own)
     out_scatter = Scatter(a, omail, out_parts, out_land, TOP_OUTS)
     scatter = Scatter(a, mail, parts, land, TOP_BACK)
     every = EverySum(amail, boxes, sum_stages(a, r))
@@ -1140,7 +1161,7 @@
         turns[pl.ds(3 * LOCAL, LOCAL), :] = attended[...].T
         grads_qkv[1] = jnp.zeros((GROUP, LOCAL), F32)
         grads_qkv[2] = jnp.zeros((GROUP, LOCAL), F32)
-        loaded("outs", "weights", "logs", "start")
+        loaded("own", "outs", "weights", "logs", "start")
 
     def back_project(y):
         chunk = rows[pl.ds(2 * y, 2)].reshape(QBLOCK, WIDTH)
@@ -1238,8 +1259,9 @@
         loaded("half")
         feed_fold.near()
         feed_sum = feed_fold.result()
-        gate_up_grad[...] = feed_sum[: 2 * UNITS]
-        down_grad[...] = feed_sum[2 * UNITS :]
+        feed_grad[...] = feed_sum
+        keep(feed_grad.at[pl.ds(0, 2 * UNITS)], gate_up_kept, 14)
+        keep(feed_grad.at[pl.ds(2 * UNITS, UNITS)], down_kept, 15)
 
     def weight_result():
         fold.near()
@@ -1247,30 +1269,34 @@
         for c in range(3):
             qkv_grad[c] = shard[c * LOCAL : (c + 1) * LOCAL].T
         out_grad[...] = shard[3 * LOCAL :]
+        keep(qkv_grad, qkv_kept, 16)
+        keep(out_grad, out_kept, 17)
 
     def layer_result():
         loaded("mixed")
         out_scatter.finish_top(total)
         out_scatter.finish_low(total)
         layer_out[...] = (mixed[...] + total[...]).astype(BF16)
+        keep(layer_out, layer_kept, 18)
 
     def first_norm():
         loaded("tokens", "grad_mixed")
         mixed[...], state["rinv"] = normalized(tokens[...].astype(F32))
 
-    def norm_half(first):
+    def norm_half(first, number):
         half = pl.ds(first, HALF)
         rinv = state["rinv"][first : first + HALF]
         back = norm_back(total[half, :], mixed[half, :], rinv, gain1[...])
         token_grad[half, :] = (grad_mixed[half, :] + back).astype(BF16)
+        keep(token_grad.at[half], token_kept.at[half], number)
 
     def norm_top():
         scatter.finish_top(total)
-        norm_half(0)
+        norm_half(0, 19)
 
     def norm_low():
         scatter.finish_low(total)
-        norm_half(HALF)
+        norm_half(HALF, 20)
 
     def norm1_sums(y):
         part = parts[pl.ds(2 * y, 2)].reshape(QBLOCK, WIDTH).astype(F32)
@@ -1317,19 +1343,21 @@
         partial(gather.send, *range(6)), partial(feed_fold.send, *range(6)), turn, G(0), G(1), G(2),
         G(3), G(4), G(5), P(a.y), G(7), G(6), G(8), out_scatter.direct_across, G(10), G(11),
         out_scatter.direct_down, G(9), out_scatter.direct_up, G(15), G(16), G(12), P(a.y_down),
-        P(a.y_up), G(14), O(2), G(13), P(a.y_far), A(0, 0, 4), A(1, 0, 2), O(1), O(4), A(1, 2, 4),
-        O(0), O(17), A(2, 0, 1), A(2, 1, 2), feed_cross, A(2, 2, 3), A(2, 3, 4), A(3, 0, 1),
-        A(3, 1, 2), A(3, 2, 3), A(3, 3, 4), I(a.y_far), I(a.y_up), I(a.y_down), I(a.y),
-        scatter.from_across, O(5), scatter.from_down_pair, N(a.y), W(0), out_scatter.over_inner,
-        scatter.from_up_pair, N(a.y_up), W(1), scatter.from_far_pair, W(2), W(3),
-        out_scatter.over_last, N(a.y_down), N(a.y_far), first_sums, K(0), K(1),
-        partial(fold.send, *range(6)), S(0), feed_result, O(3), every.second, S(4), S(3), S(1),
-        S(17), scatter.over_last, S(2), scatter.over_inner, layer_result, every.third, first_norm,
-        S(5), fold.cross, norm_low, every.fourth, norm_top, weight_result, last_sums,
+        P(a.y_up), G(14), O(2), G(13), P(a.y_far), A(0, 0, 4), A(1, 0, 2), O(1), A(1, 2, 4),
+        A(2, 0, 1), A(2, 1, 2), O(17), O(0), O(4), feed_cross, A(2, 2, 3), O(3), A(2, 3, 4),
+        A(3, 0, 1), A(3, 1, 2), A(3, 2, 3), A(3, 3, 4), I(a.y_far), I(a.y_up), I(a.y_down),
+        scatter.from_down_pair, N(a.y_down), I(a.y), out_scatter.over_last, scatter.from_across,
+        scatter.from_up_pair, W(0), feed_result, O(5), W(1), W(2), W(3), scatter.from_far_pair,
+        N(a.y_far), N(a.y_up), out_scatter.over_inner, N(a.y), first_sums, K(0), K(1),
+        partial(fold.send, *range(6)), S(0), every.second, S(4), S(1), S(17), S(3), S(2),
+        scatter.over_last, scatter.over_inner, layer_result, every.third, first_norm, S(5),
+        fold.cross, norm_low, every.fourth, norm_top, weight_result, last_sums,
     ):
         step()
     for some in (gmail, mail, omail, kmail, wmail, fmail, amail):
         some.finish()
+    for copy in started:
+        copy.wait()
 
 
 def attention_backward(*operands):
@@ -1338,17 +1366,22 @@
     return pl.pallas_call(
         attention_back_kernel,
         out_shape=(
+            jax.ShapeDtypeStruct((SUM_ROWS, LANES), F32),
             jax.ShapeDtypeStruct((ROWS, WIDTH), BF16),
             jax.ShapeDtypeStruct((ROWS, WIDTH), BF16),
             jax.ShapeDtypeStruct((3, ROWS, LOCAL), F32),
             jax.ShapeDtypeStruct((LOCAL, ROWS), F32),
             jax.ShapeDtypeStruct((2 * UNITS, ROWS), F32),
             jax.ShapeDtypeStruct((UNITS, ROWS), F32),
-            jax.ShapeDtypeStruct((SUM_ROWS, LANES), F32),
         ),
         in_specs=vmem(3) + anywhere(13),
-        out_specs=tuple(vmem(7)),
+        out_specs=tuple(vmem(1) + anywhere(6)),
         scratch_shapes=[
+            pltpu.VMEM((ROWS, WIDTH), BF16),
+            pltpu.VMEM((ROWS, WIDTH), BF16),
+            pltpu.VMEM((3, ROWS, LOCAL), F32),
+            pltpu.VMEM((LOCAL, ROWS), F32),
+            pltpu.VMEM(feed_block, F32),
             pltpu.VMEM((ROWS, WIDTH), F32),
             pltpu.VMEM((ROWS, WIDTH), F32),
             pltpu.VMEM((ROWS, WIDTH), BF16),
@@ -1382,7 +1415,7 @@
             *pairs(FOLD_MAILS),
             *pairs(FOLD_MAILS),
             *pairs(SUM_MAILS),
-            pltpu.SemaphoreType.DMA((14,)),
+            pltpu.SemaphoreType.DMA((21,)),
         ],
         compiler_params=params(2),
         name="attention_backward",
@@ -1390,7 +1423,7 @@
 
 
 def results_kernel(
-    layer_in, token_in, qkv_in, out_in, gate_up_in, down_in, sums, layer, token, qkv, out, gate_up, down, *norms
+    sums, layer_in, token_in, qkv_in, out_in, gate_up_in, down_in, layer, token, qkv, out, gate_up, down, *norms
 ):
     bias = norms[4]
     for source, target in (
@@ -1410,7 +1443,7 @@
 
 
 def results(*values):
-    shapes = [jax.ShapeDtypeStruct(item.shape, item.dtype) for item in values[:6]]
+    shapes = [jax.ShapeDtypeStruct(item.shape, item.dtype) for item in values[1:]]
     shapes += [jax.ShapeDtypeStruct((WIDTH // LANES, LANES), F32)] * 4
     shapes.append(jax.ShapeDtypeStruct((3, LOCAL), F32))
     return pl.pallas_call(
@@ -1440,7 +1473,7 @@
     frequency = np.power(10000.0, -2.0 * np.arange(ROT // 2) / ROT).astype(np.float32)
     frequency = jnp.asarray(np.tile(frequency[:, None], (1, LANES)))
     gate_up = jnp.swapaxes(gate_up_weight, 1, 2).reshape(2 * UNITS, ROWS)
-    normed2, start, logs, mixed, tables, acts, attended, rows, weights, cots, feed = attention_forward(
+    start, logs, normed2, mixed, tables, acts, attended, rows, weights, cots, feed = attention_forward(
         tokens,
         doc_ids[None],
         qkv_bias,
@@ -1452,7 +1485,7 @@
         down_weight,
         cotangent,
     )
-    branch_grad, norm2_grads, grad_mixed, halves, outs = feed_forward(
+    norm2_grads, branch_grad, grad_mixed, halves, outs = feed_forward(
         norms[2], normed2, mixed, cotangent, cots, feed
     )
     backward = attention_backward(

time: 277 us -> 273 us (0.986)
  the two profiles are of different devices: /device:TPU:4 before, /device:TPU:0 now
where the time goes in v6:
time: 273 us; the launch traced here: 268 us
  Pallas kernels  267 us (98%)
    pallas_call x1, Pallas kernels, attention_backward(): pl.pallas_call(attention_back_kernel, out_shape=(jax.ShapeDtypeStruct((SU...  101 us
    pallas_call x1, Pallas kernels, attention_forward(): pl.pallas_call(attention_kernel, out_shape=(jax.ShapeDtypeStruct((8, GROU...  97.3 us
    pallas_call x1, Pallas kernels, feed_forward(): pl.pallas_call(feed_kernel, out_shape=(jax.ShapeDtypeStruct((2, WIDTH), F...  65.3 us

profile of v6, /device:TPU:0, one launch (start us, length us, event | category | flops | bytes accessed | tf_op | source)
XLA Modules:
  0.0 267.8 jit_solution(1741826753182468205)
XLA Ops:
  0.6 97.3 %attention_forward.1 = (f32[8,1024]{1,0:T(8,128)}, f32[8,1024]{1,0:T(8,128)}, bf16[128,2048]{1,0:T(8,128)(2,1)}, f32[128,2048]{1,0:T(8,128)}, f32[3,1024,128]{2,...) custom-call(bf16[128,2048]{1,0:T(8,128)(2,1)} %tokens_in.1, ...), custom_call_target="tpu_custom_call" | custom-call | tf_op jit(solution)/shard_map/attention_forward/pallas_call | solution.py:764
  97.9 65.3 %feed_forward.1 = (f32[2,2048]{1,0:T(2,128)}, bf16[128,2048]{1,0:T(8,128)(2,1)}, f32[128,2048]{1,0:T(8,128)}, bf16[8,2112,128]{2,1,0:T(8,128)(2,1)}, bf16[8,128,2048]{2,1,0:T(8,128)(2,1)}) custom-call(f32[1,2048]{1,0:T(1,128)} %bitcast.17, bf16[128,2048]{1,0:T(8,128)(2,1)} %get-tuple-element.45.own, f32[128,2048]{1,0:T(8,128)} %get-tuple-element.46.mixed_in, ...), custom_call_target="tpu_custom_call" | custom-call | tf_op jit(solution)/shard_map/feed_forward/pallas_call | solution.py:1001
  163.2 101.1 %attention_backward.1 = (f32[72,128]{1,0:T(8,128)}, bf16[128,2048]{1,0:T(8,128)(2,1)}, bf16[128,2048]{1,0:T(8,128)(2,1)}, f32[3,128,256]{2,1,0:T(8,128)}, f32[25...) custom-call(f32[1,2048]{1,0:T(1,128)} %bitcast.19, f32[1,2048]{1,0:T(1,128)} %bitcast.21, ...), custom_call_target="tpu_custom_call" | custom-call | tf_op jit(solution)/shard_map/attention_backward/pallas_call | solution.py:1366
  264.4 3.2 %results.1 = (bf16[128,2048]{1,0:T(8,128)(2,1)}, bf16[128,2048]{1,0:T(8,128)(2,1)}, f32[3,128,256]{2,1,0:T(8,128)}, f32[256,128]{1,0:T(8,128)}, f32[1408,128]{1,...) custom-call(f32[72,128]{1,0:T(8,128)} %get-tuple-element.61.sums, ...), custom_call_target="tpu_custom_call" | custom-call | tf_op jit(solution)/shard_map/results/pallas_call | solution.py:1449
